TPU v7x, 32 devices: a whole 2x2x4 slice. The times are simulated.
32 devices in a mesh: ctx: 8 (over y, x, core), tp: 4 (over z).
Axes of the slice: x: 2, y: 2, z: 4, core: 2. Of those that a mesh axis runs over, the one named last changes fastest.
Arguments:
- queries: bfloat16 [12288, 4096], P('ctx', 'tp'), may hold values from -6 to 6
- keys: bfloat16 [12288, 4096], P('ctx', 'tp'), may hold values from -6 to 6
- values: bfloat16 [12288, 4096], P('ctx', 'tp'), may hold values from -51 to 51, as said below
- out_grad: bfloat16 [12288, 4096], P('ctx', 'tp'), may hold values from -6 to 6
- gain: float32 [4096], P('tp'), may hold values from 0.25 to 1.75
- doc_ids: int32 [48], P('ctx'), may hold values from 0 to 7, never falling along the last dimension, each value on 1 to 24 neighbouring positions
Outputs:
- normed: bfloat16 [12288, 4096], P('ctx', 'tp')
- query_grad: bfloat16 [12288, 4096], P('ctx', 'tp')
- key_grad: bfloat16 [12288, 4096], P('ctx', 'tp')
- value_grad: bfloat16 [12288, 4096], P('ctx', 'tp')
Inputs may be any that keep to these rules, and one draw needn't show every extreme that they name: `doc_ids`: never falls along the sequence; each document covers 1 to max(4, 24) blocks, and one covers exactly that many. `values`: values of order one to ten, with scales that differ from token to token and from feature to feature.
All inputs are finite; a program needn't handle non-finite values.
Results may differ from a plain program's by a relative error of at most 0.0058.
Values sent between devices are 32-bit elements; how exact they have to be, the bound alone decides.
No kernel may reach another device: no remote copies, remote signals or barrier semaphores. Data moves between devices by JAX's collectives and lax.ppermute only.
A program may use at most 128 MiB of HBM per device.

v0:
```python
import functools

import jax
import jax.numpy as jnp
from jax import lax
from jax.experimental import pallas as pl
from jax.experimental.pallas import tpu as pltpu
from jax.sharding import PartitionSpec as P

HD = 128
C = 256
QW = 4096
PAD = 8
NEVER = -1.0e9
MIB = 1 << 20

epsilon = 1e-06

F32 = jnp.float32
BF16 = jnp.bfloat16
VM = pl.BlockSpec(memory_space=pltpu.VMEM)
SM = pl.BlockSpec(memory_space=pltpu.SMEM)
ANY = pl.BlockSpec(memory_space=pl.ANY)
HB = pl.BlockSpec(memory_space=pltpu.HBM)


def dot(a, b, dims):
    return lax.dot_general(a, b, (dims, ((), ())), preferred_element_type=F32)


NN = ((1,), (0,))
NT = ((1,), (1,))
TN = ((0,), (0,))


def params(mib=12):
    return pltpu.CompilerParams(vmem_limit_bytes=mib * MIB)


def cost(flops, nbytes):
    return pl.CostEstimate(flops=int(flops), bytes_accessed=int(nbytes), transcendentals=0)


def half_start(own, cols):
    core = lax.rem(lax.axis_index("ctx"), 2)
    half = core if own else 1 - core
    return pl.multiple_of(half * cols, 128)


def head(h):
    return pl.ds(h * HD, HD)


def block(n):
    return pl.ds(pl.multiple_of(n * C, C), C)


def state_rows(n, h, heads):
    return pl.ds(pl.multiple_of((n * heads + h) * HD, HD), HD)


def key_value_states(own, blocks, heads, docs, k_hbm, v_hbm, k, v, inside, message, sems):
    off = half_start(own, heads * HD)
    copies = []
    for h in range(heads):
        src = pl.ds(off + h * HD, HD)
        pair = (
            pltpu.make_async_copy(k_hbm.at[:, src], k.at[:, head(h)], sems.at[2 * h]),
            pltpu.make_async_copy(v_hbm.at[:, src], v.at[:, head(h)], sems.at[2 * h + 1]),
        )
        for copy in pair:
            copy.start()
        copies.append(pair)
    for h in range(heads):
        for copy in copies[h]:
            copy.wait()
        running = jnp.zeros((HD, HD), F32)
        for n in range(blocks):
            inside[state_rows(n, h, heads), :] = running
            rows = pl.ds(n * C, C)
            total = running + dot(k[rows, head(h)], v[rows, head(h)], TN)
            if n + 1 < blocks:
                running = jnp.where(docs[n] == docs[n + 1], total, 0.0)
            else:
                message[head(h), :] = total
    message[heads * HD :, :] = jnp.full((PAD, HD), docs[blocks - 1].astype(F32), F32)


def local_scores(own, blocks, heads, k, v, q_hbm, g_hbm, q, g, local, scores, sems, gsem):
    off = half_start(own, heads * HD)
    cols = pl.ds(off, heads * HD)

    def q_copy(n):
        return pltpu.make_async_copy(q_hbm.at[block(n), cols], q.at[block(n), :], sems.at[n])

    for n in range(blocks):
        q_copy(n).start()
    g_copy = pltpu.make_async_copy(g_hbm.at[:, cols], g, gsem)
    g_copy.start()
    causal = lax.broadcasted_iota(jnp.int32, (C, C), 0) >= lax.broadcasted_iota(
        jnp.int32, (C, C), 1
    )

    def step(n, carry):
        q_copy(n).wait()
        rows = block(n)
        for h in range(heads):
            s = dot(q[rows, head(h)], k[rows, head(h)], NT)
            s = jnp.where(causal, s, 0.0).astype(BF16)
            scores[pl.ds(pl.multiple_of((n * heads + h) * C, C), C), :] = s
            local[rows, head(h)] = dot(s, v[rows, head(h)], NN)
        return carry

    lax.fori_loop(0, blocks, step, 0)
    g_copy.wait()


def attend(own, blocks, heads, lanes, docs, inside, carry, q, local, g, gain, *rest):
    if own:
        attended, low, sums = rest
        sums[...] = jnp.zeros((C, HD), F32)
    else:
        sums_in, attended, low, message, sums = rest
        sums[...] = sums_in[...]
    off = half_start(own, heads * HD)
    gains = gain[:, pl.ds(off, heads * HD)]
    lane = lax.broadcasted_iota(jnp.int32, (C, HD), 1)

    def step(n, carried):
        rows = block(n)
        hit = carry[heads * HD : heads * HD + 1, :] == docs[n].astype(F32)
        square = jnp.zeros((C, HD), F32)
        inner = jnp.zeros((C, HD), F32)
        for h in range(heads):
            here = state_rows(n, h, heads)
            state = inside[here, :] + jnp.where(hit, carry[head(h), :], 0.0)
            state_low = state.astype(BF16)
            low[here, :] = state_low
            out = local[rows, head(h)] + dot(q[rows, head(h)], state_low, NN)
            attended[rows, head(h)] = out
            weighted = g[rows, head(h)].astype(F32) * gains[:, h * HD : (h + 1) * HD]
            square += out * out
            inner += weighted * out
        square = jnp.sum(square, axis=1, keepdims=True)
        inner = jnp.sum(inner, axis=1, keepdims=True)
        sums[...] += jnp.where(lane == n, square, 0.0) + jnp.where(lane == n + lanes, inner, 0.0)
        return carried

    lax.fori_loop(0, blocks, step, 0)
    if not own:
        message[...] = jnp.transpose(sums[...])[: 2 * lanes, :]


def mixed(own, blocks, heads, lanes, parts, docs, *rest):
    if not own:
        pieces, rest = rest[:parts], rest[parts:]
        attended, q, g, gain, grad, inside, message, scale, slope, running, turn = rest
        total = pieces[0][...]
        for piece in pieces[1:]:
            total = total + piece[...]
        r = lax.rsqrt(total[:lanes] / QW + epsilon)
        s = r * r * r * (total[lanes:] / QW)
        turn[...] = jnp.zeros((HD, C), F32)
        turn[:lanes, :] = r
        turn[lanes : 2 * lanes, :] = s
        columns = jnp.transpose(turn[...])
        for n in range(blocks):
            rows = pl.ds(n * C, C)
            scale[rows, :] = jnp.broadcast_to(columns[:, n : n + 1], (C, HD))
            slope[rows, :] = jnp.broadcast_to(columns[:, lanes + n : lanes + n + 1], (C, HD))
    else:
        scale, slope, attended, q, g, gain, grad, inside, message, running = rest
    off = half_start(own, heads * HD)
    gains = gain[:, pl.ds(off, heads * HD)]
    running[...] = jnp.zeros((heads * HD, HD), F32)

    def step(i, carried):
        n = blocks - 1 - i
        rows = block(n)
        linked = docs[n] == docs[jnp.maximum(n - 1, 0)]
        r = scale[rows, :]
        s = slope[rows, :]
        for h in range(heads):
            weighted = g[rows, head(h)].astype(F32) * gains[:, h * HD : (h + 1) * HD]
            d = (r * weighted - attended[rows, head(h)] * s).astype(BF16)
            grad[rows, head(h)] = d
            state = running[head(h), :]
            inside[state_rows(n, h, heads), :] = state
            state = state + dot(q[rows, head(h)], d, TN)
            message[head(h), :] = state
            running[head(h), :] = jnp.where(linked, state, 0.0)
        return carried

    lax.fori_loop(0, blocks, step, 0)
    message[heads * HD :, :] = jnp.full((PAD, HD), -docs[0].astype(F32), F32)


def store_blocks(n, pairs, cols, sems):
    slot = lax.rem(n, 2)
    return [
        pltpu.make_async_copy(stage.at[slot], out.at[block(n), cols], sems.at[i, slot])
        for i, (stage, out) in enumerate(pairs)
    ]


def query_side(own, blocks, heads, k, v, q, attended, scale, gain, grad, low, scores, *rest):
    if not own:
        normed, query_grad, key_local, value_local, stage_n, stage_q, sems = rest
    else:
        _, _, normed, query_grad, key_local, value_local, stage_n, stage_q, sems = rest
    off = half_start(own, heads * HD)
    cols = pl.ds(off, heads * HD)
    gains = gain[:, cols]
    pairs = ((stage_n, normed), (stage_q, query_grad))
    causal = lax.broadcasted_iota(jnp.int32, (C, C), 0) >= lax.broadcasted_iota(
        jnp.int32, (C, C), 1
    )

    def step(n, carried):
        rows = block(n)
        slot = lax.rem(n, 2)

        @pl.when(n >= 2)
        def _():
            for copy in store_blocks(n - 2, pairs, cols, sems):
                copy.wait()

        r = scale[rows, :]
        for h in range(heads):
            d = grad[rows, head(h)]
            gs = dot(d, v[rows, head(h)], NT)
            gs = jnp.where(causal, gs, 0.0).astype(BF16)
            qg = dot(d, low[state_rows(n, h, heads), :], NT) + dot(gs, k[rows, head(h)], NN)
            stage_q[slot, :, head(h)] = qg.astype(BF16)
            key_local[rows, head(h)] = dot(gs, q[rows, head(h)], TN)
            s = scores[pl.ds(pl.multiple_of((n * heads + h) * C, C), C), :]
            value_local[rows, head(h)] = dot(s, d, TN)
            out = attended[rows, head(h)] * r * gains[:, h * HD : (h + 1) * HD]
            stage_n[slot, :, head(h)] = out.astype(BF16)
        for copy in store_blocks(n, pairs, cols, sems):
            copy.start()
        return carried

    lax.fori_loop(0, blocks, step, 0)
    for n in range(max(blocks - 2, 0), blocks):
        for copy in store_blocks(n, pairs, cols, sems):
            copy.wait()


def key_side(own, blocks, heads, docs, inside, carry, k, v, key_local, value_local, *rest):
    if own:
        key_grad, value_grad, stage_k, stage_v, sems = rest
    else:
        _, _, key_grad, value_grad, stage_k, stage_v, sems = rest
    off = half_start(own, heads * HD)
    cols = pl.ds(off, heads * HD)
    pairs = ((stage_k, key_grad), (stage_v, value_grad))

    def step(n, carried):
        rows = block(n)
        slot = lax.rem(n, 2)

        @pl.when(n >= 2)
        def _():
            for copy in store_blocks(n - 2, pairs, cols, sems):
                copy.wait()

        hit = carry[heads * HD : heads * HD + 1, :] == -docs[n].astype(F32)
        for h in range(heads):
            state = inside[state_rows(n, h, heads), :] + jnp.where(hit, carry[head(h), :], 0.0)
            leave = state.astype(BF16)
            kg = key_local[rows, head(h)] + dot(v[rows, head(h)], leave, NT)
            vg = value_local[rows, head(h)] + dot(k[rows, head(h)], leave, NN)
            stage_k[slot, :, head(h)] = kg.astype(BF16)
            stage_v[slot, :, head(h)] = vg.astype(BF16)
        for copy in store_blocks(n, pairs, cols, sems):
            copy.start()
        return carried

    lax.fori_loop(0, blocks, step, 0)
    for n in range(max(blocks - 2, 0), blocks):
        for copy in store_blocks(n, pairs, cols, sems):
            copy.wait()


def merge_kernel(reverse, outs, count, *refs):
    size = lax.axis_size("ctx")
    rank = lax.axis_index("ctx")
    if reverse:
        rank = size - 1 - rank

    def bit(b):
        return lax.rem(lax.div(rank, 1 << b), 2)

    ins, results = refs[:count], refs[count:]
    for pieces, result in zip(outs, results):
        at = 0
        latest = None
        for rows, terms in pieces:
            keys = []
            for source, start, flag in terms:
                last = ins[source].shape[0] - PAD
                key = ins[source][last : last + 1, :]
                keys.append(key if flag is None else jnp.where(flag(bit), key, NEVER))
            latest = functools.reduce(jnp.maximum, keys)
            value = None
            for (source, start, _), key in zip(terms, keys):
                part = jnp.where(key == latest, ins[source][start : start + rows, :], 0.0)
                value = part if value is None else value + part
            result[at : at + rows, :] = value
            at += rows
        result[at:, :] = jnp.broadcast_to(latest, (PAD, HD))


def merge(ins, outs, reverse):
    shapes = [pltpu.VMEM((sum(rows for rows, _ in pieces) + PAD, HD), F32) for pieces in outs]
    return pl.pallas_call(
        functools.partial(merge_kernel, reverse, outs, len(ins)),
        out_shape=shapes,
        in_specs=[VM] * len(ins),
        out_specs=[VM] * len(outs),
        compiler_params=params(),
        cost_estimate=cost(0, 1 << 18),
    )(*ins)


def swap(message, b):
    size = lax.axis_size("ctx")
    return lax.ppermute(message, "ctx", [(i, i ^ (1 << b)) for i in range(size)])


def scan(theirs, mine, reverse):
    rows = mine.shape[0] - PAD
    part = rows // 2
    top = lax.axis_size("ctx").bit_length() - 1
    lo, hi = top - 2, top - 1
    beside = swap(theirs, 0)
    halves = [[(part, [(0, start, None), (1, start, None)])] for start in (0, part)]
    total_a, total_b = merge([mine, beside], halves, reverse)
    before_a, before_b = [], []
    for b in range(1, lo):
        got_a, got_b = swap(total_a, b), swap(total_b, b)

        def is_high(bit, b=b):
            return bit(b) == 1

        ins = [total_a, total_b, got_a, got_b] + before_a + before_b
        earlier_a = [(4, 0, None)] if before_a else []
        earlier_b = [(5, 0, None)] if before_b else []
        total_a, total_b, pa, pb = merge(
            ins,
            [
                [(part, [(0, 0, None), (2, 0, None)])],
                [(part, [(1, 0, None), (3, 0, None)])],
                [(part, [(2, 0, is_high)] + earlier_a)],
                [(part, [(3, 0, is_high)] + earlier_b)],
            ],
            reverse,
        )
        before_a, before_b = [pa], [pb]
    first_a, first_b = swap(total_a, lo), swap(total_b, hi)
    next_a, next_b = merge(
        [total_a, first_a, total_b, first_b],
        [
            [(part, [(0, 0, None), (1, 0, None)])],
            [
                (
                    part,
                    [
                        (2, 0, lambda bit: bit(lo) * bit(hi) == 0),
                        (3, 0, lambda bit: bit(hi) == 1),
                    ],
                )
            ],
        ],
        reverse,
    )
    second_a, second_b = swap(next_a, hi), swap(next_b, lo)

    def carried(neighbour, flag):
        terms_a = [(0, 0, lambda bit: bit(lo) == 1), (1, 0, lambda bit: bit(hi) == 1)]
        terms_b = [(2, 0, lambda bit: bit(hi) == 1), (3, 0, lambda bit: bit(lo) + bit(hi) > 0)]
        if before_a:
            terms_a.append((6, 0, None))
            terms_b.append((7, 0, None))
        return [
            (part, terms_a + [(neighbour, 0, flag)]),
            (part, terms_b + [(neighbour, part, flag)]),
        ]

    carry_mine, carry_theirs = merge(
        [first_a, second_a, first_b, second_b, beside, mine] + before_a + before_b,
        [carried(4, lambda bit: bit(0) == 1), carried(5, lambda bit: bit(0) == 0)],
        reverse,
    )
    return carry_mine, swap(carry_theirs, 0)


def local(queries, keys, values, out_grad, gain, doc_ids):
    tokens, features = queries.shape
    heads = features // HD // 2
    cols = heads * HD
    blocks = tokens // C
    lanes = -(-blocks // 8) * 8
    pairs = blocks * heads
    tp = lax.axis_size("tp")
    gain = gain.reshape(1, features)
    rows = cols + PAD
    narrow, wide, square = C * HD * HD, C * C * HD, HD * HD
    dma = pltpu.SemaphoreType.DMA
    half_bf = pltpu.VMEM((tokens, cols), BF16)
    half_f32 = pltpu.VMEM((tokens, cols), F32)
    states_f32 = pltpu.VMEM((pairs * HD, HD), F32)
    message = pltpu.VMEM((rows, HD), F32)
    whole = pltpu.HBM((tokens, features), BF16)
    column = pltpu.VMEM((tokens, HD), F32)

    def states(own):
        return pl.pallas_call(
            functools.partial(key_value_states, own, blocks, heads),
            out_shape=[half_bf, half_bf, states_f32, message],
            in_specs=[SM, ANY, ANY],
            out_specs=[VM] * 4,
            scratch_shapes=[dma((2 * heads,))],
            compiler_params=params(),
            cost_estimate=cost(2 * pairs * narrow, 4 * tokens * cols),
        )(doc_ids, keys, values)

    def scoring(own, k, v):
        return pl.pallas_call(
            functools.partial(local_scores, own, blocks, heads),
            out_shape=[half_bf, half_bf, half_f32, pltpu.VMEM((pairs * C, C), BF16)],
            in_specs=[VM, VM, ANY, ANY],
            out_specs=[VM] * 4,
            scratch_shapes=[dma((blocks,)), dma],
            compiler_params=params(),
            cost_estimate=cost(4 * pairs * wide, 4 * tokens * cols),
        )(k, v, queries, out_grad)

    def attending(own, inside, carry, q, sv, g, sums):
        ins = [doc_ids, inside, carry, q, sv, g, gain] + ([] if own else [sums])
        last = [pltpu.VMEM((C, HD), F32)] if own else [pltpu.VMEM((2 * lanes, C), F32)]
        return pl.pallas_call(
            functools.partial(attend, own, blocks, heads, lanes),
            out_shape=[half_f32, pltpu.VMEM((pairs * HD, HD), BF16)] + last,
            in_specs=[SM] + [VM] * (len(ins) - 1),
            out_specs=[VM] * 3,
            scratch_shapes=[] if own else [pltpu.VMEM((C, HD), F32)],
            input_output_aliases={4: 0},
            compiler_params=params(),
            cost_estimate=cost(2 * pairs * narrow, 1 << 20),
        )(*ins)

    def mixing(own, before, attended, q, g):
        ins = [doc_ids] + before + [attended, q, g, gain]
        outs = [half_bf, states_f32, message] + ([] if own else [column, column])
        scratch = [pltpu.VMEM((cols, HD), F32)]
        return pl.pallas_call(
            functools.partial(mixed, own, blocks, heads, lanes, tp),
            out_shape=outs,
            in_specs=[SM] + [VM] * (len(ins) - 1),
            out_specs=[VM] * len(outs),
            scratch_shapes=scratch if own else scratch + [pltpu.VMEM((HD, C), F32)],
            compiler_params=params(),
            cost_estimate=cost(2 * pairs * narrow, 1 << 20),
        )(*ins)

    def query_grads(own, k, v, q, attended, scale, grad, low, scores, so_far):
        ins = [k, v, q, attended, scale, gain, grad, low, scores] + list(so_far)
        stage = pltpu.VMEM((2, C, cols), BF16)
        return pl.pallas_call(
            functools.partial(query_side, own, blocks, heads),
            out_shape=[whole, whole, half_f32, half_f32],
            in_specs=[VM] * 9 + [HB] * len(so_far),
            out_specs=[HB, HB, VM, VM],
            scratch_shapes=[stage, stage, dma((2, 2))],
            input_output_aliases={9: 0, 10: 1} if own else {},
            compiler_params=params(),
            cost_estimate=cost(8 * pairs * wide, 4 * tokens * cols),
        )(*ins)

    def key_grads(own, inside, carry, k, v, key_local, value_local, so_far):
        ins = [doc_ids, inside, carry, k, v, key_local, value_local] + list(so_far)
        stage = pltpu.VMEM((2, C, cols), BF16)
        return pl.pallas_call(
            functools.partial(key_side, own, blocks, heads),
            out_shape=[whole, whole],
            in_specs=[SM] + [VM] * 6 + [HB] * len(so_far),
            out_specs=[HB, HB],
            scratch_shapes=[stage, stage, dma((2, 2))],
            input_output_aliases={} if own else {7: 0, 8: 1},
            compiler_params=params(),
            cost_estimate=cost(4 * pairs * narrow, 4 * tokens * cols),
        )(*ins)

    k1, v1, inside1, theirs = states(False)
    k0, v0, inside0, mine = states(True)
    carry0, carry1 = scan(theirs, mine, False)
    q1, g1, local1, scores1 = scoring(False, k1, v1)
    q0, g0, local0, scores0 = scoring(True, k0, v0)
    att0, low0, sums = attending(True, inside0, carry0, q0, local0, g0, None)
    att1, low1, sums = attending(False, inside1, carry1, q1, local1, g1, sums)
    parts = [sums] + [
        lax.ppermute(sums, "tp", [(i, (i + s) % tp) for i in range(tp)]) for s in range(1, tp)
    ]
    grad1, after1, theirs, scale, slope = mixing(False, parts, att1, q1, g1)
    grad0, after0, mine = mixing(True, [scale, slope], att0, q0, g0)
    carry0, carry1 = scan(theirs, mine, True)
    normed, query_grad, kl1, vl1 = query_grads(
        False, k1, v1, q1, att1, scale, grad1, low1, scores1, ()
    )
    normed, query_grad, kl0, vl0 = query_grads(
        True, k0, v0, q0, att0, scale, grad0, low0, scores0, (normed, query_grad)
    )
    key_grad, value_grad = key_grads(True, after0, carry0, k0, v0, kl0, vl0, ())
    key_grad, value_grad = key_grads(
        False, after1, carry1, k1, v1, kl1, vl1, (key_grad, value_grad)
    )
    return normed, query_grad, key_grad, value_grad


def solution(mesh):
    return jax.shard_map(
        local,
        mesh=mesh,
        in_specs=(
            P("ctx", "tp"),
            P("ctx", "tp"),
            P("ctx", "tp"),
            P("ctx", "tp"),
            P("tp"),
            P("ctx"),
        ),
        out_specs=(P("ctx", "tp"), P("ctx", "tp"), P("ctx", "tp"), P("ctx", "tp")),
        check_vma=False,
    )
```

profile of v0, /device:TPU:1, one launch (start us, length us, event | category | flops | bytes accessed | tf_op | source)
XLA Modules:
  0.0 96.0 jit_solution(9433456146480621704)
XLA Ops:
  0.6 0.0 copy-start
  0.6 1.9 %copy-done = bf16[1536,1024]{1,0:T(8,128)(2,1)S(1)} copy-done((bf16[1536,1024]{1,0:T(8,128)(2,1)S(1)}, bf16[1536,1024]{1,0:T(8,128)(2,1)}, u32[]{:S(2)}) %copy-start) | copy-done | bytes 3145752
  2.5 0.0 copy-start.1
  2.5 1.9 %copy-done.1 = bf16[1536,1024]{1,0:T(8,128)(2,1)S(1)} copy-done((bf16[1536,1024]{1,0:T(8,128)(2,1)S(1)}, bf16[1536,1024]{1,0:T(8,128)(2,1)}, u32[]{:S(2)}) %copy-start.1) | copy-done | bytes 3145752
  4.4 0.0 copy-start.5
  4.4 0.7 copy-done.5
  5.1 2.7 %shard_map.95 = (bf16[1536,512]{1,0:T(8,128)(2,1)S(1)}, bf16[1536,512]{1,0:T(8,128)(2,1)S(1)}, f32[3072,128]{1,0:T(8,128)S(1)}, f32[520,128]{1,0:T(8,128)S(1)}) custom-call(s32[6]{0:T(128)S(1)} %copy-done.5, bf16[1536,1024]{1,0:T(8,128)(2,1)S(1)} %copy-done, bf16[1536,1024]{1,0:T(8,128)(2,1)S(1)} %copy-done.1), custom_call_target="tpu_custom_call" | custom-call | flops 201326592 | bytes 3145728 | tf_op jit(solution)/shard_map/pallas_call | solution.py:419
  7.8 0.0 copy-start.2
  7.8 0.0 copy-start.3
  7.8 0.1 collective-permute-start
  7.9 2.8 %shard_map.93 = (bf16[1536,512]{1,0:T(8,128)(2,1)S(1)}, bf16[1536,512]{1,0:T(8,128)(2,1)S(1)}, f32[3072,128]{1,0:T(8,128)S(1)}, f32[520,128]{1,0:T(8,128)S(1)}) custom-call(s32[6]{0:T(128)S(1)} %copy-done.5, bf16[1536,1024]{1,0:T(8,128)(2,1)S(1)} %copy-done, bf16[1536,1024]{1,0:T(8,128)(2,1)S(1)} %copy-done.1), custom_call_target="tpu_custom_call" | custom-call | flops 201326592 | bytes 3145728 | tf_op jit(solution)/shard_map/pallas_call | solution.py:419
  10.7 0.0 collective-permute-done.refs_1_.refs_4_
  10.7 2.7 %collective-permute-start.1 = (f32[264,128]{1,0:T(8,128)S(1)}, f32[264,128]{1,0:T(8,128)S(1)}, u32[]{:S(2)}, u32[]{:S(2)}) collective-permute-start(f32[264,128]{1,0:T(8,128)S(1)} %get-tuple-element.64.refs_0_), channel_id=1, source_target_pairs={{0,8},{4,12},{8,0},{12,4},{16,24},{20,28},{24,16},{28,20},{1,9},{5... | collective-permute-start | bytes 405512 | tf_op jit(solution)/shard_map/ppermute | solution.py:329
  13.4 1.2 %collective-permute-start.2 = (f32[264,128]{1,0:T(8,128)S(1)}, f32[264,128]{1,0:T(8,128)S(1)}, u32[]{:S(2)}, u32[]{:S(2)}) collective-permute-start(f32[264,128]{1,0:T(8,128)S(1)} %get-tuple-element.65.refs_2_), channel_id=1, source_target_pairs={{0,16},{4,20},{8,24},{12,28},{16,0},{20,4},{24,8},{28,12},{1,17},{... | collective-permute-start | bytes 405512 | tf_op jit(solution)/shard_map/ppermute | solution.py:329
  14.7 2.7 %collective-permute-done.1.refs_1_.refs_0_ = f32[264,128]{1,0:T(8,128)S(1)} collective-permute-done((f32[264,128]{1,0:T(8,128)S(1)}, f32[264,128]{1,0:T(8,128)S(1)}, u32[]{:S(2)}, u32[]{:S(2)}) %collective-permute-start.1) | collective-permute-done | bytes 135200 | tf_op jit(solution)/shard_map/ppermute | solution.py:329
  17.4 0.9 collective-permute-done.2.refs_3_.refs_2_
  18.4 1.3 %collective-permute-start.3 = (f32[264,128]{1,0:T(8,128)S(1)}, f32[264,128]{1,0:T(8,128)S(1)}, u32[]{:S(2)}, u32[]{:S(2)}) collective-permute-start(f32[264,128]{1,0:T(8,128)S(1)} %get-tuple-element.66), channel_id=1, source_target_pairs={{0,16},{4,20},{8,24},{12,28},{16,0},{20,4},{24,8},{28,12},{1,17},{... | collective-permute-start | bytes 405512 | tf_op jit(solution)/shard_map/ppermute | solution.py:329
  19.7 0.3 collective-permute-start.4
  20.0 2.3 %collective-permute-done.3.refs_1_ = f32[264,128]{1,0:T(8,128)S(1)} collective-permute-done((f32[264,128]{1,0:T(8,128)S(1)}, f32[264,128]{1,0:T(8,128)S(1)}, u32[]{:S(2)}, u32[]{:S(2)}) %collective-permute-start.3) | collective-permute-done | bytes 135200 | tf_op jit(solution)/shard_map/ppermute | solution.py:329
  22.3 1.5 %collective-permute-done.4.refs_3_ = f32[264,128]{1,0:T(8,128)S(1)} collective-permute-done((f32[264,128]{1,0:T(8,128)S(1)}, f32[264,128]{1,0:T(8,128)S(1)}, u32[]{:S(2)}, u32[]{:S(2)}) %collective-permute-start.4) | collective-permute-done | bytes 135200 | tf_op jit(solution)/shard_map/ppermute | solution.py:329
  23.8 0.1 shard_map.98
  24.0 2.3 %collective-permute-start.5 = (f32[520,128]{1,0:T(8,128)S(1)}, f32[520,128]{1,0:T(8,128)S(1)}, u32[]{:S(2)}, u32[]{:S(2)}) collective-permute-start(f32[520,128]{1,0:T(8,128)S(1)} %get-tuple-element.73), channel_id=1, source_target_pairs={{0,4},{4,0},{8,12},{12,8},{16,20},{20,16},{24,28},{28,24},{1,5},{5... | collective-permute-start | bytes 798728 | tf_op jit(solution)/shard_map/ppermute | solution.py:329
  26.3 0.0 copy-done.2
  26.3 0.0 copy-done.3
  26.3 4.4 %shard_map.94 = (bf16[1536,512]{1,0:T(8,128)(2,1)S(1)}, bf16[1536,512]{1,0:T(8,128)(2,1)S(1)}, f32[1536,512]{1,0:T(8,128)S(1)}, bf16[6144,256]{1,0:T(8,128)(2,1)S(1)}) custom-call(bf16[1536,512]{1,0:T(8,128)(2,1)S(1)} %get-tuple-element.58.k, bf16[1536,512]{1,0:T(8,128)(2,1)S(1)} %get-tuple-element.59.v, bf16[1536,1024]{1,0:T(8,128)(2,1)S(1)} %copy-done.2, ...), custom_call_target="tpu_custom_call" | custom-call | flops 805306368 | bytes 3145728 | tf_op jit(solution)/shard_map/pallas_call | solution.py:430
  30.7 0.0 copy-start.4
  30.7 0.0 copy-start.6
  30.7 4.4 %shard_map.100 = (bf16[1536,512]{1,0:T(8,128)(2,1)S(1)}, bf16[1536,512]{1,0:T(8,128)(2,1)S(1)}, f32[1536,512]{1,0:T(8,128)S(1)}, bf16[6144,256]{1,0:T(8,128)(2,1)S(1)}) custom-call(bf16[1536,512]{1,0:T(8,128)(2,1)S(1)} %get-tuple-element.74.k, bf16[1536,512]{1,0:T(8,128)(2,1)S(1)} %get-tuple-element.75.v, bf16[1536,1024]{1,0:T(8,128)(2,1)S(1)} %copy-done.2, ...), custom_call_target="tpu_custom_call" | custom-call | flops 805306368 | bytes 3145728 | tf_op jit(solution)/shard_map/pallas_call | solution.py:430
  35.1 0.0 copy-done.4
  35.1 0.0 copy-done.6
  35.1 3.4 %shard_map.99 = (f32[1536,512]{1,0:T(8,128)S(1)}, bf16[3072,128]{1,0:T(8,128)(2,1)S(1)}, f32[256,128]{1,0:T(8,128)S(1)}) custom-call(s32[6]{0:T(128)S(1)} %copy-done.6, f32[3072,128]{1,0:T(8,128)S(1)} %get-tuple-element.61.inside, f32[520,128]{1,0:T(8,128)S(1)} %get-tuple-element.68.carry, ...), custom_call_target="tpu_custom_call", output_to_operand_aliasing={{0}: (4, {})} | custom-call | flops 201326592 | bytes 1048576 | tf_op jit(solution)/shard_map/pallas_call | solution.py:443
  38.5 0.0 collective-permute-done.5.carry
  38.5 3.5 %shard_map.101 = (f32[1536,512]{1,0:T(8,128)S(1)}, bf16[3072,128]{1,0:T(8,128)(2,1)S(1)}, f32[16,256]{1,0:T(8,128)S(1)}) custom-call(s32[6]{0:T(128)S(1)} %copy-done.6, f32[3072,128]{1,0:T(8,128)S(1)} %get-tuple-element.72.inside, f32[520,128]{1,0:T(8,128)S(1)} %collective-permute-done.5.carry, ...), custom_call_target="tpu_custom_call", output_to_operand_aliasing={{0}: (4, {})} | custom-call | flops 201326592 | bytes 1048576 | tf_op jit(solution)/shard_map/pallas_call | solution.py:443
  42.1 3.3 %collective-permute-start.8 = (f32[16,256]{1,0:T(8,128)S(1)}, f32[16,256]{1,0:T(8,128)S(1)}, u32[]{:S(2)}, u32[]{:S(2)}) collective-permute-start(f32[16,256]{1,0:T(8,128)S(1)} %get-tuple-element.80.rest_0_), channel_id=1, source_target_pairs={{0,3},{1,0},{2,1},{3,2},{4,7},{5,4},{6,5},{7,6},{8,11},{9,8},{10,9... | collective-permute-start | bytes 49160 | tf_op jit(solution)/shard_map/ppermute | solution.py:504
  45.4 0.0 collective-permute-start.7
  45.4 0.5 collective-permute-start.6
  45.9 0.4 collective-permute-done.8.rest_3_
  46.3 2.6 %collective-permute-done.7.rest_2_ = f32[16,256]{1,0:T(8,128)S(1)} collective-permute-done((f32[16,256]{1,0:T(8,128)S(1)}, f32[16,256]{1,0:T(8,128)S(1)}, u32[]{:S(2)}, u32[]{:S(2)}) %collective-permute-start.7) | collective-permute-done | bytes 16416 | tf_op jit(solution)/shard_map/ppermute | solution.py:504
  48.9 1.0 %collective-permute-done.6.rest_1_ = f32[16,256]{1,0:T(8,128)S(1)} collective-permute-done((f32[16,256]{1,0:T(8,128)S(1)}, f32[16,256]{1,0:T(8,128)S(1)}, u32[]{:S(2)}, u32[]{:S(2)}) %collective-permute-start.6) | collective-permute-done | bytes 16416 | tf_op jit(solution)/shard_map/ppermute | solution.py:504
  49.9 3.1 %shard_map.102 = (bf16[1536,512]{1,0:T(8,128)(2,1)S(1)}, f32[3072,128]{1,0:T(8,128)S(1)}, f32[520,128]{1,0:T(8,128)S(1)}, f32[1536,128]{1,0:T(8,128)S(1)}, f32[1536,128]{1,0:T(8,128)S(1)}) custom-call(s32[6]{0:T(128)S(1)} %copy-done.6, f32[16,256]{1,0:T(8,128)S(1)} %get-tuple-element.80.rest_0_, f32[16,256]{1,0:T(8,128)S(1)} %collective-permute-done.6.rest_1_, ...), custom_call_target="tpu_custom_call" | custom-call | flops 201326592 | bytes 1048576 | tf_op jit(solution)/shard_map/pallas_call | solution.py:458
  53.0 1.5 %collective-permute-start.9 = (f32[520,128]{1,0:T(8,128)S(1)}, f32[520,128]{1,0:T(8,128)S(1)}, u32[]{:S(2)}, u32[]{:S(2)}) collective-permute-start(f32[520,128]{1,0:T(8,128)S(1)} %get-tuple-element.96), channel_id=1, source_target_pairs={{0,4},{4,0},{8,12},{12,8},{16,20},{20,16},{24,28},{28,24},{1,5},{5... | collective-permute-start | bytes 798728 | tf_op jit(solution)/shard_map/ppermute | solution.py:329
  54.5 2.6 %shard_map.103 = (bf16[1536,512]{1,0:T(8,128)(2,1)S(1)}, f32[3072,128]{1,0:T(8,128)S(1)}, f32[520,128]{1,0:T(8,128)S(1)}) custom-call(s32[6]{0:T(128)S(1)} %copy-done.6, f32[1536,128]{1,0:T(8,128)S(1)} %get-tuple-element.82.rest_0_.scale, f32[1536,128]{1,0:T(8,128)S(1)} %get-tuple-element.83.rest_1_, f32[1536,512]{1,0:T(8,128)S(1)} %get-tuple-element.71.rest_2_.attended, ...), custom_call_target="tpu_custom_call" | custom-call | flops 201326592 | bytes 1048576 | tf_op jit(solution)/shard_map/pallas_call | solution.py:458
  57.1 0.0 collective-permute-done.9.refs_1_.refs_4_
  57.1 0.3 collective-permute-start.10
  57.4 0.2 collective-permute-start.11
  57.7 4.7 %collective-permute-done.10.refs_1_.refs_0_ = f32[264,128]{1,0:T(8,128)S(1)} collective-permute-done((f32[264,128]{1,0:T(8,128)S(1)}, f32[264,128]{1,0:T(8,128)S(1)}, u32[]{:S(2)}, u32[]{:S(2)}) %collective-permute-start.10) | collective-permute-done | bytes 135200 | tf_op jit(solution)/shard_map/ppermute | solution.py:329
  62.4 0.0 collective-permute-done.11.refs_3_.refs_2_
  62.4 0.1 shard_map.107
  62.5 0.3 collective-permute-start.12
  62.7 1.1 %collective-permute-start.13 = (f32[264,128]{1,0:T(8,128)S(1)}, f32[264,128]{1,0:T(8,128)S(1)}, u32[]{:S(2)}, u32[]{:S(2)}) collective-permute-start(f32[264,128]{1,0:T(8,128)S(1)} %get-tuple-element.100), channel_id=1, source_target_pairs={{0,8},{4,12},{8,0},{12,4},{16,24},{20,28},{24,16},{28,20},{1,9},{5... | collective-permute-start | bytes 405512 | tf_op jit(solution)/shard_map/ppermute | solution.py:329
  63.9 2.5 %collective-permute-done.12.refs_1_ = f32[264,128]{1,0:T(8,128)S(1)} collective-permute-done((f32[264,128]{1,0:T(8,128)S(1)}, f32[264,128]{1,0:T(8,128)S(1)}, u32[]{:S(2)}, u32[]{:S(2)}) %collective-permute-start.12) | collective-permute-done | bytes 135200 | tf_op jit(solution)/shard_map/ppermute | solution.py:329
  66.4 0.5 collective-permute-done.13.refs_3_
  66.9 0.1 shard_map.108
  67.0 2.2 %collective-permute-start.14 = (f32[520,128]{1,0:T(8,128)S(1)}, f32[520,128]{1,0:T(8,128)S(1)}, u32[]{:S(2)}, u32[]{:S(2)}) collective-permute-start(f32[520,128]{1,0:T(8,128)S(1)} %get-tuple-element.101), channel_id=1, source_target_pairs={{0,4},{4,0},{8,12},{12,8},{16,20},{20,16},{24,28},{28,24},{1,5},{5... | collective-permute-start | bytes 798728 | tf_op jit(solution)/shard_map/ppermute | solution.py:329
  69.3 9.1 %shard_map.104 = (bf16[1536,1024]{1,0:T(8,128)(2,1)}, bf16[1536,1024]{1,0:T(8,128)(2,1)}, f32[1536,512]{1,0:T(8,128)S(1)}, f32[1536,512]{1,0:T(8,128)S(1)}) custom-call(bf16[1536,512]{1,0:T(8,128)(2,1)S(1)} %get-tuple-element.74.k, bf16[1536,512]{1,0:T(8,128)(2,1)S(1)} %get-tuple-element.75.v, bf16[1536,512]{1,0:T(8,128)(2,1)S(1)} %get-tuple-element.76.q.rest_5_, ...), custom_call_target="tpu_custom_call" | custom-call | flops 1610612736 | bytes 3145728 | tf_op jit(solution)/shard_map/pallas_call | solution.py:471
  78.4 9.1 %shard_map.105 = (bf16[1536,1024]{1,0:T(8,128)(2,1)}, bf16[1536,1024]{1,0:T(8,128)(2,1)}, f32[1536,512]{1,0:T(8,128)S(1)}, f32[1536,512]{1,0:T(8,128)S(1)}) custom-call(bf16[1536,512]{1,0:T(8,128)(2,1)S(1)} %get-tuple-element.58.k, bf16[1536,512]{1,0:T(8,128)(2,1)S(1)} %get-tuple-element.59.v, ...), custom_call_target="tpu_custom_call", output_to_operand_aliasing={{0}: (9, {}), {1}: (10, {})} | custom-call | flops 1610612736 | bytes 3145728 | tf_op jit(solution)/shard_map/pallas_call | solution.py:471
  87.6 4.1 %shard_map.109 = (bf16[1536,1024]{1,0:T(8,128)(2,1)}, bf16[1536,1024]{1,0:T(8,128)(2,1)}) custom-call(s32[6]{0:T(128)S(1)} %copy-done.6, f32[3072,128]{1,0:T(8,128)S(1)} %get-tuple-element.104.inside, f32[520,128]{1,0:T(8,128)S(1)} %get-tuple-element.105.carry, bf16[1536,512]{1,0:T(8,128)(2,1)S(1)} %get-tuple-element.58.k, ...), custom_call_target="tpu_custom_call" | custom-call | flops 402653184 | bytes 3145728 | tf_op jit(solution)/shard_map/pallas_call | solution.py:485
  91.7 0.0 collective-permute-done.14.carry
  91.7 4.2 %shard_map.110 = (bf16[1536,1024]{1,0:T(8,128)(2,1)}, bf16[1536,1024]{1,0:T(8,128)(2,1)}) custom-call(s32[6]{0:T(128)S(1)} %copy-done.6, f32[3072,128]{1,0:T(8,128)S(1)} %get-tuple-element.94.inside, f32[520,128]{1,0:T(8,128)S(1)} %collective-permute-done.14.carry, ...), custom_call_target="tpu_custom_call", output_to_operand_aliasing={{0}: (7, {}), {1}: (8, {})} | custom-call | flops 402653184 | bytes 3145728 | tf_op jit(solution)/shard_map/pallas_call | solution.py:485
  (3 shorter events, 0.1 us)
Async XLA Ops:
  0.6 1.9 %copy-start = (bf16[1536,1024]{1,0:T(8,128)(2,1)S(1)}, bf16[1536,1024]{1,0:T(8,128)(2,1)}, u32[]{:S(2)}) copy-start(bf16[1536,1024]{1,0:T(8,128)(2,1)} %k_hbm.3) | copy-start | bytes 9437188
  2.5 1.9 %copy-start.1 = (bf16[1536,1024]{1,0:T(8,128)(2,1)S(1)}, bf16[1536,1024]{1,0:T(8,128)(2,1)}, u32[]{:S(2)}) copy-start(bf16[1536,1024]{1,0:T(8,128)(2,1)} %v_hbm.3) | copy-start | bytes 9437188
  4.4 0.7 copy-start.5
  7.8 18.5 %copy-start.2 = (bf16[1536,1024]{1,0:T(8,128)(2,1)S(1)}, bf16[1536,1024]{1,0:T(8,128)(2,1)}, u32[]{:S(2)}) copy-start(bf16[1536,1024]{1,0:T(8,128)(2,1)} %q_hbm.3) | copy-start | bytes 9437188
  7.8 18.5 %copy-start.3 = (bf16[1536,1024]{1,0:T(8,128)(2,1)S(1)}, bf16[1536,1024]{1,0:T(8,128)(2,1)}, u32[]{:S(2)}) copy-start(bf16[1536,1024]{1,0:T(8,128)(2,1)} %g_hbm.3) | copy-start | bytes 9437188
  7.8 2.9 %collective-permute-start = (f32[520,128]{1,0:T(8,128)S(1)}, f32[520,128]{1,0:T(8,128)S(1)}, u32[]{:S(2)}, u32[]{:S(2)}) collective-permute-start(f32[520,128]{1,0:T(8,128)S(1)} %get-tuple-element.63), channel_id=1, source_target_pairs={{0,4},{4,0},{8,12},{12,8},{16,20},{20,16},{24,28},{28,24},{1,5},{5... | collective-permute-start | bytes 798728 | tf_op jit(solution)/shard_map/ppermute | solution.py:329
  10.7 6.7 %collective-permute-start.1 = (f32[264,128]{1,0:T(8,128)S(1)}, f32[264,128]{1,0:T(8,128)S(1)}, u32[]{:S(2)}, u32[]{:S(2)}) collective-permute-start(f32[264,128]{1,0:T(8,128)S(1)} %get-tuple-element.64.refs_0_), channel_id=1, source_target_pairs={{0,8},{4,12},{8,0},{12,4},{16,24},{20,28},{24,16},{28,20},{1,9},{5... | collective-permute-start | bytes 405512 | tf_op jit(solution)/shard_map/ppermute | solution.py:329
  13.4 4.9 %collective-permute-start.2 = (f32[264,128]{1,0:T(8,128)S(1)}, f32[264,128]{1,0:T(8,128)S(1)}, u32[]{:S(2)}, u32[]{:S(2)}) collective-permute-start(f32[264,128]{1,0:T(8,128)S(1)} %get-tuple-element.65.refs_2_), channel_id=1, source_target_pairs={{0,16},{4,20},{8,24},{12,28},{16,0},{20,4},{24,8},{28,12},{1,17},{... | collective-permute-start | bytes 405512 | tf_op jit(solution)/shard_map/ppermute | solution.py:329
  18.4 3.9 %collective-permute-start.3 = (f32[264,128]{1,0:T(8,128)S(1)}, f32[264,128]{1,0:T(8,128)S(1)}, u32[]{:S(2)}, u32[]{:S(2)}) collective-permute-start(f32[264,128]{1,0:T(8,128)S(1)} %get-tuple-element.66), channel_id=1, source_target_pairs={{0,16},{4,20},{8,24},{12,28},{16,0},{20,4},{24,8},{28,12},{1,17},{... | collective-permute-start | bytes 405512 | tf_op jit(solution)/shard_map/ppermute | solution.py:329
  19.7 4.2 %collective-permute-start.4 = (f32[264,128]{1,0:T(8,128)S(1)}, f32[264,128]{1,0:T(8,128)S(1)}, u32[]{:S(2)}, u32[]{:S(2)}) collective-permute-start(f32[264,128]{1,0:T(8,128)S(1)} %get-tuple-element.67), channel_id=1, source_target_pairs={{0,8},{4,12},{8,0},{12,4},{16,24},{20,28},{24,16},{28,20},{1,9},{5... | collective-permute-start | bytes 405512 | tf_op jit(solution)/shard_map/ppermute | solution.py:329
  24.0 14.6 %collective-permute-start.5 = (f32[520,128]{1,0:T(8,128)S(1)}, f32[520,128]{1,0:T(8,128)S(1)}, u32[]{:S(2)}, u32[]{:S(2)}) collective-permute-start(f32[520,128]{1,0:T(8,128)S(1)} %get-tuple-element.73), channel_id=1, source_target_pairs={{0,4},{4,0},{8,12},{12,8},{16,20},{20,16},{24,28},{28,24},{1,5},{5... | collective-permute-start | bytes 798728 | tf_op jit(solution)/shard_map/ppermute | solution.py:329
  30.7 4.4 %copy-start.4 = (f32[1024]{0:T(1024)S(1)}, f32[1024]{0:T(1024)}, u32[]{:S(2)}) copy-start(f32[1024]{0:T(1024)} %param.10) | copy-start | bytes 12292
  30.7 4.4 %copy-start.6 = (s32[6]{0:T(128)S(1)}, s32[6]{0:T(128)}, u32[]{:S(2)}) copy-start(s32[6]{0:T(128)} %docs.15) | copy-start | bytes 76
  42.1 4.2 %collective-permute-start.8 = (f32[16,256]{1,0:T(8,128)S(1)}, f32[16,256]{1,0:T(8,128)S(1)}, u32[]{:S(2)}, u32[]{:S(2)}) collective-permute-start(f32[16,256]{1,0:T(8,128)S(1)} %get-tuple-element.80.rest_0_), channel_id=1, source_target_pairs={{0,3},{1,0},{2,1},{3,2},{4,7},{5,4},{6,5},{7,6},{8,11},{9,8},{10,9... | collective-permute-start | bytes 49160 | tf_op jit(solution)/shard_map/ppermute | solution.py:504
  45.4 3.5 %collective-permute-start.7 = (f32[16,256]{1,0:T(8,128)S(1)}, f32[16,256]{1,0:T(8,128)S(1)}, u32[]{:S(2)}, u32[]{:S(2)}) collective-permute-start(f32[16,256]{1,0:T(8,128)S(1)} %get-tuple-element.80.rest_0_), channel_id=1, source_target_pairs={{0,2},{1,3},{2,0},{3,1},{4,6},{5,7},{6,4},{7,5},{8,10},{9,11},{10,... | collective-permute-start | bytes 49160 | tf_op jit(solution)/shard_map/ppermute | solution.py:504
  45.4 4.5 %collective-permute-start.6 = (f32[16,256]{1,0:T(8,128)S(1)}, f32[16,256]{1,0:T(8,128)S(1)}, u32[]{:S(2)}, u32[]{:S(2)}) collective-permute-start(f32[16,256]{1,0:T(8,128)S(1)} %get-tuple-element.80.rest_0_), channel_id=1, source_target_pairs={{0,1},{1,2},{2,3},{3,0},{4,5},{5,6},{6,7},{7,4},{8,9},{9,10},{10,1... | collective-permute-start | bytes 49160 | tf_op jit(solution)/shard_map/ppermute | solution.py:504
  53.0 4.1 %collective-permute-start.9 = (f32[520,128]{1,0:T(8,128)S(1)}, f32[520,128]{1,0:T(8,128)S(1)}, u32[]{:S(2)}, u32[]{:S(2)}) collective-permute-start(f32[520,128]{1,0:T(8,128)S(1)} %get-tuple-element.96), channel_id=1, source_target_pairs={{0,4},{4,0},{8,12},{12,8},{16,20},{20,16},{24,28},{28,24},{1,5},{5... | collective-permute-start | bytes 798728 | tf_op jit(solution)/shard_map/ppermute | solution.py:329
  57.1 5.3 %collective-permute-start.10 = (f32[264,128]{1,0:T(8,128)S(1)}, f32[264,128]{1,0:T(8,128)S(1)}, u32[]{:S(2)}, u32[]{:S(2)}) collective-permute-start(f32[264,128]{1,0:T(8,128)S(1)} %get-tuple-element.97.refs_0_), channel_id=1, source_target_pairs={{0,8},{4,12},{8,0},{12,4},{16,24},{20,28},{24,16},{28,20},{1,9},{5... | collective-permute-start | bytes 405512 | tf_op jit(solution)/shard_map/ppermute | solution.py:329
  57.4 5.0 %collective-permute-start.11 = (f32[264,128]{1,0:T(8,128)S(1)}, f32[264,128]{1,0:T(8,128)S(1)}, u32[]{:S(2)}, u32[]{:S(2)}) collective-permute-start(f32[264,128]{1,0:T(8,128)S(1)} %get-tuple-element.98.refs_2_), channel_id=1, source_target_pairs={{0,16},{4,20},{8,24},{12,28},{16,0},{20,4},{24,8},{28,12},{1,17},{... | collective-permute-start | bytes 405512 | tf_op jit(solution)/shard_map/ppermute | solution.py:329
  62.5 3.9 %collective-permute-start.12 = (f32[264,128]{1,0:T(8,128)S(1)}, f32[264,128]{1,0:T(8,128)S(1)}, u32[]{:S(2)}, u32[]{:S(2)}) collective-permute-start(f32[264,128]{1,0:T(8,128)S(1)} %get-tuple-element.99), channel_id=1, source_target_pairs={{0,16},{4,20},{8,24},{12,28},{16,0},{20,4},{24,8},{28,12},{1,17},{... | collective-permute-start | bytes 405512 | tf_op jit(solution)/shard_map/ppermute | solution.py:329
  62.7 4.2 %collective-permute-start.13 = (f32[264,128]{1,0:T(8,128)S(1)}, f32[264,128]{1,0:T(8,128)S(1)}, u32[]{:S(2)}, u32[]{:S(2)}) collective-permute-start(f32[264,128]{1,0:T(8,128)S(1)} %get-tuple-element.100), channel_id=1, source_target_pairs={{0,8},{4,12},{8,0},{12,4},{16,24},{20,28},{24,16},{28,20},{1,9},{5... | collective-permute-start | bytes 405512 | tf_op jit(solution)/shard_map/ppermute | solution.py:329
  67.0 24.7 %collective-permute-start.14 = (f32[520,128]{1,0:T(8,128)S(1)}, f32[520,128]{1,0:T(8,128)S(1)}, u32[]{:S(2)}, u32[]{:S(2)}) collective-permute-start(f32[520,128]{1,0:T(8,128)S(1)} %get-tuple-element.101), channel_id=1, source_target_pairs={{0,4},{4,0},{8,12},{12,8},{16,20},{20,16},{24,28},{28,24},{1,5},{5... | collective-permute-start | bytes 798728 | tf_op jit(solution)/shard_map/ppermute | solution.py:329
where the time goes:
time: 96.2 us; the launch traced here: 96 us
  Pallas kernels  53.8 us (56%)
  waiting for transfers between devices  19.2 us (20%)
  starting transfers between devices  17.5 us (18%)
  local copies, waits for them, and re-layouts  4.45 us (5%)
  between operations  0.99 us (1%)
    pallas_call x2, Pallas kernels, query_grads(): pl.pallas_call(functools.partial(query_side, own, blocks, heads), out_sha...  18.2 us
    ppermute x12, waiting for transfers between devices, swap(): return lax.ppermute(message, 'ctx', [(i, i ^ 1 << b) for i in range(size)])  15.2 us
    ppermute x12, starting transfers between devices, swap(): return lax.ppermute(message, 'ctx', [(i, i ^ 1 << b) for i in range(size)])  13.7 us
    pallas_call x2, Pallas kernels, scoring(): pl.pallas_call(functools.partial(local_scores, own, blocks, heads), out_s...  8.78 us
    pallas_call x2, Pallas kernels, key_grads(): pl.pallas_call(functools.partial(key_side, own, blocks, heads), out_shape...  8.3 us
    pallas_call x2, Pallas kernels, attending(): pl.pallas_call(functools.partial(attend, own, blocks, heads, lanes), out_...  6.93 us
    pallas_call x2, Pallas kernels, mixing(): pl.pallas_call(functools.partial(mixed, own, blocks, heads, lanes, tp), o...  5.7 us
    pallas_call x2, Pallas kernels, states(): pl.pallas_call(functools.partial(key_value_states, own, blocks, heads), o...  5.44 us
  transfers between devices with their start and end apart: 15, of which 10 were waited for; matrix products, arithmetic and copies ran while one was open for 0% of the time, Pallas kernels for 42%

commit v1 on v0

--- a/solution.py
+++ b/solution.py
@@ -13,6 +13,7 @@
 PAD = 8
 NEVER = -1.0e9
 MIB = 1 << 20
+UNROLL = 1
 
 epsilon = 1e-06
 
@@ -45,6 +46,10 @@
     core = lax.rem(lax.axis_index("ctx"), 2)
     half = core if own else 1 - core
     return pl.multiple_of(half * cols, 128)
+
+
+def label(name, own):
+    return name + ("_own" if own else "_other")
 
 
 def head(h):
@@ -74,11 +79,12 @@
     for h in range(heads):
         for copy in copies[h]:
             copy.wait()
+        per_block = [pl.ds(n * C, C) for n in range(blocks)]
+        sums = [dot(k[rows, head(h)], v[rows, head(h)], TN) for rows in per_block]
         running = jnp.zeros((HD, HD), F32)
         for n in range(blocks):
             inside[state_rows(n, h, heads), :] = running
-            rows = pl.ds(n * C, C)
-            total = running + dot(k[rows, head(h)], v[rows, head(h)], TN)
+            total = running + sums[n]
             if n + 1 < blocks:
                 running = jnp.where(docs[n] == docs[n + 1], total, 0.0)
             else:
@@ -86,33 +92,31 @@
     message[heads * HD :, :] = jnp.full((PAD, HD), docs[blocks - 1].astype(F32), F32)
 
 
-def local_scores(own, blocks, heads, k, v, q_hbm, g_hbm, q, g, local, scores, sems, gsem):
+def causal_mask():
+    return lax.broadcasted_iota(jnp.int32, (C, C), 0) >= lax.broadcasted_iota(jnp.int32, (C, C), 1)
+
+
+def score_rows(n, h, heads):
+    return pl.ds(pl.multiple_of((n * heads + h) * C, C), C)
+
+
+def local_scores(own, blocks, heads, after, k, v, q, local, scores, done):
     off = half_start(own, heads * HD)
-    cols = pl.ds(off, heads * HD)
-
-    def q_copy(n):
-        return pltpu.make_async_copy(q_hbm.at[block(n), cols], q.at[block(n), :], sems.at[n])
-
-    for n in range(blocks):
-        q_copy(n).start()
-    g_copy = pltpu.make_async_copy(g_hbm.at[:, cols], g, gsem)
-    g_copy.start()
-    causal = lax.broadcasted_iota(jnp.int32, (C, C), 0) >= lax.broadcasted_iota(
-        jnp.int32, (C, C), 1
-    )
+    causal = causal_mask()
+    every = range(heads)
 
     def step(n, carry):
-        q_copy(n).wait()
         rows = block(n)
-        for h in range(heads):
-            s = dot(q[rows, head(h)], k[rows, head(h)], NT)
-            s = jnp.where(causal, s, 0.0).astype(BF16)
-            scores[pl.ds(pl.multiple_of((n * heads + h) * C, C), C), :] = s
-            local[rows, head(h)] = dot(s, v[rows, head(h)], NN)
+        raw = [dot(q[rows, pl.ds(off + h * HD, HD)], k[rows, head(h)], NT) for h in every]
+        low = [jnp.where(causal, s, 0.0).astype(BF16) for s in raw]
+        outs = [dot(low[h], v[rows, head(h)], NN) for h in every]
+        for h in every:
+            scores[score_rows(n, h, heads), :] = low[h]
+            local[rows, head(h)] = outs[h]
         return carry
 
-    lax.fori_loop(0, blocks, step, 0)
-    g_copy.wait()
+    lax.fori_loop(0, blocks, step, 0, unroll=UNROLL)
+    done[...] = jnp.zeros(done.shape, F32)
 
 
 def attend(own, blocks, heads, lanes, docs, inside, carry, q, local, g, gain, *rest):
@@ -125,28 +129,37 @@
     off = half_start(own, heads * HD)
     gains = gain[:, pl.ds(off, heads * HD)]
     lane = lax.broadcasted_iota(jnp.int32, (C, HD), 1)
+    every = range(heads)
 
     def step(n, carried):
         rows = block(n)
         hit = carry[heads * HD : heads * HD + 1, :] == docs[n].astype(F32)
-        square = jnp.zeros((C, HD), F32)
-        inner = jnp.zeros((C, HD), F32)
-        for h in range(heads):
-            here = state_rows(n, h, heads)
-            state = inside[here, :] + jnp.where(hit, carry[head(h), :], 0.0)
-            state_low = state.astype(BF16)
-            low[here, :] = state_low
-            out = local[rows, head(h)] + dot(q[rows, head(h)], state_low, NN)
-            attended[rows, head(h)] = out
-            weighted = g[rows, head(h)].astype(F32) * gains[:, h * HD : (h + 1) * HD]
-            square += out * out
-            inner += weighted * out
+        states = []
+        for h in every:
+            state = inside[state_rows(n, h, heads), :] + jnp.where(hit, carry[head(h), :], 0.0)
+            states.append(state.astype(BF16))
+        outs = [dot(q[rows, pl.ds(off + h * HD, HD)], states[h], NN) for h in every]
+        outs = [outs[h] + local[rows, head(h)] for h in every]
+        square = functools.reduce(jnp.add, [out * out for out in outs])
+        inner = functools.reduce(
+            jnp.add,
+            [
+                g[rows, pl.ds(off + h * HD, HD)].astype(F32)
+                * gains[:, h * HD : (h + 1) * HD]
+                * outs[h]
+                for h in every
+            ],
+        )
         square = jnp.sum(square, axis=1, keepdims=True)
         inner = jnp.sum(inner, axis=1, keepdims=True)
-        sums[...] += jnp.where(lane == n, square, 0.0) + jnp.where(lane == n + lanes, inner, 0.0)
+        placed = jnp.where(lane == n, square, 0.0) + jnp.where(lane == n + lanes, inner, 0.0)
+        for h in every:
+            low[state_rows(n, h, heads), :] = states[h]
+            attended[rows, head(h)] = outs[h]
+        sums[...] += placed
         return carried
 
-    lax.fori_loop(0, blocks, step, 0)
+    lax.fori_loop(0, blocks, step, 0, unroll=UNROLL)
     if not own:
         message[...] = jnp.transpose(sums[...])[: 2 * lanes, :]
 
@@ -173,6 +186,7 @@
     off = half_start(own, heads * HD)
     gains = gain[:, pl.ds(off, heads * HD)]
     running[...] = jnp.zeros((heads * HD, HD), F32)
+    every = range(heads)
 
     def step(i, carried):
         n = blocks - 1 - i
@@ -180,18 +194,22 @@
         linked = docs[n] == docs[jnp.maximum(n - 1, 0)]
         r = scale[rows, :]
         s = slope[rows, :]
-        for h in range(heads):
-            weighted = g[rows, head(h)].astype(F32) * gains[:, h * HD : (h + 1) * HD]
-            d = (r * weighted - attended[rows, head(h)] * s).astype(BF16)
-            grad[rows, head(h)] = d
-            state = running[head(h), :]
-            inside[state_rows(n, h, heads), :] = state
-            state = state + dot(q[rows, head(h)], d, TN)
-            message[head(h), :] = state
-            running[head(h), :] = jnp.where(linked, state, 0.0)
+        ds = []
+        for h in every:
+            weighted = g[rows, pl.ds(off + h * HD, HD)].astype(F32)
+            weighted = weighted * gains[:, h * HD : (h + 1) * HD]
+            ds.append((r * weighted - attended[rows, head(h)] * s).astype(BF16))
+        sums = [dot(q[rows, pl.ds(off + h * HD, HD)], ds[h], TN) for h in every]
+        befores = [running[head(h), :] for h in every]
+        for h in every:
+            grad[rows, head(h)] = ds[h]
+            inside[state_rows(n, h, heads), :] = befores[h]
+            total = befores[h] + sums[h]
+            message[head(h), :] = total
+            running[head(h), :] = jnp.where(linked, total, 0.0)
         return carried
 
-    lax.fori_loop(0, blocks, step, 0)
+    lax.fori_loop(0, blocks, step, 0, unroll=UNROLL)
     message[heads * HD :, :] = jnp.full((PAD, HD), -docs[0].astype(F32), F32)
 
 
@@ -203,18 +221,15 @@
     ]
 
 
-def query_side(own, blocks, heads, k, v, q, attended, scale, gain, grad, low, scores, *rest):
-    if not own:
-        normed, query_grad, key_local, value_local, stage_n, stage_q, sems = rest
-    else:
-        _, _, normed, query_grad, key_local, value_local, stage_n, stage_q, sems = rest
+def query_side(own, blocks, heads, after, k, v, q, attended, scale, gain, grad, low, scores, *rest):
+    rest = rest[2:] if own else rest
+    normed, query_grad, key_local, value_local, done, stage_n, stage_q, sems = rest
     off = half_start(own, heads * HD)
     cols = pl.ds(off, heads * HD)
     gains = gain[:, cols]
     pairs = ((stage_n, normed), (stage_q, query_grad))
-    causal = lax.broadcasted_iota(jnp.int32, (C, C), 0) >= lax.broadcasted_iota(
-        jnp.int32, (C, C), 1
-    )
+    causal = causal_mask()
+    every = range(heads)
 
     def step(n, carried):
         rows = block(n)
@@ -226,17 +241,23 @@
                 copy.wait()
 
         r = scale[rows, :]
-        for h in range(heads):
-            d = grad[rows, head(h)]
-            gs = dot(d, v[rows, head(h)], NT)
-            gs = jnp.where(causal, gs, 0.0).astype(BF16)
-            qg = dot(d, low[state_rows(n, h, heads), :], NT) + dot(gs, k[rows, head(h)], NN)
-            stage_q[slot, :, head(h)] = qg.astype(BF16)
-            key_local[rows, head(h)] = dot(gs, q[rows, head(h)], TN)
-            s = scores[pl.ds(pl.multiple_of((n * heads + h) * C, C), C), :]
-            value_local[rows, head(h)] = dot(s, d, TN)
-            out = attended[rows, head(h)] * r * gains[:, h * HD : (h + 1) * HD]
-            stage_n[slot, :, head(h)] = out.astype(BF16)
+        ds = [grad[rows, head(h)] for h in every]
+        raw = [dot(ds[h], v[rows, head(h)], NT) for h in every]
+        gs = [jnp.where(causal, x, 0.0).astype(BF16) for x in raw]
+        qg = [
+            dot(ds[h], low[state_rows(n, h, heads), :], NT) + dot(gs[h], k[rows, head(h)], NN)
+            for h in every
+        ]
+        kg = [dot(gs[h], q[rows, pl.ds(off + h * HD, HD)], TN) for h in every]
+        vg = [dot(scores[score_rows(n, h, heads), :], ds[h], TN) for h in every]
+        outs = [
+            attended[rows, head(h)] * r * gains[:, h * HD : (h + 1) * HD] for h in every
+        ]
+        for h in every:
+            stage_q[slot, :, head(h)] = qg[h].astype(BF16)
+            stage_n[slot, :, head(h)] = outs[h].astype(BF16)
+            key_local[rows, head(h)] = kg[h]
+            value_local[rows, head(h)] = vg[h]
         for copy in store_blocks(n, pairs, cols, sems):
             copy.start()
         return carried
@@ -245,16 +266,16 @@
     for n in range(max(blocks - 2, 0), blocks):
         for copy in store_blocks(n, pairs, cols, sems):
             copy.wait()
+    done[...] = jnp.zeros(done.shape, F32)
 
 
 def key_side(own, blocks, heads, docs, inside, carry, k, v, key_local, value_local, *rest):
-    if own:
-        key_grad, value_grad, stage_k, stage_v, sems = rest
-    else:
-        _, _, key_grad, value_grad, stage_k, stage_v, sems = rest
+    rest = rest if own else rest[2:]
+    key_grad, value_grad, stage_k, stage_v, sems = rest
     off = half_start(own, heads * HD)
     cols = pl.ds(off, heads * HD)
     pairs = ((stage_k, key_grad), (stage_v, value_grad))
+    every = range(heads)
 
     def step(n, carried):
         rows = block(n)
@@ -266,13 +287,17 @@
                 copy.wait()
 
         hit = carry[heads * HD : heads * HD + 1, :] == -docs[n].astype(F32)
-        for h in range(heads):
+        states = []
+        for h in every:
             state = inside[state_rows(n, h, heads), :] + jnp.where(hit, carry[head(h), :], 0.0)
-            leave = state.astype(BF16)
-            kg = key_local[rows, head(h)] + dot(v[rows, head(h)], leave, NT)
-            vg = value_local[rows, head(h)] + dot(k[rows, head(h)], leave, NN)
-            stage_k[slot, :, head(h)] = kg.astype(BF16)
-            stage_v[slot, :, head(h)] = vg.astype(BF16)
+            states.append(state.astype(BF16))
+        kg = [dot(v[rows, head(h)], states[h], NT) for h in every]
+        vg = [dot(k[rows, head(h)], states[h], NN) for h in every]
+        kg = [(kg[h] + key_local[rows, head(h)]).astype(BF16) for h in every]
+        vg = [(vg[h] + value_local[rows, head(h)]).astype(BF16) for h in every]
+        for h in every:
+            stage_k[slot, :, head(h)] = kg[h]
+            stage_v[slot, :, head(h)] = vg[h]
         for copy in store_blocks(n, pairs, cols, sems):
             copy.start()
         return carried
@@ -312,10 +337,12 @@
         result[at:, :] = jnp.broadcast_to(latest, (PAD, HD))
 
 
-def merge(ins, outs, reverse):
+def merge(ins, outs, reverse, after=()):
     shapes = [pltpu.VMEM((sum(rows for rows, _ in pieces) + PAD, HD), F32) for pieces in outs]
+    ins = list(ins) + list(after)
     return pl.pallas_call(
         functools.partial(merge_kernel, reverse, outs, len(ins)),
+        name="merge",
         out_shape=shapes,
         in_specs=[VM] * len(ins),
         out_specs=[VM] * len(outs),
@@ -329,7 +356,7 @@
     return lax.ppermute(message, "ctx", [(i, i ^ (1 << b)) for i in range(size)])
 
 
-def scan(theirs, mine, reverse):
+def scan(theirs, mine, reverse, first_work, second_work):
     rows = mine.shape[0] - PAD
     part = rows // 2
     top = lax.axis_size("ctx").bit_length() - 1
@@ -359,6 +386,7 @@
         )
         before_a, before_b = [pa], [pb]
     first_a, first_b = swap(total_a, lo), swap(total_b, hi)
+    first_done = first_work(total_a)
     next_a, next_b = merge(
         [total_a, first_a, total_b, first_b],
         [
@@ -374,8 +402,10 @@
             ],
         ],
         reverse,
+        first_done[-1:],
     )
     second_a, second_b = swap(next_a, hi), swap(next_b, lo)
+    second_done = second_work(next_a, first_done)
 
     def carried(neighbour, flag):
         terms_a = [(0, 0, lambda bit: bit(lo) == 1), (1, 0, lambda bit: bit(hi) == 1)]
@@ -392,8 +422,9 @@
         [first_a, second_a, first_b, second_b, beside, mine] + before_a + before_b,
         [carried(4, lambda bit: bit(0) == 1), carried(5, lambda bit: bit(0) == 0)],
         reverse,
+        second_done[-1:],
     )
-    return carry_mine, swap(carry_theirs, 0)
+    return carry_mine, swap(carry_theirs, 0), first_done[:-1], second_done[:-1]
 
 
 def local(queries, keys, values, out_grad, gain, doc_ids):
@@ -415,33 +446,41 @@
     whole = pltpu.HBM((tokens, features), BF16)
     column = pltpu.VMEM((tokens, HD), F32)
 
+    keys, values = [pltpu.with_memory_space_constraint(x, pltpu.HBM) for x in (keys, values)]
+    queries, out_grad = [
+        pltpu.with_memory_space_constraint(x, pltpu.VMEM) for x in (queries, out_grad)
+    ]
+    token = pltpu.VMEM((PAD, HD), F32)
+
     def states(own):
         return pl.pallas_call(
             functools.partial(key_value_states, own, blocks, heads),
+            name=label("states", own),
             out_shape=[half_bf, half_bf, states_f32, message],
-            in_specs=[SM, ANY, ANY],
+            in_specs=[SM, HB, HB],
             out_specs=[VM] * 4,
             scratch_shapes=[dma((2 * heads,))],
             compiler_params=params(),
             cost_estimate=cost(2 * pairs * narrow, 4 * tokens * cols),
         )(doc_ids, keys, values)
 
-    def scoring(own, k, v):
+    def scoring(own, k, v, after):
         return pl.pallas_call(
             functools.partial(local_scores, own, blocks, heads),
-            out_shape=[half_bf, half_bf, half_f32, pltpu.VMEM((pairs * C, C), BF16)],
-            in_specs=[VM, VM, ANY, ANY],
-            out_specs=[VM] * 4,
-            scratch_shapes=[dma((blocks,)), dma],
+            name=label("scoring", own),
+            out_shape=[half_f32, pltpu.VMEM((pairs * C, C), BF16), token],
+            in_specs=[VM] * 4,
+            out_specs=[VM] * 3,
             compiler_params=params(),
             cost_estimate=cost(4 * pairs * wide, 4 * tokens * cols),
-        )(k, v, queries, out_grad)
-
-    def attending(own, inside, carry, q, sv, g, sums):
-        ins = [doc_ids, inside, carry, q, sv, g, gain] + ([] if own else [sums])
+        )(after, k, v, queries)
+
+    def attending(own, inside, carry, sv, sums):
+        ins = [doc_ids, inside, carry, queries, sv, out_grad, gain] + ([] if own else [sums])
         last = [pltpu.VMEM((C, HD), F32)] if own else [pltpu.VMEM((2 * lanes, C), F32)]
         return pl.pallas_call(
             functools.partial(attend, own, blocks, heads, lanes),
+            name=label("attend", own),
             out_shape=[half_f32, pltpu.VMEM((pairs * HD, HD), BF16)] + last,
             in_specs=[SM] + [VM] * (len(ins) - 1),
             out_specs=[VM] * 3,
@@ -451,12 +490,13 @@
             cost_estimate=cost(2 * pairs * narrow, 1 << 20),
         )(*ins)
 
-    def mixing(own, before, attended, q, g):
-        ins = [doc_ids] + before + [attended, q, g, gain]
+    def mixing(own, before, attended):
+        ins = [doc_ids] + before + [attended, queries, out_grad, gain]
         outs = [half_bf, states_f32, message] + ([] if own else [column, column])
         scratch = [pltpu.VMEM((cols, HD), F32)]
         return pl.pallas_call(
             functools.partial(mixed, own, blocks, heads, lanes, tp),
+            name=label("mixed", own),
             out_shape=outs,
             in_specs=[SM] + [VM] * (len(ins) - 1),
             out_specs=[VM] * len(outs),
@@ -465,16 +505,17 @@
             cost_estimate=cost(2 * pairs * narrow, 1 << 20),
         )(*ins)
 
-    def query_grads(own, k, v, q, attended, scale, grad, low, scores, so_far):
-        ins = [k, v, q, attended, scale, gain, grad, low, scores] + list(so_far)
+    def query_grads(own, k, v, attended, scale, grad, low, scores, so_far, after):
+        ins = [after, k, v, queries, attended, scale, gain, grad, low, scores] + list(so_far)
         stage = pltpu.VMEM((2, C, cols), BF16)
         return pl.pallas_call(
             functools.partial(query_side, own, blocks, heads),
-            out_shape=[whole, whole, half_f32, half_f32],
-            in_specs=[VM] * 9 + [HB] * len(so_far),
-            out_specs=[HB, HB, VM, VM],
+            name=label("query_side", own),
+            out_shape=[whole, whole, half_f32, half_f32, token],
+            in_specs=[VM] * 10 + [HB] * len(so_far),
+            out_specs=[HB, HB, VM, VM, VM],
             scratch_shapes=[stage, stage, dma((2, 2))],
-            input_output_aliases={9: 0, 10: 1} if own else {},
+            input_output_aliases={10: 0, 11: 1} if own else {},
             compiler_params=params(),
             cost_estimate=cost(8 * pairs * wide, 4 * tokens * cols),
         )(*ins)
@@ -484,6 +525,7 @@
         stage = pltpu.VMEM((2, C, cols), BF16)
         return pl.pallas_call(
             functools.partial(key_side, own, blocks, heads),
+            name=label("key_side", own),
             out_shape=[whole, whole],
             in_specs=[SM] + [VM] * 6 + [HB] * len(so_far),
             out_specs=[HB, HB],
@@ -495,22 +537,28 @@
 
     k1, v1, inside1, theirs = states(False)
     k0, v0, inside0, mine = states(True)
-    carry0, carry1 = scan(theirs, mine, False)
-    q1, g1, local1, scores1 = scoring(False, k1, v1)
-    q0, g0, local0, scores0 = scoring(True, k0, v0)
-    att0, low0, sums = attending(True, inside0, carry0, q0, local0, g0, None)
-    att1, low1, sums = attending(False, inside1, carry1, q1, local1, g1, sums)
+    carry0, carry1, (local1, scores1), (local0, scores0) = scan(
+        theirs,
+        mine,
+        False,
+        lambda after: scoring(False, k1, v1, after),
+        lambda after, _: scoring(True, k0, v0, after),
+    )
+    att0, low0, sums = attending(True, inside0, carry0, local0, None)
+    att1, low1, sums = attending(False, inside1, carry1, local1, sums)
     parts = [sums] + [
         lax.ppermute(sums, "tp", [(i, (i + s) % tp) for i in range(tp)]) for s in range(1, tp)
     ]
-    grad1, after1, theirs, scale, slope = mixing(False, parts, att1, q1, g1)
-    grad0, after0, mine = mixing(True, [scale, slope], att0, q0, g0)
-    carry0, carry1 = scan(theirs, mine, True)
-    normed, query_grad, kl1, vl1 = query_grads(
-        False, k1, v1, q1, att1, scale, grad1, low1, scores1, ()
-    )
-    normed, query_grad, kl0, vl0 = query_grads(
-        True, k0, v0, q0, att0, scale, grad0, low0, scores0, (normed, query_grad)
+    grad1, after1, theirs, scale, slope = mixing(False, parts, att1)
+    grad0, after0, mine = mixing(True, [scale, slope], att0)
+    carry0, carry1, (_, _, kl1, vl1), (normed, query_grad, kl0, vl0) = scan(
+        theirs,
+        mine,
+        True,
+        lambda after: query_grads(False, k1, v1, att1, scale, grad1, low1, scores1, (), after),
+        lambda after, done: query_grads(
+            True, k0, v0, att0, scale, grad0, low0, scores0, done[:2], after
+        ),
     )
     key_grad, value_grad = key_grads(True, after0, carry0, k0, v0, kl0, vl0, ())
     key_grad, value_grad = key_grads(

time: 96.2 us -> 69.8 us (0.73)
  waiting for transfers between devices: 19.2 us -> 5.65 us
  Pallas kernels: 53.8 us -> 44.8 us
  local copies, waits for them, and re-layouts: 4.45 us -> 0.67 us
    ppermute x12, waiting for transfers between devices: 15.2 us -> 1.66 us  [swap(): return lax.ppermute(message, 'ctx', [(i, i ^ 1 << b) for i in range(size)])]
    pallas_call x12, Pallas kernels: 53.4 us -> 44.3 us  [the longest x2 11.9 us: query_grads(): pl.pallas_call(functools.partial(query_side, own, blocks, heads), name=la...]
    unnamed x14 -> x10, local copies, waits for them, and re-layouts: 4.45 us -> 0.67 us
  transfers between devices with their start and end apart: 15 -> 15, of which waited for: 10 -> 5; matrix products, arithmetic and copies ran while one was open for 0% -> 0% of each run, Pallas kernels for 42% -> 44%
where the time goes in v1:
time: 69.8 us; the launch traced here: 69.6 us
  Pallas kernels  44.8 us (64%)
  starting transfers between devices  17.7 us (25%)
  waiting for transfers between devices  5.65 us (8%)
  between operations  0.85 us (1%)
    ppermute x12, starting transfers between devices, swap(): return lax.ppermute(message, 'ctx', [(i, i ^ 1 << b) for i in range(size)])  13.9 us
    pallas_call x2, Pallas kernels, query_grads(): pl.pallas_call(functools.partial(query_side, own, blocks, heads), name=la...  11.9 us
    pallas_call x2, Pallas kernels, key_grads(): pl.pallas_call(functools.partial(key_side, own, blocks, heads), name=labe...  8.04 us
    pallas_call x2, Pallas kernels, mixing(): pl.pallas_call(functools.partial(mixed, own, blocks, heads, lanes, tp), n...  6.44 us
    pallas_call x2, Pallas kernels, states(): pl.pallas_call(functools.partial(key_value_states, own, blocks, heads), n...  6.29 us
    pallas_call x2, Pallas kernels, attending(): pl.pallas_call(functools.partial(attend, own, blocks, heads, lanes), name...  6.16 us
    pallas_call x2, Pallas kernels, scoring(): pl.pallas_call(functools.partial(local_scores, own, blocks, heads), name=...  5.49 us
    ppermute x3, waiting for transfers between devices, local(): lax.ppermute(sums, 'tp', [(i, (i + s) % tp) for i in range(tp)])  3.99 us
  transfers between devices with their start and end apart: 15, of which 5 were waited for; matrix products, arithmetic and copies ran while one was open for 0% of the time, Pallas kernels for 44%

profile of v1, /device:TPU:1, one launch (start us, length us, event | category | flops | bytes accessed | tf_op | source)
XLA Modules:
  0.0 69.6 jit_solution(10143328169091200651)
XLA Ops:
  0.6 0.0 copy-start.3
  0.6 0.6 copy-done.3
  1.3 3.0 %states_other.1 = (bf16[1536,512]{1,0:T(8,128)(2,1)S(1)}, bf16[1536,512]{1,0:T(8,128)(2,1)S(1)}, f32[3072,128]{1,0:T(8,128)S(1)}, f32[520,128]{1,0:T(8,128)S(1)}) custom-call(s32[6]{0:T(128)S(1)} %copy-done.3, bf16[1536,1024]{1,0:T(8,128)(2,1)} %k_hbm.3, bf16[1536,1024]{1,0:T(8,128)(2,1)} %v_hbm.3), custom_call_target="tpu_custom_call" | custom-call | flops 201326592 | bytes 3145728 | tf_op jit(solution)/shard_map/states_other/pallas_call | solution.py:456
  4.3 0.0 copy-start
  4.3 0.1 collective-permute-start
  4.4 3.3 %states_own.1 = (bf16[1536,512]{1,0:T(8,128)(2,1)S(1)}, bf16[1536,512]{1,0:T(8,128)(2,1)S(1)}, f32[3072,128]{1,0:T(8,128)S(1)}, f32[520,128]{1,0:T(8,128)S(1)}) custom-call(s32[6]{0:T(128)S(1)} %copy-done.3, bf16[1536,1024]{1,0:T(8,128)(2,1)} %k_hbm.3, bf16[1536,1024]{1,0:T(8,128)(2,1)} %v_hbm.3), custom_call_target="tpu_custom_call" | custom-call | flops 201326592 | bytes 3145728 | tf_op jit(solution)/shard_map/states_own/pallas_call | solution.py:456
  7.7 0.0 collective-permute-done.refs_1_.refs_4_
  7.8 2.5 %collective-permute-start.2 = (f32[264,128]{1,0:T(8,128)S(1)}, f32[264,128]{1,0:T(8,128)S(1)}, u32[]{:S(2)}, u32[]{:S(2)}) collective-permute-start(f32[264,128]{1,0:T(8,128)S(1)} %get-tuple-element.62.refs_2_), channel_id=1, source_target_pairs={{0,16},{4,20},{8,24},{12,28},{16,0},{20,4},{24,8},{28,12},{1,17},{... | collective-permute-start | bytes 405512 | tf_op jit(solution)/shard_map/ppermute | solution.py:356
  10.3 1.2 %collective-permute-start.1 = (f32[264,128]{1,0:T(8,128)S(1)}, f32[264,128]{1,0:T(8,128)S(1)}, u32[]{:S(2)}, u32[]{:S(2)}) collective-permute-start(f32[264,128]{1,0:T(8,128)S(1)} %get-tuple-element.61.after.refs_0_), channel_id=1, source_target_pairs={{0,8},{4,12},{8,0},{12,4},{16,24},{20,28},{24,16},{28,20},{1,9},{5... | collective-permute-start | bytes 405512 | tf_op jit(solution)/shard_map/ppermute | solution.py:356
  11.5 0.0 copy-done
  11.5 2.7 %scoring_other.1 = (f32[1536,512]{1,0:T(8,128)S(1)}, bf16[6144,256]{1,0:T(8,128)(2,1)S(1)}, f32[8,128]{1,0:T(8,128)S(1)}) custom-call(f32[264,128]{1,0:T(8,128)S(1)} %get-tuple-element.61.after.refs_0_, bf16[1536,512]{1,0:T(8,128)(2,1)S(1)} %get-tuple-element.63.k, bf16[1536,512]{1,0:T(8,128)(2,1)S(1)} %get-tuple-element.64.v, bf16[1536,1024]{1,0:T(8,128)(2,1)S(1)} %copy-done), custom_call_target="tpu_custom_call" | custom-call | flops 805306368 | bytes 3145728 | tf_op jit(solution)/shard_map/scoring_other/pallas_call | solution.py:468
  14.2 0.0 collective-permute-done.2.refs_3_.refs_2_
  14.3 0.6 collective-permute-done.1.refs_1_.refs_0_
  14.9 1.3 %collective-permute-start.4 = (f32[264,128]{1,0:T(8,128)S(1)}, f32[264,128]{1,0:T(8,128)S(1)}, u32[]{:S(2)}, u32[]{:S(2)}) collective-permute-start(f32[264,128]{1,0:T(8,128)S(1)} %get-tuple-element.67), channel_id=1, source_target_pairs={{0,8},{4,12},{8,0},{12,4},{16,24},{20,28},{24,16},{28,20},{1,9},{5... | collective-permute-start | bytes 405512 | tf_op jit(solution)/shard_map/ppermute | solution.py:356
  16.1 0.3 collective-permute-start.3
  16.5 0.0 copy-start.1
  16.5 0.0 copy-start.2
  16.5 0.0 copy-start.4
  16.5 2.7 %scoring_own.1 = (f32[1536,512]{1,0:T(8,128)S(1)}, bf16[6144,256]{1,0:T(8,128)(2,1)S(1)}, f32[8,128]{1,0:T(8,128)S(1)}) custom-call(f32[264,128]{1,0:T(8,128)S(1)} %get-tuple-element.66.after, bf16[1536,512]{1,0:T(8,128)(2,1)S(1)} %get-tuple-element.68.k, bf16[1536,512]{1,0:T(8,128)(2,1)S(1)} %get-tuple-element.69.v, bf16[1536,1024]{1,0:T(8,128)(2,1)S(1)} %copy-done), custom_call_target="tpu_custom_call" | custom-call | flops 805306368 | bytes 3145728 | tf_op jit(solution)/shard_map/scoring_own/pallas_call | solution.py:468
  19.2 0.0 collective-permute-done.4.refs_3_
  19.2 1.1 %collective-permute-done.3.refs_1_ = f32[264,128]{1,0:T(8,128)S(1)} collective-permute-done((f32[264,128]{1,0:T(8,128)S(1)}, f32[264,128]{1,0:T(8,128)S(1)}, u32[]{:S(2)}, u32[]{:S(2)}) %collective-permute-start.3) | collective-permute-done | bytes 135200 | tf_op jit(solution)/shard_map/ppermute | solution.py:356
  20.3 0.1 merge.8
  20.5 2.7 %collective-permute-start.5 = (f32[520,128]{1,0:T(8,128)S(1)}, f32[520,128]{1,0:T(8,128)S(1)}, u32[]{:S(2)}, u32[]{:S(2)}) collective-permute-start(f32[520,128]{1,0:T(8,128)S(1)} %get-tuple-element.71), channel_id=1, source_target_pairs={{0,4},{4,0},{8,12},{12,8},{16,20},{20,16},{24,28},{28,24},{1,5},{5... | collective-permute-start | bytes 798728 | tf_op jit(solution)/shard_map/ppermute | solution.py:356
  23.1 0.0 copy-done.1
  23.1 0.0 copy-done.2
  23.1 0.0 copy-done.4
  23.1 3.1 %attend_own.1 = (f32[1536,512]{1,0:T(8,128)S(1)}, bf16[3072,128]{1,0:T(8,128)(2,1)S(1)}, f32[256,128]{1,0:T(8,128)S(1)}) custom-call(s32[6]{0:T(128)S(1)} %copy-done.4, f32[3072,128]{1,0:T(8,128)S(1)} %get-tuple-element.73.inside, f32[520,128]{1,0:T(8,128)S(1)} %get-tuple-element.74.carry, ...), custom_call_target="tpu_custom_call", output_to_operand_aliasing={{0}: (4, {})} | custom-call | flops 201326592 | bytes 1048576 | tf_op jit(solution)/shard_map/attend_own/pallas_call | solution.py:481
  26.2 0.0 collective-permute-done.5.carry
  26.2 3.1 %attend_other.1 = (f32[1536,512]{1,0:T(8,128)S(1)}, bf16[3072,128]{1,0:T(8,128)(2,1)S(1)}, f32[16,256]{1,0:T(8,128)S(1)}) custom-call(s32[6]{0:T(128)S(1)} %copy-done.4, f32[3072,128]{1,0:T(8,128)S(1)} %get-tuple-element.58.inside, f32[520,128]{1,0:T(8,128)S(1)} %collective-permute-done.5.carry, ...), custom_call_target="tpu_custom_call", output_to_operand_aliasing={{0}: (4, {})} | custom-call | flops 201326592 | bytes 1048576 | tf_op jit(solution)/shard_map/attend_other/pallas_call | solution.py:481
  29.3 3.3 %collective-permute-start.8 = (f32[16,256]{1,0:T(8,128)S(1)}, f32[16,256]{1,0:T(8,128)S(1)}, u32[]{:S(2)}, u32[]{:S(2)}) collective-permute-start(f32[16,256]{1,0:T(8,128)S(1)} %get-tuple-element.77.rest_0_), channel_id=1, source_target_pairs={{0,3},{1,0},{2,1},{3,2},{4,7},{5,4},{6,5},{7,6},{8,11},{9,8},{10,9... | collective-permute-start | bytes 49160 | tf_op jit(solution)/shard_map/ppermute | solution.py:550
  32.7 0.0 collective-permute-start.7
  32.7 0.4 collective-permute-start.6
  33.1 0.4 collective-permute-done.8.rest_3_
  33.5 2.6 %collective-permute-done.7.rest_2_ = f32[16,256]{1,0:T(8,128)S(1)} collective-permute-done((f32[16,256]{1,0:T(8,128)S(1)}, f32[16,256]{1,0:T(8,128)S(1)}, u32[]{:S(2)}, u32[]{:S(2)}) %collective-permute-start.7) | collective-permute-done | bytes 16416 | tf_op jit(solution)/shard_map/ppermute | solution.py:550
  36.1 1.0 %collective-permute-done.6.rest_1_ = f32[16,256]{1,0:T(8,128)S(1)} collective-permute-done((f32[16,256]{1,0:T(8,128)S(1)}, f32[16,256]{1,0:T(8,128)S(1)}, u32[]{:S(2)}, u32[]{:S(2)}) %collective-permute-start.6) | collective-permute-done | bytes 16416 | tf_op jit(solution)/shard_map/ppermute | solution.py:550
  37.1 3.5 %mixed_other.1 = (bf16[1536,512]{1,0:T(8,128)(2,1)S(1)}, f32[3072,128]{1,0:T(8,128)S(1)}, f32[520,128]{1,0:T(8,128)S(1)}, f32[1536,128]{1,0:T(8,128)S(1)}, f32[1536,128]{1,0:T(8,128)S(1)}) custom-call(s32[6]{0:T(128)S(1)} %copy-done.4, f32[16,256]{1,0:T(8,128)S(1)} %get-tuple-element.77.rest_0_, f32[16,256]{1,0:T(8,128)S(1)} %collective-permute-done.6.rest_1_, ...), custom_call_target="tpu_custom_call" | custom-call | flops 201326592 | bytes 1048576 | tf_op jit(solution)/shard_map/mixed_other/pallas_call | solution.py:497
  40.6 1.5 %collective-permute-start.9 = (f32[520,128]{1,0:T(8,128)S(1)}, f32[520,128]{1,0:T(8,128)S(1)}, u32[]{:S(2)}, u32[]{:S(2)}) collective-permute-start(f32[520,128]{1,0:T(8,128)S(1)} %get-tuple-element.83), channel_id=1, source_target_pairs={{0,4},{4,0},{8,12},{12,8},{16,20},{20,16},{24,28},{28,24},{1,5},{5... | collective-permute-start | bytes 798728 | tf_op jit(solution)/shard_map/ppermute | solution.py:356
  42.1 3.0 %mixed_own.1 = (bf16[1536,512]{1,0:T(8,128)(2,1)S(1)}, f32[3072,128]{1,0:T(8,128)S(1)}, f32[520,128]{1,0:T(8,128)S(1)}) custom-call(s32[6]{0:T(128)S(1)} %copy-done.4, f32[1536,128]{1,0:T(8,128)S(1)} %get-tuple-element.79.rest_0_.scale, f32[1536,128]{1,0:T(8,128)S(1)} %get-tuple-element.80.rest_1_, f32[1536,512]{1,0:T(8,128)S(1)} %get-tuple-element.81.rest_2_.attended, ...), custom_call_target="tpu_custom_call" | custom-call | flops 201326592 | bytes 1048576 | tf_op jit(solution)/shard_map/mixed_own/pallas_call | solution.py:497
  45.0 0.0 collective-permute-done.9.refs_1_.refs_4_
  45.1 0.3 collective-permute-start.11
  45.4 0.3 collective-permute-start.10
  45.7 5.9 %query_side_other.1 = (bf16[1536,1024]{1,0:T(8,128)(2,1)}, bf16[1536,1024]{1,0:T(8,128)(2,1)}, f32[1536,512]{1,0:T(8,128)S(1)}, f32[1536,512]{1,0:T(8,128)S(1)}, f32[8,128]{1,0:T(8,128)S(1)}) custom-call(f32[264,128]{1,0:T(8,128)S(1)} %get-tuple-element.84.after.refs_0_, bf16[1536,512]{1,0:T(8,128)(2,1)S(1)} %get-tuple-element.63.k, ...), custom_call_target="tpu_custom_call" | custom-call | flops 1610612736 | bytes 3145728 | tf_op jit(solution)/shard_map/query_side_other/pallas_call | solution.py:511
  51.6 0.0 collective-permute-done.11.refs_3_.refs_2_
  51.6 0.0 collective-permute-done.10.refs_1_.refs_0_
  51.6 0.1 merge.10
  51.7 1.3 %collective-permute-start.13 = (f32[264,128]{1,0:T(8,128)S(1)}, f32[264,128]{1,0:T(8,128)S(1)}, u32[]{:S(2)}, u32[]{:S(2)}) collective-permute-start(f32[264,128]{1,0:T(8,128)S(1)} %get-tuple-element.99), channel_id=1, source_target_pairs={{0,8},{4,12},{8,0},{12,4},{16,24},{20,28},{24,16},{28,20},{1,9},{5... | collective-permute-start | bytes 405512 | tf_op jit(solution)/shard_map/ppermute | solution.py:356
  52.9 1.2 %collective-permute-start.12 = (f32[264,128]{1,0:T(8,128)S(1)}, f32[264,128]{1,0:T(8,128)S(1)}, u32[]{:S(2)}, u32[]{:S(2)}) collective-permute-start(f32[264,128]{1,0:T(8,128)S(1)} %get-tuple-element.90.after), channel_id=1, source_target_pairs={{0,16},{4,20},{8,24},{12,28},{16,0},{20,4},{24,8},{28,12},{1,17},{... | collective-permute-start | bytes 405512 | tf_op jit(solution)/shard_map/ppermute | solution.py:356
  54.2 6.0 %query_side_own.1 = (bf16[1536,1024]{1,0:T(8,128)(2,1)}, bf16[1536,1024]{1,0:T(8,128)(2,1)}, f32[1536,512]{1,0:T(8,128)S(1)}, f32[1536,512]{1,0:T(8,128)S(1)}, f32[8,128]{1,0:T(8,128)S(1)}) custom-call(f32[264,128]{1,0:T(8,128)S(1)} %get-tuple-element.90.after, ...), custom_call_target="tpu_custom_call", output_to_operand_aliasing={{0}: (10, {}), {1}: (11, {})} | custom-call | flops 1610612736 | bytes 3145728 | tf_op jit(solution)/shard_map/query_side_own/pallas_call | solution.py:511
  60.1 0.0 collective-permute-done.13.refs_3_
  60.1 0.0 collective-permute-done.12.refs_1_
  60.2 0.1 merge.11
  60.3 1.2 %collective-permute-start.14 = (f32[520,128]{1,0:T(8,128)S(1)}, f32[520,128]{1,0:T(8,128)S(1)}, u32[]{:S(2)}, u32[]{:S(2)}) collective-permute-start(f32[520,128]{1,0:T(8,128)S(1)} %get-tuple-element.101), channel_id=1, source_target_pairs={{0,4},{4,0},{8,12},{12,8},{16,20},{20,16},{24,28},{28,24},{1,5},{5... | collective-permute-start | bytes 798728 | tf_op jit(solution)/shard_map/ppermute | solution.py:356
  61.5 4.0 %key_side_own.1 = (bf16[1536,1024]{1,0:T(8,128)(2,1)}, bf16[1536,1024]{1,0:T(8,128)(2,1)}) custom-call(s32[6]{0:T(128)S(1)} %copy-done.4, f32[3072,128]{1,0:T(8,128)S(1)} %get-tuple-element.104.inside, f32[520,128]{1,0:T(8,128)S(1)} %get-tuple-element.105.carry, bf16[1536,512]{1,0:T(8,128)(2,1)S(1)} %get-tuple-element.68.k, ...), custom_call_target="tpu_custom_call" | custom-call | flops 402653184 | bytes 3145728 | tf_op jit(solution)/shard_map/key_side_own/pallas_call | solution.py:526
  65.5 0.0 collective-permute-done.14.carry
  65.6 4.0 %key_side_other.1 = (bf16[1536,1024]{1,0:T(8,128)(2,1)}, bf16[1536,1024]{1,0:T(8,128)(2,1)}) custom-call(s32[6]{0:T(128)S(1)} %copy-done.4, f32[3072,128]{1,0:T(8,128)S(1)} %get-tuple-element.98.inside, f32[520,128]{1,0:T(8,128)S(1)} %collective-permute-done.14.carry, ...), custom_call_target="tpu_custom_call", output_to_operand_aliasing={{0}: (7, {}), {1}: (8, {})} | custom-call | flops 402653184 | bytes 3145728 | tf_op jit(solution)/shard_map/key_side_other/pallas_call | solution.py:526
  (3 shorter events, 0.1 us)
Async XLA Ops:
  0.6 0.7 copy-start.3
  4.3 7.2 %copy-start = (bf16[1536,1024]{1,0:T(8,128)(2,1)S(1)}, bf16[1536,1024]{1,0:T(8,128)(2,1)}, u32[]{:S(2)}) copy-start(bf16[1536,1024]{1,0:T(8,128)(2,1)} %q.11) | copy-start | bytes 9437188
  4.3 3.4 %collective-permute-start = (f32[520,128]{1,0:T(8,128)S(1)}, f32[520,128]{1,0:T(8,128)S(1)}, u32[]{:S(2)}, u32[]{:S(2)}) collective-permute-start(f32[520,128]{1,0:T(8,128)S(1)} %get-tuple-element.60), channel_id=1, source_target_pairs={{0,4},{4,0},{8,12},{12,8},{16,20},{20,16},{24,28},{28,24},{1,5},{5... | collective-permute-start | bytes 798728 | tf_op jit(solution)/shard_map/ppermute | solution.py:356
  7.8 6.5 %collective-permute-start.2 = (f32[264,128]{1,0:T(8,128)S(1)}, f32[264,128]{1,0:T(8,128)S(1)}, u32[]{:S(2)}, u32[]{:S(2)}) collective-permute-start(f32[264,128]{1,0:T(8,128)S(1)} %get-tuple-element.62.refs_2_), channel_id=1, source_target_pairs={{0,16},{4,20},{8,24},{12,28},{16,0},{20,4},{24,8},{28,12},{1,17},{... | collective-permute-start | bytes 405512 | tf_op jit(solution)/shard_map/ppermute | solution.py:356
  10.3 4.5 %collective-permute-start.1 = (f32[264,128]{1,0:T(8,128)S(1)}, f32[264,128]{1,0:T(8,128)S(1)}, u32[]{:S(2)}, u32[]{:S(2)}) collective-permute-start(f32[264,128]{1,0:T(8,128)S(1)} %get-tuple-element.61.after.refs_0_), channel_id=1, source_target_pairs={{0,8},{4,12},{8,0},{12,4},{16,24},{20,28},{24,16},{28,20},{1,9},{5... | collective-permute-start | bytes 405512 | tf_op jit(solution)/shard_map/ppermute | solution.py:356
  14.9 4.4 %collective-permute-start.4 = (f32[264,128]{1,0:T(8,128)S(1)}, f32[264,128]{1,0:T(8,128)S(1)}, u32[]{:S(2)}, u32[]{:S(2)}) collective-permute-start(f32[264,128]{1,0:T(8,128)S(1)} %get-tuple-element.67), channel_id=1, source_target_pairs={{0,8},{4,12},{8,0},{12,4},{16,24},{20,28},{24,16},{28,20},{1,9},{5... | collective-permute-start | bytes 405512 | tf_op jit(solution)/shard_map/ppermute | solution.py:356
  16.1 4.2 %collective-permute-start.3 = (f32[264,128]{1,0:T(8,128)S(1)}, f32[264,128]{1,0:T(8,128)S(1)}, u32[]{:S(2)}, u32[]{:S(2)}) collective-permute-start(f32[264,128]{1,0:T(8,128)S(1)} %get-tuple-element.66.after), channel_id=1, source_target_pairs={{0,16},{4,20},{8,24},{12,28},{16,0},{20,4},{24,8},{28,12},{1,17},{... | collective-permute-start | bytes 405512 | tf_op jit(solution)/shard_map/ppermute | solution.py:356
  16.5 6.6 %copy-start.1 = (bf16[1536,1024]{1,0:T(8,128)(2,1)S(1)}, bf16[1536,1024]{1,0:T(8,128)(2,1)}, u32[]{:S(2)}) copy-start(bf16[1536,1024]{1,0:T(8,128)(2,1)} %rest_4_.1) | copy-start | bytes 9437188
  16.5 6.6 %copy-start.2 = (f32[1024]{0:T(1024)S(1)}, f32[1024]{0:T(1024)}, u32[]{:S(2)}) copy-start(f32[1024]{0:T(1024)} %param.10) | copy-start | bytes 12292
  16.5 6.6 %copy-start.4 = (s32[6]{0:T(128)S(1)}, s32[6]{0:T(128)}, u32[]{:S(2)}) copy-start(s32[6]{0:T(128)} %docs.15) | copy-start | bytes 76
  20.5 5.7 %collective-permute-start.5 = (f32[520,128]{1,0:T(8,128)S(1)}, f32[520,128]{1,0:T(8,128)S(1)}, u32[]{:S(2)}, u32[]{:S(2)}) collective-permute-start(f32[520,128]{1,0:T(8,128)S(1)} %get-tuple-element.71), channel_id=1, source_target_pairs={{0,4},{4,0},{8,12},{12,8},{16,20},{20,16},{24,28},{28,24},{1,5},{5... | collective-permute-start | bytes 798728 | tf_op jit(solution)/shard_map/ppermute | solution.py:356
  29.3 4.2 %collective-permute-start.8 = (f32[16,256]{1,0:T(8,128)S(1)}, f32[16,256]{1,0:T(8,128)S(1)}, u32[]{:S(2)}, u32[]{:S(2)}) collective-permute-start(f32[16,256]{1,0:T(8,128)S(1)} %get-tuple-element.77.rest_0_), channel_id=1, source_target_pairs={{0,3},{1,0},{2,1},{3,2},{4,7},{5,4},{6,5},{7,6},{8,11},{9,8},{10,9... | collective-permute-start | bytes 49160 | tf_op jit(solution)/shard_map/ppermute | solution.py:550
  32.7 3.5 %collective-permute-start.7 = (f32[16,256]{1,0:T(8,128)S(1)}, f32[16,256]{1,0:T(8,128)S(1)}, u32[]{:S(2)}, u32[]{:S(2)}) collective-permute-start(f32[16,256]{1,0:T(8,128)S(1)} %get-tuple-element.77.rest_0_), channel_id=1, source_target_pairs={{0,2},{1,3},{2,0},{3,1},{4,6},{5,7},{6,4},{7,5},{8,10},{9,11},{10,... | collective-permute-start | bytes 49160 | tf_op jit(solution)/shard_map/ppermute | solution.py:550
  32.7 4.4 %collective-permute-start.6 = (f32[16,256]{1,0:T(8,128)S(1)}, f32[16,256]{1,0:T(8,128)S(1)}, u32[]{:S(2)}, u32[]{:S(2)}) collective-permute-start(f32[16,256]{1,0:T(8,128)S(1)} %get-tuple-element.77.rest_0_), channel_id=1, source_target_pairs={{0,1},{1,2},{2,3},{3,0},{4,5},{5,6},{6,7},{7,4},{8,9},{9,10},{10,1... | collective-permute-start | bytes 49160 | tf_op jit(solution)/shard_map/ppermute | solution.py:550
  40.6 4.5 %collective-permute-start.9 = (f32[520,128]{1,0:T(8,128)S(1)}, f32[520,128]{1,0:T(8,128)S(1)}, u32[]{:S(2)}, u32[]{:S(2)}) collective-permute-start(f32[520,128]{1,0:T(8,128)S(1)} %get-tuple-element.83), channel_id=1, source_target_pairs={{0,4},{4,0},{8,12},{12,8},{16,20},{20,16},{24,28},{28,24},{1,5},{5... | collective-permute-start | bytes 798728 | tf_op jit(solution)/shard_map/ppermute | solution.py:356
  45.1 6.5 %collective-permute-start.11 = (f32[264,128]{1,0:T(8,128)S(1)}, f32[264,128]{1,0:T(8,128)S(1)}, u32[]{:S(2)}, u32[]{:S(2)}) collective-permute-start(f32[264,128]{1,0:T(8,128)S(1)} %get-tuple-element.85.refs_2_), channel_id=1, source_target_pairs={{0,16},{4,20},{8,24},{12,28},{16,0},{20,4},{24,8},{28,12},{1,17},{... | collective-permute-start | bytes 405512 | tf_op jit(solution)/shard_map/ppermute | solution.py:356
  45.4 6.2 %collective-permute-start.10 = (f32[264,128]{1,0:T(8,128)S(1)}, f32[264,128]{1,0:T(8,128)S(1)}, u32[]{:S(2)}, u32[]{:S(2)}) collective-permute-start(f32[264,128]{1,0:T(8,128)S(1)} %get-tuple-element.84.after.refs_0_), channel_id=1, source_target_pairs={{0,8},{4,12},{8,0},{12,4},{16,24},{20,28},{24,16},{28,20},{1,9},{5... | collective-permute-start | bytes 405512 | tf_op jit(solution)/shard_map/ppermute | solution.py:356
  51.7 8.5 %collective-permute-start.13 = (f32[264,128]{1,0:T(8,128)S(1)}, f32[264,128]{1,0:T(8,128)S(1)}, u32[]{:S(2)}, u32[]{:S(2)}) collective-permute-start(f32[264,128]{1,0:T(8,128)S(1)} %get-tuple-element.99), channel_id=1, source_target_pairs={{0,8},{4,12},{8,0},{12,4},{16,24},{20,28},{24,16},{28,20},{1,9},{5... | collective-permute-start | bytes 405512 | tf_op jit(solution)/shard_map/ppermute | solution.py:356
  52.9 7.2 %collective-permute-start.12 = (f32[264,128]{1,0:T(8,128)S(1)}, f32[264,128]{1,0:T(8,128)S(1)}, u32[]{:S(2)}, u32[]{:S(2)}) collective-permute-start(f32[264,128]{1,0:T(8,128)S(1)} %get-tuple-element.90.after), channel_id=1, source_target_pairs={{0,16},{4,20},{8,24},{12,28},{16,0},{20,4},{24,8},{28,12},{1,17},{... | collective-permute-start | bytes 405512 | tf_op jit(solution)/shard_map/ppermute | solution.py:356
  60.3 5.2 %collective-permute-start.14 = (f32[520,128]{1,0:T(8,128)S(1)}, f32[520,128]{1,0:T(8,128)S(1)}, u32[]{:S(2)}, u32[]{:S(2)}) collective-permute-start(f32[520,128]{1,0:T(8,128)S(1)} %get-tuple-element.101), channel_id=1, source_target_pairs={{0,4},{4,0},{8,12},{12,8},{16,20},{20,16},{24,28},{28,24},{1,5},{5... | collective-permute-start | bytes 798728 | tf_op jit(solution)/shard_map/ppermute | solution.py:356

commit v2 on v1

--- a/solution.py
+++ b/solution.py
@@ -13,15 +13,19 @@
 PAD = 8
 NEVER = -1.0e9
 MIB = 1 << 20
-UNROLL = 1
+U_SCORE = 6
+U_ATT = 6
+U_MIX = 6
+U_Q = 6
+U_K = 6
+T_ATT = 128
+T_MIX = 128
 
 epsilon = 1e-06
 
 F32 = jnp.float32
 BF16 = jnp.bfloat16
 VM = pl.BlockSpec(memory_space=pltpu.VMEM)
-SM = pl.BlockSpec(memory_space=pltpu.SMEM)
-ANY = pl.BlockSpec(memory_space=pl.ANY)
 HB = pl.BlockSpec(memory_space=pltpu.HBM)
 
 
@@ -64,21 +68,30 @@
     return pl.ds(pl.multiple_of((n * heads + h) * HD, HD), HD)
 
 
-def key_value_states(own, blocks, heads, docs, k_hbm, v_hbm, k, v, inside, message, sems):
+def key_value_states(own, blocks, heads, docs_hbm, k_hbm, v_hbm, *rest):
+    if own:
+        k, v, inside, message, docs, sems = rest
+    else:
+        k, v, inside, message, table, docs, sems = rest
     off = half_start(own, heads * HD)
+    docs_copy = pltpu.make_async_copy(docs_hbm, docs, sems.at[2 * heads])
+    width = 2 * HD if heads % 2 == 0 else HD
     copies = []
-    for h in range(heads):
-        src = pl.ds(off + h * HD, HD)
+    for i in range(heads * HD // width):
+        src, dst = pl.ds(off + i * width, width), pl.ds(i * width, width)
         pair = (
-            pltpu.make_async_copy(k_hbm.at[:, src], k.at[:, head(h)], sems.at[2 * h]),
-            pltpu.make_async_copy(v_hbm.at[:, src], v.at[:, head(h)], sems.at[2 * h + 1]),
+            pltpu.make_async_copy(k_hbm.at[:, src], k.at[:, dst], sems.at[2 * i]),
+            pltpu.make_async_copy(v_hbm.at[:, src], v.at[:, dst], sems.at[2 * i + 1]),
         )
         for copy in pair:
             copy.start()
         copies.append(pair)
+    docs_copy.start()
+    docs_copy.wait()
     for h in range(heads):
-        for copy in copies[h]:
-            copy.wait()
+        if h * HD % width == 0:
+            for copy in copies[h * HD // width]:
+                copy.wait()
         per_block = [pl.ds(n * C, C) for n in range(blocks)]
         sums = [dot(k[rows, head(h)], v[rows, head(h)], TN) for rows in per_block]
         running = jnp.zeros((HD, HD), F32)
@@ -90,6 +103,10 @@
             else:
                 message[head(h), :] = total
     message[heads * HD :, :] = jnp.full((PAD, HD), docs[blocks - 1].astype(F32), F32)
+    if not own:
+        table[...] = jnp.zeros(table.shape, F32)
+        for n in range(blocks):
+            table[n : n + 1, :] = jnp.full((1, HD), docs[n].astype(F32), F32)
 
 
 def causal_mask():
@@ -100,14 +117,25 @@
     return pl.ds(pl.multiple_of((n * heads + h) * C, C), C)
 
 
-def local_scores(own, blocks, heads, after, k, v, q, local, scores, done):
-    off = half_start(own, heads * HD)
+def local_scores(
+    own, blocks, heads, after, k, v, q_hbm, g_hbm, q, g, local, scores, done, q_sems, g_sem
+):
+    cols = pl.ds(half_start(own, heads * HD), heads * HD)
+
+    def q_copy(n):
+        return pltpu.make_async_copy(q_hbm.at[block(n), cols], q.at[block(n), :], q_sems.at[n])
+
+    for n in range(blocks):
+        q_copy(n).start()
+    g_copy = pltpu.make_async_copy(g_hbm.at[:, cols], g, g_sem)
+    g_copy.start()
     causal = causal_mask()
     every = range(heads)
 
     def step(n, carry):
+        q_copy(n).wait()
         rows = block(n)
-        raw = [dot(q[rows, pl.ds(off + h * HD, HD)], k[rows, head(h)], NT) for h in every]
+        raw = [dot(q[rows, head(h)], k[rows, head(h)], NT) for h in every]
         low = [jnp.where(causal, s, 0.0).astype(BF16) for s in raw]
         outs = [dot(low[h], v[rows, head(h)], NN) for h in every]
         for h in every:
@@ -115,7 +143,8 @@
             local[rows, head(h)] = outs[h]
         return carry
 
-    lax.fori_loop(0, blocks, step, 0, unroll=UNROLL)
+    lax.fori_loop(0, blocks, step, 0, unroll=U_SCORE)
+    g_copy.wait()
     done[...] = jnp.zeros(done.shape, F32)
 
 
@@ -128,38 +157,34 @@
         sums[...] = sums_in[...]
     off = half_start(own, heads * HD)
     gains = gain[:, pl.ds(off, heads * HD)]
-    lane = lax.broadcasted_iota(jnp.int32, (C, HD), 1)
+    lane = lax.broadcasted_iota(jnp.int32, (T_ATT, HD), 1)
     every = range(heads)
 
     def step(n, carried):
-        rows = block(n)
-        hit = carry[heads * HD : heads * HD + 1, :] == docs[n].astype(F32)
+        hit = carry[heads * HD : heads * HD + 1, :] == docs[pl.ds(n, 1), :]
         states = []
         for h in every:
             state = inside[state_rows(n, h, heads), :] + jnp.where(hit, carry[head(h), :], 0.0)
             states.append(state.astype(BF16))
-        outs = [dot(q[rows, pl.ds(off + h * HD, HD)], states[h], NN) for h in every]
-        outs = [outs[h] + local[rows, head(h)] for h in every]
-        square = functools.reduce(jnp.add, [out * out for out in outs])
-        inner = functools.reduce(
-            jnp.add,
-            [
-                g[rows, pl.ds(off + h * HD, HD)].astype(F32)
-                * gains[:, h * HD : (h + 1) * HD]
-                * outs[h]
-                for h in every
-            ],
-        )
-        square = jnp.sum(square, axis=1, keepdims=True)
-        inner = jnp.sum(inner, axis=1, keepdims=True)
-        placed = jnp.where(lane == n, square, 0.0) + jnp.where(lane == n + lanes, inner, 0.0)
-        for h in every:
             low[state_rows(n, h, heads), :] = states[h]
-            attended[rows, head(h)] = outs[h]
-        sums[...] += placed
+        for t in range(0, C, T_ATT):
+            rows = pl.ds(pl.multiple_of(n * C + t, T_ATT), T_ATT)
+            square = jnp.zeros((T_ATT, HD), F32)
+            inner = jnp.zeros((T_ATT, HD), F32)
+            for h in every:
+                out = local[rows, head(h)] + dot(q[rows, head(h)], states[h], NN)
+                attended[rows, head(h)] = out
+                square += out * out
+                weighted = g[rows, head(h)].astype(F32) * gains[:, h * HD : (h + 1) * HD]
+                inner += weighted * out
+            square = jnp.sum(square, axis=1, keepdims=True)
+            inner = jnp.sum(inner, axis=1, keepdims=True)
+            sums[t : t + T_ATT, :] += jnp.where(lane == n, square, 0.0) + jnp.where(
+                lane == n + lanes, inner, 0.0
+            )
         return carried
 
-    lax.fori_loop(0, blocks, step, 0, unroll=UNROLL)
+    lax.fori_loop(0, blocks, step, 0, unroll=U_ATT)
     if not own:
         message[...] = jnp.transpose(sums[...])[: 2 * lanes, :]
 
@@ -191,30 +216,29 @@
     def step(i, carried):
         n = blocks - 1 - i
         rows = block(n)
-        linked = docs[n] == docs[jnp.maximum(n - 1, 0)]
-        r = scale[rows, :]
-        s = slope[rows, :]
-        ds = []
-        for h in every:
-            weighted = g[rows, pl.ds(off + h * HD, HD)].astype(F32)
-            weighted = weighted * gains[:, h * HD : (h + 1) * HD]
-            ds.append((r * weighted - attended[rows, head(h)] * s).astype(BF16))
-        sums = [dot(q[rows, pl.ds(off + h * HD, HD)], ds[h], TN) for h in every]
+        linked = docs[pl.ds(n, 1), :] == docs[pl.ds(jnp.maximum(n - 1, 0), 1), :]
+        for t in range(0, C, T_MIX):
+            part = pl.ds(pl.multiple_of(n * C + t, T_MIX), T_MIX)
+            r = scale[part, :]
+            s = slope[part, :]
+            for h in every:
+                weighted = g[part, head(h)].astype(F32) * gains[:, h * HD : (h + 1) * HD]
+                d = r * weighted - attended[part, head(h)] * s
+                grad[part, head(h)] = d.astype(BF16)
+        sums = [dot(q[rows, head(h)], grad[rows, head(h)], TN) for h in every]
         befores = [running[head(h), :] for h in every]
         for h in every:
-            grad[rows, head(h)] = ds[h]
             inside[state_rows(n, h, heads), :] = befores[h]
             total = befores[h] + sums[h]
             message[head(h), :] = total
             running[head(h), :] = jnp.where(linked, total, 0.0)
         return carried
 
-    lax.fori_loop(0, blocks, step, 0, unroll=UNROLL)
-    message[heads * HD :, :] = jnp.full((PAD, HD), -docs[0].astype(F32), F32)
-
-
-def store_blocks(n, pairs, cols, sems):
-    slot = lax.rem(n, 2)
+    lax.fori_loop(0, blocks, step, 0, unroll=U_MIX)
+    message[heads * HD :, :] = jnp.broadcast_to(-docs[0:1, :], (PAD, HD))
+
+
+def store_blocks(n, slot, pairs, cols, sems):
     return [
         pltpu.make_async_copy(stage.at[slot], out.at[block(n), cols], sems.at[i, slot])
         for i, (stage, out) in enumerate(pairs)
@@ -233,13 +257,6 @@
 
     def step(n, carried):
         rows = block(n)
-        slot = lax.rem(n, 2)
-
-        @pl.when(n >= 2)
-        def _():
-            for copy in store_blocks(n - 2, pairs, cols, sems):
-                copy.wait()
-
         r = scale[rows, :]
         ds = [grad[rows, head(h)] for h in every]
         raw = [dot(ds[h], v[rows, head(h)], NT) for h in every]
@@ -248,23 +265,23 @@
             dot(ds[h], low[state_rows(n, h, heads), :], NT) + dot(gs[h], k[rows, head(h)], NN)
             for h in every
         ]
-        kg = [dot(gs[h], q[rows, pl.ds(off + h * HD, HD)], TN) for h in every]
+        kg = [dot(gs[h], q[rows, head(h)], TN) for h in every]
         vg = [dot(scores[score_rows(n, h, heads), :], ds[h], TN) for h in every]
         outs = [
             attended[rows, head(h)] * r * gains[:, h * HD : (h + 1) * HD] for h in every
         ]
         for h in every:
-            stage_q[slot, :, head(h)] = qg[h].astype(BF16)
-            stage_n[slot, :, head(h)] = outs[h].astype(BF16)
+            stage_q[n, :, head(h)] = qg[h].astype(BF16)
+            stage_n[n, :, head(h)] = outs[h].astype(BF16)
             key_local[rows, head(h)] = kg[h]
             value_local[rows, head(h)] = vg[h]
-        for copy in store_blocks(n, pairs, cols, sems):
+        for copy in store_blocks(n, n, pairs, cols, sems):
             copy.start()
         return carried
 
-    lax.fori_loop(0, blocks, step, 0)
-    for n in range(max(blocks - 2, 0), blocks):
-        for copy in store_blocks(n, pairs, cols, sems):
+    lax.fori_loop(0, blocks, step, 0, unroll=U_Q)
+    for n in range(blocks):
+        for copy in store_blocks(n, n, pairs, cols, sems):
             copy.wait()
     done[...] = jnp.zeros(done.shape, F32)
 
@@ -279,14 +296,7 @@
 
     def step(n, carried):
         rows = block(n)
-        slot = lax.rem(n, 2)
-
-        @pl.when(n >= 2)
-        def _():
-            for copy in store_blocks(n - 2, pairs, cols, sems):
-                copy.wait()
-
-        hit = carry[heads * HD : heads * HD + 1, :] == -docs[n].astype(F32)
+        hit = carry[heads * HD : heads * HD + 1, :] == -docs[pl.ds(n, 1), :]
         states = []
         for h in every:
             state = inside[state_rows(n, h, heads), :] + jnp.where(hit, carry[head(h), :], 0.0)
@@ -296,15 +306,15 @@
         kg = [(kg[h] + key_local[rows, head(h)]).astype(BF16) for h in every]
         vg = [(vg[h] + value_local[rows, head(h)]).astype(BF16) for h in every]
         for h in every:
-            stage_k[slot, :, head(h)] = kg[h]
-            stage_v[slot, :, head(h)] = vg[h]
-        for copy in store_blocks(n, pairs, cols, sems):
+            stage_k[n, :, head(h)] = kg[h]
+            stage_v[n, :, head(h)] = vg[h]
+        for copy in store_blocks(n, n, pairs, cols, sems):
             copy.start()
         return carried
 
-    lax.fori_loop(0, blocks, step, 0)
-    for n in range(max(blocks - 2, 0), blocks):
-        for copy in store_blocks(n, pairs, cols, sems):
+    lax.fori_loop(0, blocks, step, 0, unroll=U_K)
+    for n in range(blocks):
+        for copy in store_blocks(n, n, pairs, cols, sems):
             copy.wait()
 
 
@@ -446,118 +456,120 @@
     whole = pltpu.HBM((tokens, features), BF16)
     column = pltpu.VMEM((tokens, HD), F32)
 
-    keys, values = [pltpu.with_memory_space_constraint(x, pltpu.HBM) for x in (keys, values)]
-    queries, out_grad = [
-        pltpu.with_memory_space_constraint(x, pltpu.VMEM) for x in (queries, out_grad)
+    keys, values, queries, out_grad, docs_hbm = [
+        pltpu.with_memory_space_constraint(x, pltpu.HBM)
+        for x in (keys, values, queries, out_grad, doc_ids)
     ]
     token = pltpu.VMEM((PAD, HD), F32)
 
     def states(own):
+        outs = [half_bf, half_bf, states_f32, message]
+        outs += [] if own else [pltpu.VMEM((lanes, HD), F32)]
         return pl.pallas_call(
             functools.partial(key_value_states, own, blocks, heads),
             name=label("states", own),
-            out_shape=[half_bf, half_bf, states_f32, message],
-            in_specs=[SM, HB, HB],
-            out_specs=[VM] * 4,
-            scratch_shapes=[dma((2 * heads,))],
+            out_shape=outs,
+            in_specs=[HB, HB, HB],
+            out_specs=[VM] * len(outs),
+            scratch_shapes=[pltpu.SMEM((blocks,), jnp.int32), dma((2 * heads + 1,))],
             compiler_params=params(),
             cost_estimate=cost(2 * pairs * narrow, 4 * tokens * cols),
-        )(doc_ids, keys, values)
+        )(docs_hbm, keys, values)
 
     def scoring(own, k, v, after):
         return pl.pallas_call(
             functools.partial(local_scores, own, blocks, heads),
             name=label("scoring", own),
-            out_shape=[half_f32, pltpu.VMEM((pairs * C, C), BF16), token],
-            in_specs=[VM] * 4,
-            out_specs=[VM] * 3,
+            out_shape=[half_bf, half_bf, half_f32, pltpu.VMEM((pairs * C, C), BF16), token],
+            in_specs=[VM] * 3 + [HB] * 2,
+            out_specs=[VM] * 5,
+            scratch_shapes=[dma((blocks,)), dma],
             compiler_params=params(),
             cost_estimate=cost(4 * pairs * wide, 4 * tokens * cols),
-        )(after, k, v, queries)
-
-    def attending(own, inside, carry, sv, sums):
-        ins = [doc_ids, inside, carry, queries, sv, out_grad, gain] + ([] if own else [sums])
+        )(after, k, v, queries, out_grad)
+
+    def attending(own, inside, carry, q, sv, g, sums):
+        ins = [docs, inside, carry, q, sv, g, gain] + ([] if own else [sums])
         last = [pltpu.VMEM((C, HD), F32)] if own else [pltpu.VMEM((2 * lanes, C), F32)]
         return pl.pallas_call(
             functools.partial(attend, own, blocks, heads, lanes),
             name=label("attend", own),
             out_shape=[half_f32, pltpu.VMEM((pairs * HD, HD), BF16)] + last,
-            in_specs=[SM] + [VM] * (len(ins) - 1),
+            in_specs=[VM] * len(ins),
             out_specs=[VM] * 3,
             scratch_shapes=[] if own else [pltpu.VMEM((C, HD), F32)],
-            input_output_aliases={4: 0},
             compiler_params=params(),
             cost_estimate=cost(2 * pairs * narrow, 1 << 20),
         )(*ins)
 
-    def mixing(own, before, attended):
-        ins = [doc_ids] + before + [attended, queries, out_grad, gain]
+    def mixing(own, before, attended, q, g):
+        ins = [docs] + before + [attended, q, g, gain]
         outs = [half_bf, states_f32, message] + ([] if own else [column, column])
         scratch = [pltpu.VMEM((cols, HD), F32)]
         return pl.pallas_call(
             functools.partial(mixed, own, blocks, heads, lanes, tp),
             name=label("mixed", own),
             out_shape=outs,
-            in_specs=[SM] + [VM] * (len(ins) - 1),
+            in_specs=[VM] * len(ins),
             out_specs=[VM] * len(outs),
             scratch_shapes=scratch if own else scratch + [pltpu.VMEM((HD, C), F32)],
             compiler_params=params(),
             cost_estimate=cost(2 * pairs * narrow, 1 << 20),
         )(*ins)
 
-    def query_grads(own, k, v, attended, scale, grad, low, scores, so_far, after):
-        ins = [after, k, v, queries, attended, scale, gain, grad, low, scores] + list(so_far)
-        stage = pltpu.VMEM((2, C, cols), BF16)
+    def query_grads(own, k, v, q, attended, scale, grad, low, scores, so_far, after):
+        ins = [after, k, v, q, attended, scale, gain, grad, low, scores] + list(so_far)
+        stage = pltpu.VMEM((blocks, C, cols), BF16)
         return pl.pallas_call(
             functools.partial(query_side, own, blocks, heads),
             name=label("query_side", own),
             out_shape=[whole, whole, half_f32, half_f32, token],
             in_specs=[VM] * 10 + [HB] * len(so_far),
             out_specs=[HB, HB, VM, VM, VM],
-            scratch_shapes=[stage, stage, dma((2, 2))],
+            scratch_shapes=[stage, stage, dma((2, blocks))],
             input_output_aliases={10: 0, 11: 1} if own else {},
             compiler_params=params(),
             cost_estimate=cost(8 * pairs * wide, 4 * tokens * cols),
         )(*ins)
 
     def key_grads(own, inside, carry, k, v, key_local, value_local, so_far):
-        ins = [doc_ids, inside, carry, k, v, key_local, value_local] + list(so_far)
-        stage = pltpu.VMEM((2, C, cols), BF16)
+        ins = [docs, inside, carry, k, v, key_local, value_local] + list(so_far)
+        stage = pltpu.VMEM((blocks, C, cols), BF16)
         return pl.pallas_call(
             functools.partial(key_side, own, blocks, heads),
             name=label("key_side", own),
             out_shape=[whole, whole],
-            in_specs=[SM] + [VM] * 6 + [HB] * len(so_far),
+            in_specs=[VM] * 7 + [HB] * len(so_far),
             out_specs=[HB, HB],
-            scratch_shapes=[stage, stage, dma((2, 2))],
+            scratch_shapes=[stage, stage, dma((2, blocks))],
             input_output_aliases={} if own else {7: 0, 8: 1},
             compiler_params=params(),
             cost_estimate=cost(4 * pairs * narrow, 4 * tokens * cols),
         )(*ins)
 
-    k1, v1, inside1, theirs = states(False)
+    k1, v1, inside1, theirs, docs = states(False)
     k0, v0, inside0, mine = states(True)
-    carry0, carry1, (local1, scores1), (local0, scores0) = scan(
+    carry0, carry1, (q1, g1, local1, scores1), (q0, g0, local0, scores0) = scan(
         theirs,
         mine,
         False,
         lambda after: scoring(False, k1, v1, after),
         lambda after, _: scoring(True, k0, v0, after),
     )
-    att0, low0, sums = attending(True, inside0, carry0, local0, None)
-    att1, low1, sums = attending(False, inside1, carry1, local1, sums)
+    att0, low0, sums = attending(True, inside0, carry0, q0, local0, g0, None)
+    att1, low1, sums = attending(False, inside1, carry1, q1, local1, g1, sums)
     parts = [sums] + [
         lax.ppermute(sums, "tp", [(i, (i + s) % tp) for i in range(tp)]) for s in range(1, tp)
     ]
-    grad1, after1, theirs, scale, slope = mixing(False, parts, att1)
-    grad0, after0, mine = mixing(True, [scale, slope], att0)
+    grad1, after1, theirs, scale, slope = mixing(False, parts, att1, q1, g1)
+    grad0, after0, mine = mixing(True, [scale, slope], att0, q0, g0)
     carry0, carry1, (_, _, kl1, vl1), (normed, query_grad, kl0, vl0) = scan(
         theirs,
         mine,
         True,
-        lambda after: query_grads(False, k1, v1, att1, scale, grad1, low1, scores1, (), after),
+        lambda after: query_grads(False, k1, v1, q1, att1, scale, grad1, low1, scores1, (), after),
         lambda after, done: query_grads(
-            True, k0, v0, att0, scale, grad0, low0, scores0, done[:2], after
+            True, k0, v0, q0, att0, scale, grad0, low0, scores0, done[:2], after
         ),
     )
     key_grad, value_grad = key_grads(True, after0, carry0, k0, v0, kl0, vl0, ())

time: 69.8 us -> 56.2 us (0.81)
  Pallas kernels: 44.8 us -> 33.1 us
  waiting for transfers between devices: 5.65 us -> 4.23 us
    pallas_call x2, Pallas kernels: 8.04 us -> 4.08 us  [key_grads(): pl.pallas_call(functools.partial(key_side, own, blocks, heads), name=labe...]
    pallas_call x2, Pallas kernels: 6.44 us -> 3.04 us  [mixing(): pl.pallas_call(functools.partial(mixed, own, blocks, heads, lanes, tp), n...]
    pallas_call x2, Pallas kernels: 6.16 us -> 2.87 us  [attending(): pl.pallas_call(functools.partial(attend, own, blocks, heads, lanes), name...]
    pallas_call x2, Pallas kernels: 5.49 us -> 7.3 us  [scoring(): pl.pallas_call(functools.partial(local_scores, own, blocks, heads), name=...]
    pallas_call x2, Pallas kernels: 11.9 us -> 10.4 us  [query_grads(): pl.pallas_call(functools.partial(query_side, own, blocks, heads), name=la...]
    ppermute x12, waiting for transfers between devices: 1.66 us -> 0.2 us  [swap(): return lax.ppermute(message, 'ctx', [(i, i ^ 1 << b) for i in range(size)])]
    pallas_call x2, Pallas kernels: 6.29 us -> 4.98 us  [states(): pl.pallas_call(functools.partial(key_value_states, own, blocks, heads), n...]
  transfers between devices with their start and end apart: 15 -> 15, of which waited for: 5 -> 4; matrix products, arithmetic and copies ran while one was open for 0% -> 0% of each run, Pallas kernels for 44% -> 45%
where the time goes in v2:
time: 56.2 us; the launch traced here: 56 us
  Pallas kernels  33.1 us (59%)
  starting transfers between devices  17.6 us (31%)
  waiting for transfers between devices  4.23 us (8%)
  between operations  0.99 us (2%)
    ppermute x12, starting transfers between devices, swap(): return lax.ppermute(message, 'ctx', [(i, i ^ 1 << b) for i in range(size)])  13.8 us
    pallas_call x2, Pallas kernels, query_grads(): pl.pallas_call(functools.partial(query_side, own, blocks, heads), name=la...  10.4 us
    pallas_call x2, Pallas kernels, scoring(): pl.pallas_call(functools.partial(local_scores, own, blocks, heads), name=...  7.3 us
    pallas_call x2, Pallas kernels, states(): pl.pallas_call(functools.partial(key_value_states, own, blocks, heads), n...  4.98 us
    pallas_call x2, Pallas kernels, key_grads(): pl.pallas_call(functools.partial(key_side, own, blocks, heads), name=labe...  4.08 us
    ppermute x3, waiting for transfers between devices, local(): lax.ppermute(sums, 'tp', [(i, (i + s) % tp) for i in range(tp)])  4.03 us
    ppermute x3, starting transfers between devices, local(): lax.ppermute(sums, 'tp', [(i, (i + s) % tp) for i in range(tp)])  3.82 us
    pallas_call x2, Pallas kernels, mixing(): pl.pallas_call(functools.partial(mixed, own, blocks, heads, lanes, tp), n...  3.04 us
  transfers between devices with their start and end apart: 15, of which 4 were waited for; matrix products, arithmetic and copies ran while one was open for 0% of the time, Pallas kernels for 45%

profile of v2, /device:TPU:1, one launch (start us, length us, event | category | flops | bytes accessed | tf_op | source)
XLA Modules:
  0.0 56.0 jit_solution(13468069983784690923)
XLA Ops:
  0.6 2.5 %states_other.1 = (bf16[1536,512]{1,0:T(8,128)(2,1)S(1)}, bf16[1536,512]{1,0:T(8,128)(2,1)S(1)}, f32[3072,128]{1,0:T(8,128)S(1)}, f32[520,128]{1,0:T(8,128)S(1)}, f32[8,128]{1,0:T(8,128)S(1)}) custom-call(s32[6]{0:T(128)} %docs_hbm.3, bf16[1536,1024]{1,0:T(8,128)(2,1)} %k_hbm.3, bf16[1536,1024]{1,0:T(8,128)(2,1)} %v_hbm.3), custom_call_target="tpu_custom_call" | custom-call | flops 201326592 | bytes 3145728 | tf_op jit(solution)/shard_map/states_other/pallas_call | solution.py:468
  3.1 0.2 collective-permute-start
  3.3 2.5 %states_own.1 = (bf16[1536,512]{1,0:T(8,128)(2,1)S(1)}, bf16[1536,512]{1,0:T(8,128)(2,1)S(1)}, f32[3072,128]{1,0:T(8,128)S(1)}, f32[520,128]{1,0:T(8,128)S(1)}) custom-call(s32[6]{0:T(128)} %docs_hbm.3, bf16[1536,1024]{1,0:T(8,128)(2,1)} %k_hbm.3, bf16[1536,1024]{1,0:T(8,128)(2,1)} %v_hbm.3), custom_call_target="tpu_custom_call" | custom-call | flops 201326592 | bytes 3145728 | tf_op jit(solution)/shard_map/states_own/pallas_call | solution.py:468
  5.8 0.0 collective-permute-done.refs_1_.refs_4_
  5.8 2.8 %collective-permute-start.2 = (f32[264,128]{1,0:T(8,128)S(1)}, f32[264,128]{1,0:T(8,128)S(1)}, u32[]{:S(2)}, u32[]{:S(2)}) collective-permute-start(f32[264,128]{1,0:T(8,128)S(1)} %get-tuple-element.68.refs_2_), channel_id=1, source_target_pairs={{0,16},{4,20},{8,24},{12,28},{16,0},{20,4},{24,8},{28,12},{1,17},{... | collective-permute-start | bytes 405512 | tf_op jit(solution)/shard_map/ppermute | solution.py:366
  8.6 1.2 %collective-permute-start.1 = (f32[264,128]{1,0:T(8,128)S(1)}, f32[264,128]{1,0:T(8,128)S(1)}, u32[]{:S(2)}, u32[]{:S(2)}) collective-permute-start(f32[264,128]{1,0:T(8,128)S(1)} %get-tuple-element.67.after.refs_0_), channel_id=1, source_target_pairs={{0,8},{4,12},{8,0},{12,4},{16,24},{20,28},{24,16},{28,20},{1,9},{5... | collective-permute-start | bytes 405512 | tf_op jit(solution)/shard_map/ppermute | solution.py:366
  9.8 3.7 %scoring_other.1 = (bf16[1536,512]{1,0:T(8,128)(2,1)S(1)}, bf16[1536,512]{1,0:T(8,128)(2,1)S(1)}, f32[1536,512]{1,0:T(8,128)S(1)}, bf16[6144,256]{1,0:T(8,128)(2,1)S(1)}, f32[8,128]{1,0:T(8,128)S(1)}) custom-call(f32[264,128]{1,0:T(8,128)S(1)} %get-tuple-element.67.after.refs_0_, bf16[1536,512]{1,0:T(8,128)(2,1)S(1)} %get-tuple-element.69.k, ...), custom_call_target="tpu_custom_call" | custom-call | flops 805306368 | bytes 3145728 | tf_op jit(solution)/shard_map/scoring_other/pallas_call | solution.py:480
  13.5 0.0 collective-permute-done.2.refs_3_.refs_2_
  13.5 0.0 collective-permute-done.1.refs_1_.refs_0_
  13.5 1.3 %collective-permute-start.4 = (f32[264,128]{1,0:T(8,128)S(1)}, f32[264,128]{1,0:T(8,128)S(1)}, u32[]{:S(2)}, u32[]{:S(2)}) collective-permute-start(f32[264,128]{1,0:T(8,128)S(1)} %get-tuple-element.73), channel_id=1, source_target_pairs={{0,8},{4,12},{8,0},{12,4},{16,24},{20,28},{24,16},{28,20},{1,9},{5... | collective-permute-start | bytes 405512 | tf_op jit(solution)/shard_map/ppermute | solution.py:366
  14.8 0.3 collective-permute-start.3
  15.1 0.0 copy-start
  15.1 3.7 %scoring_own.1 = (bf16[1536,512]{1,0:T(8,128)(2,1)S(1)}, bf16[1536,512]{1,0:T(8,128)(2,1)S(1)}, f32[1536,512]{1,0:T(8,128)S(1)}, bf16[6144,256]{1,0:T(8,128)(2,1)S(1)}, f32[8,128]{1,0:T(8,128)S(1)}) custom-call(f32[264,128]{1,0:T(8,128)S(1)} %get-tuple-element.72.after, bf16[1536,512]{1,0:T(8,128)(2,1)S(1)} %get-tuple-element.74.k, ...), custom_call_target="tpu_custom_call" | custom-call | flops 805306368 | bytes 3145728 | tf_op jit(solution)/shard_map/scoring_own/pallas_call | solution.py:480
  18.8 0.0 collective-permute-done.4.refs_3_
  18.8 0.2 collective-permute-done.3.refs_1_
  19.0 0.1 merge.8
  19.1 2.3 %collective-permute-start.5 = (f32[520,128]{1,0:T(8,128)S(1)}, f32[520,128]{1,0:T(8,128)S(1)}, u32[]{:S(2)}, u32[]{:S(2)}) collective-permute-start(f32[520,128]{1,0:T(8,128)S(1)} %get-tuple-element.77), channel_id=1, source_target_pairs={{0,4},{4,0},{8,12},{12,8},{16,20},{20,16},{24,28},{28,24},{1,5},{5... | collective-permute-start | bytes 798728 | tf_op jit(solution)/shard_map/ppermute | solution.py:366
  21.4 0.0 copy-done
  21.4 1.4 %attend_own.1 = (f32[1536,512]{1,0:T(8,128)S(1)}, bf16[3072,128]{1,0:T(8,128)(2,1)S(1)}, f32[256,128]{1,0:T(8,128)S(1)}) custom-call(f32[8,128]{1,0:T(8,128)S(1)} %get-tuple-element.63.docs, f32[3072,128]{1,0:T(8,128)S(1)} %get-tuple-element.81.inside, f32[520,128]{1,0:T(8,128)S(1)} %get-tuple-element.82.carry, ...), custom_call_target="tpu_custom_call" | custom-call | flops 201326592 | bytes 1048576 | tf_op jit(solution)/shard_map/attend_own/pallas_call | solution.py:494
  22.8 0.0 collective-permute-done.5.carry
  22.8 1.5 %attend_other.1 = (f32[1536,512]{1,0:T(8,128)S(1)}, bf16[3072,128]{1,0:T(8,128)(2,1)S(1)}, f32[16,256]{1,0:T(8,128)S(1)}) custom-call(f32[8,128]{1,0:T(8,128)S(1)} %get-tuple-element.63.docs, f32[3072,128]{1,0:T(8,128)S(1)} %get-tuple-element.64.inside, f32[520,128]{1,0:T(8,128)S(1)} %collective-permute-done.5.carry, ...), custom_call_target="tpu_custom_call" | custom-call | flops 201326592 | bytes 1048576 | tf_op jit(solution)/shard_map/attend_other/pallas_call | solution.py:494
  24.3 3.4 %collective-permute-start.8 = (f32[16,256]{1,0:T(8,128)S(1)}, f32[16,256]{1,0:T(8,128)S(1)}, u32[]{:S(2)}, u32[]{:S(2)}) collective-permute-start(f32[16,256]{1,0:T(8,128)S(1)} %get-tuple-element.87.rest_0_), channel_id=1, source_target_pairs={{0,3},{1,0},{2,1},{3,2},{4,7},{5,4},{6,5},{7,6},{8,11},{9,8},{10,9... | collective-permute-start | bytes 49160 | tf_op jit(solution)/shard_map/ppermute | solution.py:562
  27.7 0.0 collective-permute-start.7
  27.7 0.4 collective-permute-start.6
  28.1 0.4 collective-permute-done.8.rest_3_
  28.5 2.6 %collective-permute-done.7.rest_2_ = f32[16,256]{1,0:T(8,128)S(1)} collective-permute-done((f32[16,256]{1,0:T(8,128)S(1)}, f32[16,256]{1,0:T(8,128)S(1)}, u32[]{:S(2)}, u32[]{:S(2)}) %collective-permute-start.7) | collective-permute-done | bytes 16416 | tf_op jit(solution)/shard_map/ppermute | solution.py:562
  31.2 1.0 %collective-permute-done.6.rest_1_ = f32[16,256]{1,0:T(8,128)S(1)} collective-permute-done((f32[16,256]{1,0:T(8,128)S(1)}, f32[16,256]{1,0:T(8,128)S(1)}, u32[]{:S(2)}, u32[]{:S(2)}) %collective-permute-start.6) | collective-permute-done | bytes 16416 | tf_op jit(solution)/shard_map/ppermute | solution.py:562
  32.2 1.6 %mixed_other.1 = (bf16[1536,512]{1,0:T(8,128)(2,1)S(1)}, f32[3072,128]{1,0:T(8,128)S(1)}, f32[520,128]{1,0:T(8,128)S(1)}, f32[1536,128]{1,0:T(8,128)S(1)}, f32[1536,128]{1,0:T(8,128)S(1)}) custom-call(f32[8,128]{1,0:T(8,128)S(1)} %get-tuple-element.63.docs, f32[16,256]{1,0:T(8,128)S(1)} %get-tuple-element.87.rest_0_, ...), custom_call_target="tpu_custom_call" | custom-call | flops 201326592 | bytes 1048576 | tf_op jit(solution)/shard_map/mixed_other/pallas_call | solution.py:509
  33.7 1.5 %collective-permute-start.9 = (f32[520,128]{1,0:T(8,128)S(1)}, f32[520,128]{1,0:T(8,128)S(1)}, u32[]{:S(2)}, u32[]{:S(2)}) collective-permute-start(f32[520,128]{1,0:T(8,128)S(1)} %get-tuple-element.93), channel_id=1, source_target_pairs={{0,4},{4,0},{8,12},{12,8},{16,20},{20,16},{24,28},{28,24},{1,5},{5... | collective-permute-start | bytes 798728 | tf_op jit(solution)/shard_map/ppermute | solution.py:366
  35.2 1.5 %mixed_own.1 = (bf16[1536,512]{1,0:T(8,128)(2,1)S(1)}, f32[3072,128]{1,0:T(8,128)S(1)}, f32[520,128]{1,0:T(8,128)S(1)}) custom-call(f32[8,128]{1,0:T(8,128)S(1)} %get-tuple-element.63.docs, f32[1536,128]{1,0:T(8,128)S(1)} %get-tuple-element.89.rest_0_.scale, f32[1536,128]{1,0:T(8,128)S(1)} %get-tuple-element.90.rest_1_, ...), custom_call_target="tpu_custom_call" | custom-call | flops 201326592 | bytes 1048576 | tf_op jit(solution)/shard_map/mixed_own/pallas_call | solution.py:509
  36.7 0.0 collective-permute-done.9.refs_1_.refs_4_
  36.7 0.5 collective-permute-start.11
  37.2 0.3 collective-permute-start.10
  37.5 5.2 %query_side_other.1 = (bf16[1536,1024]{1,0:T(8,128)(2,1)}, bf16[1536,1024]{1,0:T(8,128)(2,1)}, f32[1536,512]{1,0:T(8,128)S(1)}, f32[1536,512]{1,0:T(8,128)S(1)}, f32[8,128]{1,0:T(8,128)S(1)}) custom-call(f32[264,128]{1,0:T(8,128)S(1)} %get-tuple-element.94.after.refs_0_, bf16[1536,512]{1,0:T(8,128)(2,1)S(1)} %get-tuple-element.69.k, ...), custom_call_target="tpu_custom_call" | custom-call | flops 1610612736 | bytes 3145728 | tf_op jit(solution)/shard_map/query_side_other/pallas_call | solution.py:523
  42.7 0.0 collective-permute-done.11.refs_3_.refs_2_
  42.7 0.0 collective-permute-done.10.refs_1_.refs_0_
  42.8 1.3 %collective-permute-start.13 = (f32[264,128]{1,0:T(8,128)S(1)}, f32[264,128]{1,0:T(8,128)S(1)}, u32[]{:S(2)}, u32[]{:S(2)}) collective-permute-start(f32[264,128]{1,0:T(8,128)S(1)} %get-tuple-element.109), channel_id=1, source_target_pairs={{0,8},{4,12},{8,0},{12,4},{16,24},{20,28},{24,16},{28,20},{1,9},{5... | collective-permute-start | bytes 405512 | tf_op jit(solution)/shard_map/ppermute | solution.py:366
  44.0 1.1 %collective-permute-start.12 = (f32[264,128]{1,0:T(8,128)S(1)}, f32[264,128]{1,0:T(8,128)S(1)}, u32[]{:S(2)}, u32[]{:S(2)}) collective-permute-start(f32[264,128]{1,0:T(8,128)S(1)} %get-tuple-element.100.after), channel_id=1, source_target_pairs={{0,16},{4,20},{8,24},{12,28},{16,0},{20,4},{24,8},{28,12},{1,17},{... | collective-permute-start | bytes 405512 | tf_op jit(solution)/shard_map/ppermute | solution.py:366
  45.1 5.2 %query_side_own.1 = (bf16[1536,1024]{1,0:T(8,128)(2,1)}, bf16[1536,1024]{1,0:T(8,128)(2,1)}, f32[1536,512]{1,0:T(8,128)S(1)}, f32[1536,512]{1,0:T(8,128)S(1)}, f32[8,128]{1,0:T(8,128)S(1)}) custom-call(f32[264,128]{1,0:T(8,128)S(1)} %get-tuple-element.100.after, ...), custom_call_target="tpu_custom_call", output_to_operand_aliasing={{0}: (10, {}), {1}: (11, {})} | custom-call | flops 1610612736 | bytes 3145728 | tf_op jit(solution)/shard_map/query_side_own/pallas_call | solution.py:523
  50.3 0.0 collective-permute-done.13.refs_3_
  50.3 0.0 collective-permute-done.12.refs_1_
  50.3 0.1 merge.11
  50.5 1.2 %collective-permute-start.14 = (f32[520,128]{1,0:T(8,128)S(1)}, f32[520,128]{1,0:T(8,128)S(1)}, u32[]{:S(2)}, u32[]{:S(2)}) collective-permute-start(f32[520,128]{1,0:T(8,128)S(1)} %get-tuple-element.111), channel_id=1, source_target_pairs={{0,4},{4,0},{8,12},{12,8},{16,20},{20,16},{24,28},{28,24},{1,5},{5... | collective-permute-start | bytes 798728 | tf_op jit(solution)/shard_map/ppermute | solution.py:366
  51.7 2.0 %key_side_own.1 = (bf16[1536,1024]{1,0:T(8,128)(2,1)}, bf16[1536,1024]{1,0:T(8,128)(2,1)}) custom-call(f32[8,128]{1,0:T(8,128)S(1)} %get-tuple-element.63.docs, f32[3072,128]{1,0:T(8,128)S(1)} %get-tuple-element.114.inside, f32[520,128]{1,0:T(8,128)S(1)} %get-tuple-element.115.carry, bf16[1536,512]{1,0:T(8,128)(2,1)S(1)} %get-tuple-element.74.k, ...), custom_call_target="tpu_custom_call" | custom-call | flops 402653184 | bytes 3145728 | tf_op jit(solution)/shard_map/key_side_own/pallas_call | solution.py:538
  53.8 0.0 collective-permute-done.14.carry
  53.8 2.0 %key_side_other.1 = (bf16[1536,1024]{1,0:T(8,128)(2,1)}, bf16[1536,1024]{1,0:T(8,128)(2,1)}) custom-call(f32[8,128]{1,0:T(8,128)S(1)} %get-tuple-element.63.docs, f32[3072,128]{1,0:T(8,128)S(1)} %get-tuple-element.108.inside, f32[520,128]{1,0:T(8,128)S(1)} %collective-permute-done.14.carry, ...), custom_call_target="tpu_custom_call", output_to_operand_aliasing={{0}: (7, {}), {1}: (8, {})} | custom-call | flops 402653184 | bytes 3145728 | tf_op jit(solution)/shard_map/key_side_other/pallas_call | solution.py:538
  (4 shorter events, 0.2 us)
Async XLA Ops:
  3.1 2.7 %collective-permute-start = (f32[520,128]{1,0:T(8,128)S(1)}, f32[520,128]{1,0:T(8,128)S(1)}, u32[]{:S(2)}, u32[]{:S(2)}) collective-permute-start(f32[520,128]{1,0:T(8,128)S(1)} %get-tuple-element.66), channel_id=1, source_target_pairs={{0,4},{4,0},{8,12},{12,8},{16,20},{20,16},{24,28},{28,24},{1,5},{5... | collective-permute-start | bytes 798728 | tf_op jit(solution)/shard_map/ppermute | solution.py:366
  5.8 7.6 %collective-permute-start.2 = (f32[264,128]{1,0:T(8,128)S(1)}, f32[264,128]{1,0:T(8,128)S(1)}, u32[]{:S(2)}, u32[]{:S(2)}) collective-permute-start(f32[264,128]{1,0:T(8,128)S(1)} %get-tuple-element.68.refs_2_), channel_id=1, source_target_pairs={{0,16},{4,20},{8,24},{12,28},{16,0},{20,4},{24,8},{28,12},{1,17},{... | collective-permute-start | bytes 405512 | tf_op jit(solution)/shard_map/ppermute | solution.py:366
  8.6 4.9 %collective-permute-start.1 = (f32[264,128]{1,0:T(8,128)S(1)}, f32[264,128]{1,0:T(8,128)S(1)}, u32[]{:S(2)}, u32[]{:S(2)}) collective-permute-start(f32[264,128]{1,0:T(8,128)S(1)} %get-tuple-element.67.after.refs_0_), channel_id=1, source_target_pairs={{0,8},{4,12},{8,0},{12,4},{16,24},{20,28},{24,16},{28,20},{1,9},{5... | collective-permute-start | bytes 405512 | tf_op jit(solution)/shard_map/ppermute | solution.py:366
  13.5 5.3 %collective-permute-start.4 = (f32[264,128]{1,0:T(8,128)S(1)}, f32[264,128]{1,0:T(8,128)S(1)}, u32[]{:S(2)}, u32[]{:S(2)}) collective-permute-start(f32[264,128]{1,0:T(8,128)S(1)} %get-tuple-element.73), channel_id=1, source_target_pairs={{0,8},{4,12},{8,0},{12,4},{16,24},{20,28},{24,16},{28,20},{1,9},{5... | collective-permute-start | bytes 405512 | tf_op jit(solution)/shard_map/ppermute | solution.py:366
  14.8 4.2 %collective-permute-start.3 = (f32[264,128]{1,0:T(8,128)S(1)}, f32[264,128]{1,0:T(8,128)S(1)}, u32[]{:S(2)}, u32[]{:S(2)}) collective-permute-start(f32[264,128]{1,0:T(8,128)S(1)} %get-tuple-element.72.after), channel_id=1, source_target_pairs={{0,16},{4,20},{8,24},{12,28},{16,0},{20,4},{24,8},{28,12},{1,17},{... | collective-permute-start | bytes 405512 | tf_op jit(solution)/shard_map/ppermute | solution.py:366
  15.1 6.3 %copy-start = (f32[1024]{0:T(1024)S(1)}, f32[1024]{0:T(1024)}, u32[]{:S(2)}) copy-start(f32[1024]{0:T(1024)} %param.10) | copy-start | bytes 12292
  19.1 3.7 %collective-permute-start.5 = (f32[520,128]{1,0:T(8,128)S(1)}, f32[520,128]{1,0:T(8,128)S(1)}, u32[]{:S(2)}, u32[]{:S(2)}) collective-permute-start(f32[520,128]{1,0:T(8,128)S(1)} %get-tuple-element.77), channel_id=1, source_target_pairs={{0,4},{4,0},{8,12},{12,8},{16,20},{20,16},{24,28},{28,24},{1,5},{5... | collective-permute-start | bytes 798728 | tf_op jit(solution)/shard_map/ppermute | solution.py:366
  24.3 4.2 %collective-permute-start.8 = (f32[16,256]{1,0:T(8,128)S(1)}, f32[16,256]{1,0:T(8,128)S(1)}, u32[]{:S(2)}, u32[]{:S(2)}) collective-permute-start(f32[16,256]{1,0:T(8,128)S(1)} %get-tuple-element.87.rest_0_), channel_id=1, source_target_pairs={{0,3},{1,0},{2,1},{3,2},{4,7},{5,4},{6,5},{7,6},{8,11},{9,8},{10,9... | collective-permute-start | bytes 49160 | tf_op jit(solution)/shard_map/ppermute | solution.py:562
  27.7 3.5 %collective-permute-start.7 = (f32[16,256]{1,0:T(8,128)S(1)}, f32[16,256]{1,0:T(8,128)S(1)}, u32[]{:S(2)}, u32[]{:S(2)}) collective-permute-start(f32[16,256]{1,0:T(8,128)S(1)} %get-tuple-element.87.rest_0_), channel_id=1, source_target_pairs={{0,2},{1,3},{2,0},{3,1},{4,6},{5,7},{6,4},{7,5},{8,10},{9,11},{10,... | collective-permute-start | bytes 49160 | tf_op jit(solution)/shard_map/ppermute | solution.py:562
  27.7 4.5 %collective-permute-start.6 = (f32[16,256]{1,0:T(8,128)S(1)}, f32[16,256]{1,0:T(8,128)S(1)}, u32[]{:S(2)}, u32[]{:S(2)}) collective-permute-start(f32[16,256]{1,0:T(8,128)S(1)} %get-tuple-element.87.rest_0_), channel_id=1, source_target_pairs={{0,1},{1,2},{2,3},{3,0},{4,5},{5,6},{6,7},{7,4},{8,9},{9,10},{10,1... | collective-permute-start | bytes 49160 | tf_op jit(solution)/shard_map/ppermute | solution.py:562
  33.7 2.9 %collective-permute-start.9 = (f32[520,128]{1,0:T(8,128)S(1)}, f32[520,128]{1,0:T(8,128)S(1)}, u32[]{:S(2)}, u32[]{:S(2)}) collective-permute-start(f32[520,128]{1,0:T(8,128)S(1)} %get-tuple-element.93), channel_id=1, source_target_pairs={{0,4},{4,0},{8,12},{12,8},{16,20},{20,16},{24,28},{28,24},{1,5},{5... | collective-permute-start | bytes 798728 | tf_op jit(solution)/shard_map/ppermute | solution.py:366
  36.7 6.0 %collective-permute-start.11 = (f32[264,128]{1,0:T(8,128)S(1)}, f32[264,128]{1,0:T(8,128)S(1)}, u32[]{:S(2)}, u32[]{:S(2)}) collective-permute-start(f32[264,128]{1,0:T(8,128)S(1)} %get-tuple-element.95.refs_2_), channel_id=1, source_target_pairs={{0,16},{4,20},{8,24},{12,28},{16,0},{20,4},{24,8},{28,12},{1,17},{... | collective-permute-start | bytes 405512 | tf_op jit(solution)/shard_map/ppermute | solution.py:366
  37.2 5.5 %collective-permute-start.10 = (f32[264,128]{1,0:T(8,128)S(1)}, f32[264,128]{1,0:T(8,128)S(1)}, u32[]{:S(2)}, u32[]{:S(2)}) collective-permute-start(f32[264,128]{1,0:T(8,128)S(1)} %get-tuple-element.94.after.refs_0_), channel_id=1, source_target_pairs={{0,8},{4,12},{8,0},{12,4},{16,24},{20,28},{24,16},{28,20},{1,9},{5... | collective-permute-start | bytes 405512 | tf_op jit(solution)/shard_map/ppermute | solution.py:366
  42.8 7.5 %collective-permute-start.13 = (f32[264,128]{1,0:T(8,128)S(1)}, f32[264,128]{1,0:T(8,128)S(1)}, u32[]{:S(2)}, u32[]{:S(2)}) collective-permute-start(f32[264,128]{1,0:T(8,128)S(1)} %get-tuple-element.109), channel_id=1, source_target_pairs={{0,8},{4,12},{8,0},{12,4},{16,24},{20,28},{24,16},{28,20},{1,9},{5... | collective-permute-start | bytes 405512 | tf_op jit(solution)/shard_map/ppermute | solution.py:366
  44.0 6.3 %collective-permute-start.12 = (f32[264,128]{1,0:T(8,128)S(1)}, f32[264,128]{1,0:T(8,128)S(1)}, u32[]{:S(2)}, u32[]{:S(2)}) collective-permute-start(f32[264,128]{1,0:T(8,128)S(1)} %get-tuple-element.100.after), channel_id=1, source_target_pairs={{0,16},{4,20},{8,24},{12,28},{16,0},{20,4},{24,8},{28,12},{1,17},{... | collective-permute-start | bytes 405512 | tf_op jit(solution)/shard_map/ppermute | solution.py:366
  50.5 3.3 %collective-permute-start.14 = (f32[520,128]{1,0:T(8,128)S(1)}, f32[520,128]{1,0:T(8,128)S(1)}, u32[]{:S(2)}, u32[]{:S(2)}) collective-permute-start(f32[520,128]{1,0:T(8,128)S(1)} %get-tuple-element.111), channel_id=1, source_target_pairs={{0,4},{4,0},{8,12},{12,8},{16,20},{20,16},{24,28},{28,24},{1,5},{5... | collective-permute-start | bytes 798728 | tf_op jit(solution)/shard_map/ppermute | solution.py:366

commit v3 on v2

--- a/solution.py
+++ b/solution.py
@@ -15,7 +15,6 @@
 MIB = 1 << 20
 U_SCORE = 6
 U_ATT = 6
-U_MIX = 6
 U_Q = 6
 U_K = 6
 T_ATT = 128
@@ -65,28 +64,37 @@
 
 
 def state_rows(n, h, heads):
-    return pl.ds(pl.multiple_of((n * heads + h) * HD, HD), HD)
-
-
-def key_value_states(own, blocks, heads, docs_hbm, k_hbm, v_hbm, *rest):
+    start = (n * heads + h) * HD
+    return pl.ds(start if isinstance(start, int) else pl.multiple_of(start, HD), HD)
+
+
+def key_value_states(own, blocks, heads, *refs):
     if own:
-        k, v, inside, message, docs, sems = rest
+        k, docs_hbm, v_hbm, v, inside, message, docs, sems = refs
     else:
-        k, v, inside, message, table, docs, sems = rest
+        docs_hbm, k_hbm, v_hbm, k, v, inside, message, table, k_own, docs, sems = refs
     off = half_start(own, heads * HD)
     docs_copy = pltpu.make_async_copy(docs_hbm, docs, sems.at[2 * heads])
     width = 2 * HD if heads % 2 == 0 else HD
+    groups = heads * HD // width
     copies = []
-    for i in range(heads * HD // width):
+    for i in range(groups):
         src, dst = pl.ds(off + i * width, width), pl.ds(i * width, width)
-        pair = (
-            pltpu.make_async_copy(k_hbm.at[:, src], k.at[:, dst], sems.at[2 * i]),
-            pltpu.make_async_copy(v_hbm.at[:, src], v.at[:, dst], sems.at[2 * i + 1]),
+        copies.append([pltpu.make_async_copy(v_hbm.at[:, src], v.at[:, dst], sems.at[2 * i])])
+        if not own:
+            copies[i].append(
+                pltpu.make_async_copy(k_hbm.at[:, src], k.at[:, dst], sems.at[2 * i + 1])
+            )
+        for copy in copies[i]:
+            copy.start()
+    docs_copy.start()
+    if not own:
+        ahead = pltpu.make_async_copy(
+            k_hbm.at[:, pl.ds(half_start(True, heads * HD), heads * HD)],
+            k_own,
+            sems.at[2 * heads + 1],
         )
-        for copy in pair:
-            copy.start()
-        copies.append(pair)
-    docs_copy.start()
+        ahead.start()
     docs_copy.wait()
     for h in range(heads):
         if h * HD % width == 0:
@@ -107,6 +115,7 @@
         table[...] = jnp.zeros(table.shape, F32)
         for n in range(blocks):
             table[n : n + 1, :] = jnp.full((1, HD), docs[n].astype(F32), F32)
+        ahead.wait()
 
 
 def causal_mask():
@@ -192,7 +201,7 @@
 def mixed(own, blocks, heads, lanes, parts, docs, *rest):
     if not own:
         pieces, rest = rest[:parts], rest[parts:]
-        attended, q, g, gain, grad, inside, message, scale, slope, running, turn = rest
+        attended, q, g, gain, grad, inside, message, scale, slope, turn = rest
         total = pieces[0][...]
         for piece in pieces[1:]:
             total = total + piece[...]
@@ -207,18 +216,16 @@
             scale[rows, :] = jnp.broadcast_to(columns[:, n : n + 1], (C, HD))
             slope[rows, :] = jnp.broadcast_to(columns[:, lanes + n : lanes + n + 1], (C, HD))
     else:
-        scale, slope, attended, q, g, gain, grad, inside, message, running = rest
+        scale, slope, attended, q, g, gain, grad, inside, message = rest
     off = half_start(own, heads * HD)
     gains = gain[:, pl.ds(off, heads * HD)]
-    running[...] = jnp.zeros((heads * HD, HD), F32)
     every = range(heads)
-
-    def step(i, carried):
-        n = blocks - 1 - i
-        rows = block(n)
-        linked = docs[pl.ds(n, 1), :] == docs[pl.ds(jnp.maximum(n - 1, 0), 1), :]
+    for h in every:
+        inside[state_rows(blocks - 1, h, heads), :] = jnp.zeros((HD, HD), F32)
+    for n in reversed(range(blocks)):
+        rows = pl.ds(n * C, C)
         for t in range(0, C, T_MIX):
-            part = pl.ds(pl.multiple_of(n * C + t, T_MIX), T_MIX)
+            part = pl.ds(n * C + t, T_MIX)
             r = scale[part, :]
             s = slope[part, :]
             for h in every:
@@ -226,15 +233,13 @@
                 d = r * weighted - attended[part, head(h)] * s
                 grad[part, head(h)] = d.astype(BF16)
         sums = [dot(q[rows, head(h)], grad[rows, head(h)], TN) for h in every]
-        befores = [running[head(h), :] for h in every]
         for h in every:
-            inside[state_rows(n, h, heads), :] = befores[h]
-            total = befores[h] + sums[h]
-            message[head(h), :] = total
-            running[head(h), :] = jnp.where(linked, total, 0.0)
-        return carried
-
-    lax.fori_loop(0, blocks, step, 0, unroll=U_MIX)
+            total = inside[state_rows(n, h, heads), :] + sums[h]
+            if n > 0:
+                linked = docs[n : n + 1, :] == docs[n - 1 : n, :]
+                inside[state_rows(n - 1, h, heads), :] = jnp.where(linked, total, 0.0)
+            else:
+                message[head(h), :] = total
     message[heads * HD :, :] = jnp.broadcast_to(-docs[0:1, :], (PAD, HD))
 
 
@@ -265,8 +270,8 @@
             dot(ds[h], low[state_rows(n, h, heads), :], NT) + dot(gs[h], k[rows, head(h)], NN)
             for h in every
         ]
-        kg = [dot(gs[h], q[rows, head(h)], TN) for h in every]
-        vg = [dot(scores[score_rows(n, h, heads), :], ds[h], TN) for h in every]
+        kg = [dot(q[rows, head(h)], gs[h], TN).T for h in every]
+        vg = [dot(ds[h], scores[score_rows(n, h, heads), :], TN).T for h in every]
         outs = [
             attended[rows, head(h)] * r * gains[:, h * HD : (h + 1) * HD] for h in every
         ]
@@ -320,40 +325,35 @@
 
 def merge_kernel(reverse, outs, count, *refs):
     size = lax.axis_size("ctx")
-    rank = lax.axis_index("ctx")
-    if reverse:
-        rank = size - 1 - rank
+    place = lax.axis_index("ctx")
+    rank = size - 1 - place if reverse else place
+    core = lax.rem(place, 2)
 
     def bit(b):
         return lax.rem(lax.div(rank, 1 << b), 2)
 
     ins, results = refs[:count], refs[count:]
-    for pieces, result in zip(outs, results):
-        at = 0
-        latest = None
-        for rows, terms in pieces:
-            keys = []
-            for source, start, flag in terms:
-                last = ins[source].shape[0] - PAD
-                key = ins[source][last : last + 1, :]
-                keys.append(key if flag is None else jnp.where(flag(bit), key, NEVER))
-            latest = functools.reduce(jnp.maximum, keys)
-            value = None
-            for (source, start, _), key in zip(terms, keys):
-                part = jnp.where(key == latest, ins[source][start : start + rows, :], 0.0)
-                value = part if value is None else value + part
-            result[at : at + rows, :] = value
-            at += rows
-        result[at:, :] = jnp.broadcast_to(latest, (PAD, HD))
+    rows = results[0].shape[0] - PAD
+    for terms, result in zip(outs, results):
+        keys = []
+        for source, flag in terms:
+            key = ins[source][rows : rows + 1, :]
+            keys.append(key if flag is None else jnp.where(flag(bit, core), key, NEVER))
+        latest = functools.reduce(jnp.maximum, keys)
+        parts = [
+            jnp.where(key == latest, ins[source][:rows, :], 0.0)
+            for (source, _), key in zip(terms, keys)
+        ]
+        result[:rows, :] = functools.reduce(jnp.add, parts)
+        result[rows:, :] = jnp.broadcast_to(latest, (PAD, HD))
 
 
 def merge(ins, outs, reverse, after=()):
-    shapes = [pltpu.VMEM((sum(rows for rows, _ in pieces) + PAD, HD), F32) for pieces in outs]
     ins = list(ins) + list(after)
     return pl.pallas_call(
         functools.partial(merge_kernel, reverse, outs, len(ins)),
         name="merge",
-        out_shape=shapes,
+        out_shape=[pltpu.VMEM(ins[0].shape, F32)] * len(outs),
         in_specs=[VM] * len(ins),
         out_specs=[VM] * len(outs),
         compiler_params=params(),
@@ -361,80 +361,61 @@
     )(*ins)
 
 
-def swap(message, b):
+def swap(message, even, odd):
     size = lax.axis_size("ctx")
-    return lax.ppermute(message, "ctx", [(i, i ^ (1 << b)) for i in range(size)])
+    pairs = [(i, i ^ (1 << (odd if i % 2 else even))) for i in range(size)]
+    return lax.ppermute(message, "ctx", pairs)
 
 
 def scan(theirs, mine, reverse, first_work, second_work):
-    rows = mine.shape[0] - PAD
-    part = rows // 2
     top = lax.axis_size("ctx").bit_length() - 1
     lo, hi = top - 2, top - 1
-    beside = swap(theirs, 0)
-    halves = [[(part, [(0, start, None), (1, start, None)])] for start in (0, part)]
-    total_a, total_b = merge([mine, beside], halves, reverse)
-    before_a, before_b = [], []
+    beside = swap(theirs, 0, 0)
+    (total,) = merge([mine, beside], [[(0, None), (1, None)]], reverse)
+    before = []
     for b in range(1, lo):
-        got_a, got_b = swap(total_a, b), swap(total_b, b)
-
-        def is_high(bit, b=b):
+        got = swap(total, b, b)
+
+        def is_high(bit, core, b=b):
             return bit(b) == 1
 
-        ins = [total_a, total_b, got_a, got_b] + before_a + before_b
-        earlier_a = [(4, 0, None)] if before_a else []
-        earlier_b = [(5, 0, None)] if before_b else []
-        total_a, total_b, pa, pb = merge(
-            ins,
-            [
-                [(part, [(0, 0, None), (2, 0, None)])],
-                [(part, [(1, 0, None), (3, 0, None)])],
-                [(part, [(2, 0, is_high)] + earlier_a)],
-                [(part, [(3, 0, is_high)] + earlier_b)],
-            ],
+        earlier = [(2, None)] if before else []
+        total, prior = merge(
+            [total, got] + before,
+            [[(0, None), (1, None)], [(1, is_high)] + earlier],
             reverse,
         )
-        before_a, before_b = [pa], [pb]
-    first_a, first_b = swap(total_a, lo), swap(total_b, hi)
-    first_done = first_work(total_a)
-    next_a, next_b = merge(
-        [total_a, first_a, total_b, first_b],
+        before = [prior]
+    first = swap(total, lo, hi)
+    first_done = first_work(total)
+    (onward,) = merge(
+        [total, first],
         [
-            [(part, [(0, 0, None), (1, 0, None)])],
             [
-                (
-                    part,
-                    [
-                        (2, 0, lambda bit: bit(lo) * bit(hi) == 0),
-                        (3, 0, lambda bit: bit(hi) == 1),
-                    ],
-                )
-            ],
+                (0, lambda bit, core: core * bit(lo) * bit(hi) == 0),
+                (1, lambda bit, core: core * (1 - bit(hi)) == 0),
+            ]
         ],
         reverse,
         first_done[-1:],
     )
-    second_a, second_b = swap(next_a, hi), swap(next_b, lo)
-    second_done = second_work(next_a, first_done)
-
-    def carried(neighbour, flag):
-        terms_a = [(0, 0, lambda bit: bit(lo) == 1), (1, 0, lambda bit: bit(hi) == 1)]
-        terms_b = [(2, 0, lambda bit: bit(hi) == 1), (3, 0, lambda bit: bit(lo) + bit(hi) > 0)]
-        if before_a:
-            terms_a.append((6, 0, None))
-            terms_b.append((7, 0, None))
+    second = swap(onward, hi, lo)
+    second_done = second_work(onward, first_done)
+
+    def carried(neighbour, low_core):
         return [
-            (part, terms_a + [(neighbour, 0, flag)]),
-            (part, terms_b + [(neighbour, part, flag)]),
-        ]
+            (0, lambda bit, core: (1 - core) * bit(lo) + core * bit(hi) == 1),
+            (1, lambda bit, core: bit(hi) + core * bit(lo) > 0),
+            (neighbour, lambda bit, core: bit(0) == low_core),
+        ] + ([(4, None)] if before else [])
 
     carry_mine, carry_theirs = merge(
-        [first_a, second_a, first_b, second_b, beside, mine] + before_a + before_b,
-        [carried(4, lambda bit: bit(0) == 1), carried(5, lambda bit: bit(0) == 0)],
+        [first, second, beside, mine] + before,
+        [carried(2, 1), carried(3, 0)],
         reverse,
         second_done[-1:],
     )
-    return carry_mine, swap(carry_theirs, 0), first_done[:-1], second_done[:-1]
+    return carry_mine, swap(carry_theirs, 0, 0), first_done[:-1], second_done[:-1]
 
 
 def local(queries, keys, values, out_grad, gain, doc_ids):
@@ -462,19 +443,21 @@
     ]
     token = pltpu.VMEM((PAD, HD), F32)
 
-    def states(own):
-        outs = [half_bf, half_bf, states_f32, message]
-        outs += [] if own else [pltpu.VMEM((lanes, HD), F32)]
+    def states(own, k):
+        ins = [k, docs_hbm, values] if own else [docs_hbm, keys, values]
+        outs = [half_bf, states_f32, message]
+        if not own:
+            outs = [half_bf] + outs + [pltpu.VMEM((lanes, HD), F32), half_bf]
         return pl.pallas_call(
             functools.partial(key_value_states, own, blocks, heads),
             name=label("states", own),
             out_shape=outs,
-            in_specs=[HB, HB, HB],
+            in_specs=[VM, HB, HB] if own else [HB, HB, HB],
             out_specs=[VM] * len(outs),
-            scratch_shapes=[pltpu.SMEM((blocks,), jnp.int32), dma((2 * heads + 1,))],
+            scratch_shapes=[pltpu.SMEM((blocks,), jnp.int32), dma((2 * heads + 2,))],
             compiler_params=params(),
             cost_estimate=cost(2 * pairs * narrow, 4 * tokens * cols),
-        )(docs_hbm, keys, values)
+        )(*ins)
 
     def scoring(own, k, v, after):
         return pl.pallas_call(
@@ -505,14 +488,13 @@
     def mixing(own, before, attended, q, g):
         ins = [docs] + before + [attended, q, g, gain]
         outs = [half_bf, states_f32, message] + ([] if own else [column, column])
-        scratch = [pltpu.VMEM((cols, HD), F32)]
         return pl.pallas_call(
             functools.partial(mixed, own, blocks, heads, lanes, tp),
             name=label("mixed", own),
             out_shape=outs,
             in_specs=[VM] * len(ins),
             out_specs=[VM] * len(outs),
-            scratch_shapes=scratch if own else scratch + [pltpu.VMEM((HD, C), F32)],
+            scratch_shapes=[] if own else [pltpu.VMEM((HD, C), F32)],
             compiler_params=params(),
             cost_estimate=cost(2 * pairs * narrow, 1 << 20),
         )(*ins)
@@ -547,8 +529,8 @@
             cost_estimate=cost(4 * pairs * narrow, 4 * tokens * cols),
         )(*ins)
 
-    k1, v1, inside1, theirs, docs = states(False)
-    k0, v0, inside0, mine = states(True)
+    k1, v1, inside1, theirs, docs, k0 = states(False, None)
+    v0, inside0, mine = states(True, k0)
     carry0, carry1, (q1, g1, local1, scores1), (q0, g0, local0, scores0) = scan(
         theirs,
         mine,

time: 56.2 us -> 53.1 us (0.945)
  Pallas kernels: 33.1 us -> 31.2 us
  starting transfers between devices: 17.6 us -> 15.9 us
  waiting for transfers between devices: 4.23 us -> 4.95 us
    ppermute x12 -> x8, starting transfers between devices: 13.8 us -> 11.6 us  [swap(): return lax.ppermute(message, 'ctx', pairs)]
    pallas_call x2, Pallas kernels: 10.4 us -> 8.82 us  [query_grads(): pl.pallas_call(functools.partial(query_side, own, blocks, heads), name=la...]
    ppermute x12 -> x8, waiting for transfers between devices: 0.2 us -> 0.92 us  [swap(): return lax.ppermute(message, 'ctx', pairs)]
  transfers between devices with their start and end apart: 15 -> 11, of which waited for: 4 -> 5; matrix products, arithmetic and copies ran while one was open for 0% -> 0% of each run, Pallas kernels for 45% -> 44%
where the time goes in v3:
time: 53.1 us; the launch traced here: 52.9 us
  Pallas kernels  31.2 us (59%)
  starting transfers between devices  15.9 us (30%)
  waiting for transfers between devices  4.95 us (9%)
  between operations  0.94 us (2%)
    ppermute x8, starting transfers between devices, swap(): return lax.ppermute(message, 'ctx', pairs)  11.6 us
    pallas_call x2, Pallas kernels, query_grads(): pl.pallas_call(functools.partial(query_side, own, blocks, heads), name=la...  8.82 us
    pallas_call x2, Pallas kernels, scoring(): pl.pallas_call(functools.partial(local_scores, own, blocks, heads), name=...  7.31 us
    pallas_call x2, Pallas kernels, states(): pl.pallas_call(functools.partial(key_value_states, own, blocks, heads), n...  4.58 us
    ppermute x3, starting transfers between devices, local(): lax.ppermute(sums, 'tp', [(i, (i + s) % tp) for i in range(tp)])  4.31 us
    pallas_call x2, Pallas kernels, key_grads(): pl.pallas_call(functools.partial(key_side, own, blocks, heads), name=labe...  4.07 us
    ppermute x3, waiting for transfers between devices, local(): lax.ppermute(sums, 'tp', [(i, (i + s) % tp) for i in range(tp)])  4.03 us
    pallas_call x2, Pallas kernels, mixing(): pl.pallas_call(functools.partial(mixed, own, blocks, heads, lanes, tp), n...  3.07 us
  transfers between devices with their start and end apart: 11, of which 5 were waited for; matrix products, arithmetic and copies ran while one was open for 0% of the time, Pallas kernels for 44%

profile of v3, /device:TPU:1, one launch (start us, length us, event | category | flops | bytes accessed | tf_op | source)
XLA Modules:
  0.0 52.9 jit_solution(12535902644511284721)
XLA Ops:
  0.6 2.5 %states_other.1 = (bf16[1536,512]{1,0:T(8,128)(2,1)S(1)}, bf16[1536,512]{1,0:T(8,128)(2,1)S(1)}, f32[3072,128]{1,0:T(8,128)S(1)}, f32[520,128]{1,0:T(8,128)S(1)}...) custom-call(s32[6]{0:T(128)} %refs_1_.3, bf16[1536,1024]{1,0:T(8,128)(2,1)} %refs_1_.2, bf16[1536,1024]{1,0:T(8,128)(2,1)} %refs_2_.3), custom_call_target="tpu_custom_call" | custom-call | flops 201326592 | bytes 3145728 | tf_op jit(solution)/shard_map/states_other/pallas_call | solution.py:451
  3.2 0.1 collective-permute-start
  3.3 2.1 %states_own.1 = (bf16[1536,512]{1,0:T(8,128)(2,1)S(1)}, f32[3072,128]{1,0:T(8,128)S(1)}, f32[520,128]{1,0:T(8,128)S(1)}) custom-call(bf16[1536,512]{1,0:T(8,128)(2,1)S(1)} %get-tuple-element.57.refs_0_.k, s32[6]{0:T(128)} %refs_1_.3, bf16[1536,1024]{1,0:T(8,128)(2,1)} %refs_2_.3), custom_call_target="tpu_custom_call" | custom-call | flops 201326592 | bytes 3145728 | tf_op jit(solution)/shard_map/states_own/pallas_call | solution.py:451
  5.4 0.0 collective-permute-done.refs_1_.refs_2_
  5.4 2.8 %collective-permute-start.1 = (f32[520,128]{1,0:T(8,128)S(1)}, f32[520,128]{1,0:T(8,128)S(1)}, u32[]{:S(2)}, u32[]{:S(2)}) collective-permute-start(f32[520,128]{1,0:T(8,128)S(1)} %merge.6.after.refs_0_), channel_id=1, source_target_pairs={{0,8},{4,20},{8,0},{12,28},{16,24},{20,4},{24,16},{28,12},{1,9},{5... | collective-permute-start | bytes 798728 | tf_op jit(solution)/shard_map/ppermute | solution.py:367
  8.2 3.7 %scoring_other.1 = (bf16[1536,512]{1,0:T(8,128)(2,1)S(1)}, bf16[1536,512]{1,0:T(8,128)(2,1)S(1)}, f32[1536,512]{1,0:T(8,128)S(1)}, bf16[6144,256]{1,0:T(8,128)(2,1)S(1)}, f32[8,128]{1,0:T(8,128)S(1)}) custom-call(f32[520,128]{1,0:T(8,128)S(1)} %merge.6.after.refs_0_, bf16[1536,512]{1,0:T(8,128)(2,1)S(1)} %get-tuple-element.60.k, ...), custom_call_target="tpu_custom_call" | custom-call | flops 805306368 | bytes 3145728 | tf_op jit(solution)/shard_map/scoring_other/pallas_call | solution.py:463
  11.8 0.4 collective-permute-done.1.refs_1_.refs_0_
  12.3 1.5 %collective-permute-start.2 = (f32[520,128]{1,0:T(8,128)S(1)}, f32[520,128]{1,0:T(8,128)S(1)}, u32[]{:S(2)}, u32[]{:S(2)}) collective-permute-start(f32[520,128]{1,0:T(8,128)S(1)} %merge.7.after), channel_id=1, source_target_pairs={{0,16},{4,12},{8,24},{12,4},{16,0},{20,28},{24,8},{28,20},{1,17},{... | collective-permute-start | bytes 798728 | tf_op jit(solution)/shard_map/ppermute | solution.py:367
  13.8 0.0 copy-start
  13.8 3.7 %scoring_own.1 = (bf16[1536,512]{1,0:T(8,128)(2,1)S(1)}, bf16[1536,512]{1,0:T(8,128)(2,1)S(1)}, f32[1536,512]{1,0:T(8,128)S(1)}, bf16[6144,256]{1,0:T(8,128)(2,1)S(1)}, f32[8,128]{1,0:T(8,128)S(1)}) custom-call(f32[520,128]{1,0:T(8,128)S(1)} %merge.7.after, bf16[1536,512]{1,0:T(8,128)(2,1)S(1)} %get-tuple-element.57.refs_0_.k, ...), custom_call_target="tpu_custom_call" | custom-call | flops 805306368 | bytes 3145728 | tf_op jit(solution)/shard_map/scoring_own/pallas_call | solution.py:463
  17.5 0.5 collective-permute-done.2.refs_1_
  17.9 0.1 merge.8
  18.1 1.5 %collective-permute-start.3 = (f32[520,128]{1,0:T(8,128)S(1)}, f32[520,128]{1,0:T(8,128)S(1)}, u32[]{:S(2)}, u32[]{:S(2)}) collective-permute-start(f32[520,128]{1,0:T(8,128)S(1)} %get-tuple-element.65), channel_id=1, source_target_pairs={{0,4},{4,0},{8,12},{12,8},{16,20},{20,16},{24,28},{28,24},{1,5},{5... | collective-permute-start | bytes 798728 | tf_op jit(solution)/shard_map/ppermute | solution.py:367
  19.6 0.0 copy-done
  19.6 1.4 %attend_own.1 = (f32[1536,512]{1,0:T(8,128)S(1)}, bf16[3072,128]{1,0:T(8,128)(2,1)S(1)}, f32[256,128]{1,0:T(8,128)S(1)}) custom-call(f32[8,128]{1,0:T(8,128)S(1)} %get-tuple-element.55.docs, f32[3072,128]{1,0:T(8,128)S(1)} %get-tuple-element.69.inside, f32[520,128]{1,0:T(8,128)S(1)} %get-tuple-element.70.carry, ...), custom_call_target="tpu_custom_call" | custom-call | flops 201326592 | bytes 1048576 | tf_op jit(solution)/shard_map/attend_own/pallas_call | solution.py:477
  21.0 0.0 collective-permute-done.3.carry
  21.0 1.5 %attend_other.1 = (f32[1536,512]{1,0:T(8,128)S(1)}, bf16[3072,128]{1,0:T(8,128)(2,1)S(1)}, f32[16,256]{1,0:T(8,128)S(1)}) custom-call(f32[8,128]{1,0:T(8,128)S(1)} %get-tuple-element.55.docs, f32[3072,128]{1,0:T(8,128)S(1)} %get-tuple-element.56.inside, f32[520,128]{1,0:T(8,128)S(1)} %collective-permute-done.3.carry, ...), custom_call_target="tpu_custom_call" | custom-call | flops 201326592 | bytes 1048576 | tf_op jit(solution)/shard_map/attend_other/pallas_call | solution.py:477
  22.5 3.9 %collective-permute-start.6 = (f32[16,256]{1,0:T(8,128)S(1)}, f32[16,256]{1,0:T(8,128)S(1)}, u32[]{:S(2)}, u32[]{:S(2)}) collective-permute-start(f32[16,256]{1,0:T(8,128)S(1)} %get-tuple-element.75.rest_0_), channel_id=1, source_target_pairs={{0,3},{1,0},{2,1},{3,2},{4,7},{5,4},{6,5},{7,6},{8,11},{9,8},{10,9... | collective-permute-start | bytes 49160 | tf_op jit(solution)/shard_map/ppermute | solution.py:544
  26.3 0.0 collective-permute-start.5
  26.3 0.5 collective-permute-start.4
  26.8 0.4 collective-permute-done.6.rest_3_
  27.2 2.6 %collective-permute-done.5.rest_2_ = f32[16,256]{1,0:T(8,128)S(1)} collective-permute-done((f32[16,256]{1,0:T(8,128)S(1)}, f32[16,256]{1,0:T(8,128)S(1)}, u32[]{:S(2)}, u32[]{:S(2)}) %collective-permute-start.5) | collective-permute-done | bytes 16416 | tf_op jit(solution)/shard_map/ppermute | solution.py:544
  29.8 1.0 %collective-permute-done.4.rest_1_ = f32[16,256]{1,0:T(8,128)S(1)} collective-permute-done((f32[16,256]{1,0:T(8,128)S(1)}, f32[16,256]{1,0:T(8,128)S(1)}, u32[]{:S(2)}, u32[]{:S(2)}) %collective-permute-start.4) | collective-permute-done | bytes 16416 | tf_op jit(solution)/shard_map/ppermute | solution.py:544
  30.8 1.6 %mixed_other.1 = (bf16[1536,512]{1,0:T(8,128)(2,1)S(1)}, f32[3072,128]{1,0:T(8,128)S(1)}, f32[520,128]{1,0:T(8,128)S(1)}, f32[1536,128]{1,0:T(8,128)S(1)}, f32[1536,128]{1,0:T(8,128)S(1)}) custom-call(f32[8,128]{1,0:T(8,128)S(1)} %get-tuple-element.55.docs, f32[16,256]{1,0:T(8,128)S(1)} %get-tuple-element.75.rest_0_, ...), custom_call_target="tpu_custom_call" | custom-call | flops 201326592 | bytes 1048576 | tf_op jit(solution)/shard_map/mixed_other/pallas_call | solution.py:491
  32.4 1.5 %collective-permute-start.7 = (f32[520,128]{1,0:T(8,128)S(1)}, f32[520,128]{1,0:T(8,128)S(1)}, u32[]{:S(2)}, u32[]{:S(2)}) collective-permute-start(f32[520,128]{1,0:T(8,128)S(1)} %get-tuple-element.81), channel_id=1, source_target_pairs={{0,4},{4,0},{8,12},{12,8},{16,20},{20,16},{24,28},{28,24},{1,5},{5... | collective-permute-start | bytes 798728 | tf_op jit(solution)/shard_map/ppermute | solution.py:367
  33.9 1.5 %mixed_own.1 = (bf16[1536,512]{1,0:T(8,128)(2,1)S(1)}, f32[3072,128]{1,0:T(8,128)S(1)}, f32[520,128]{1,0:T(8,128)S(1)}) custom-call(f32[8,128]{1,0:T(8,128)S(1)} %get-tuple-element.55.docs, f32[1536,128]{1,0:T(8,128)S(1)} %get-tuple-element.77.rest_0_.scale, f32[1536,128]{1,0:T(8,128)S(1)} %get-tuple-element.78.rest_1_, ...), custom_call_target="tpu_custom_call" | custom-call | flops 201326592 | bytes 1048576 | tf_op jit(solution)/shard_map/mixed_own/pallas_call | solution.py:491
  35.4 0.0 collective-permute-done.7.refs_1_.refs_2_
  35.4 1.3 %collective-permute-start.8 = (f32[520,128]{1,0:T(8,128)S(1)}, f32[520,128]{1,0:T(8,128)S(1)}, u32[]{:S(2)}, u32[]{:S(2)}) collective-permute-start(f32[520,128]{1,0:T(8,128)S(1)} %merge.9.after.refs_0_), channel_id=1, source_target_pairs={{0,8},{4,20},{8,0},{12,28},{16,24},{20,4},{24,16},{28,12},{1,9},{5... | collective-permute-start | bytes 798728 | tf_op jit(solution)/shard_map/ppermute | solution.py:367
  36.7 4.4 %query_side_other.1 = (bf16[1536,1024]{1,0:T(8,128)(2,1)}, bf16[1536,1024]{1,0:T(8,128)(2,1)}, f32[1536,512]{1,0:T(8,128)S(1)}, f32[1536,512]{1,0:T(8,128)S(1)}, f32[8,128]{1,0:T(8,128)S(1)}) custom-call(f32[520,128]{1,0:T(8,128)S(1)} %merge.9.after.refs_0_, bf16[1536,512]{1,0:T(8,128)(2,1)S(1)} %get-tuple-element.60.k, ...), custom_call_target="tpu_custom_call" | custom-call | flops 1610612736 | bytes 3145728 | tf_op jit(solution)/shard_map/query_side_other/pallas_call | solution.py:505
  41.1 0.0 collective-permute-done.8.refs_1_.refs_0_
  41.2 0.1 merge.10.after
  41.2 1.3 %collective-permute-start.9 = (f32[520,128]{1,0:T(8,128)S(1)}, f32[520,128]{1,0:T(8,128)S(1)}, u32[]{:S(2)}, u32[]{:S(2)}) collective-permute-start(f32[520,128]{1,0:T(8,128)S(1)} %merge.10.after), channel_id=1, source_target_pairs={{0,16},{4,12},{8,24},{12,4},{16,0},{20,28},{24,8},{28,20},{1,17},{... | collective-permute-start | bytes 798728 | tf_op jit(solution)/shard_map/ppermute | solution.py:367
  42.5 4.4 %query_side_own.1 = (bf16[1536,1024]{1,0:T(8,128)(2,1)}, bf16[1536,1024]{1,0:T(8,128)(2,1)}, f32[1536,512]{1,0:T(8,128)S(1)}, f32[1536,512]{1,0:T(8,128)S(1)}, f32[8,128]{1,0:T(8,128)S(1)}) custom-call(f32[520,128]{1,0:T(8,128)S(1)} %merge.10.after, ...), custom_call_target="tpu_custom_call", output_to_operand_aliasing={{0}: (10, {}), {1}: (11, {})} | custom-call | flops 1610612736 | bytes 3145728 | tf_op jit(solution)/shard_map/query_side_own/pallas_call | solution.py:505
  46.9 0.0 collective-permute-done.9.refs_1_
  46.9 0.1 merge.11
  47.1 1.6 %collective-permute-start.10 = (f32[520,128]{1,0:T(8,128)S(1)}, f32[520,128]{1,0:T(8,128)S(1)}, u32[]{:S(2)}, u32[]{:S(2)}) collective-permute-start(f32[520,128]{1,0:T(8,128)S(1)} %get-tuple-element.95), channel_id=1, source_target_pairs={{0,4},{4,0},{8,12},{12,8},{16,20},{20,16},{24,28},{28,24},{1,5},{5... | collective-permute-start | bytes 798728 | tf_op jit(solution)/shard_map/ppermute | solution.py:367
  48.7 2.0 %key_side_own.1 = (bf16[1536,1024]{1,0:T(8,128)(2,1)}, bf16[1536,1024]{1,0:T(8,128)(2,1)}) custom-call(f32[8,128]{1,0:T(8,128)S(1)} %get-tuple-element.55.docs, f32[3072,128]{1,0:T(8,128)S(1)} %get-tuple-element.98.inside, f32[520,128]{1,0:T(8,128)S(1)} %get-tuple-element.99.carry, bf16[1536,512]{1,0:T(8,128)(2,1)S(1)} %get-tuple-element.57.refs_0_.k, ...), custom_call_target="tpu_custom_call" | custom-call | flops 402653184 | bytes 3145728 | tf_op jit(solution)/shard_map/key_side_own/pallas_call | solution.py:520
  50.7 0.0 collective-permute-done.10.carry
  50.7 2.0 %key_side_other.1 = (bf16[1536,1024]{1,0:T(8,128)(2,1)}, bf16[1536,1024]{1,0:T(8,128)(2,1)}) custom-call(f32[8,128]{1,0:T(8,128)S(1)} %get-tuple-element.55.docs, f32[3072,128]{1,0:T(8,128)S(1)} %get-tuple-element.93.inside, f32[520,128]{1,0:T(8,128)S(1)} %collective-permute-done.10.carry, ...), custom_call_target="tpu_custom_call", output_to_operand_aliasing={{0}: (7, {}), {1}: (8, {})} | custom-call | flops 402653184 | bytes 3145728 | tf_op jit(solution)/shard_map/key_side_other/pallas_call | solution.py:520
  (3 shorter events, 0.1 us)
Async XLA Ops:
  3.2 2.2 %collective-permute-start = (f32[520,128]{1,0:T(8,128)S(1)}, f32[520,128]{1,0:T(8,128)S(1)}, u32[]{:S(2)}, u32[]{:S(2)}) collective-permute-start(f32[520,128]{1,0:T(8,128)S(1)} %get-tuple-element.59), channel_id=1, source_target_pairs={{0,4},{4,0},{8,12},{12,8},{16,20},{20,16},{24,28},{28,24},{1,5},{5... | collective-permute-start | bytes 798728 | tf_op jit(solution)/shard_map/ppermute | solution.py:367
  5.4 6.9 %collective-permute-start.1 = (f32[520,128]{1,0:T(8,128)S(1)}, f32[520,128]{1,0:T(8,128)S(1)}, u32[]{:S(2)}, u32[]{:S(2)}) collective-permute-start(f32[520,128]{1,0:T(8,128)S(1)} %merge.6.after.refs_0_), channel_id=1, source_target_pairs={{0,8},{4,20},{8,0},{12,28},{16,24},{20,4},{24,16},{28,12},{1,9},{5... | collective-permute-start | bytes 798728 | tf_op jit(solution)/shard_map/ppermute | solution.py:367
  12.3 5.6 %collective-permute-start.2 = (f32[520,128]{1,0:T(8,128)S(1)}, f32[520,128]{1,0:T(8,128)S(1)}, u32[]{:S(2)}, u32[]{:S(2)}) collective-permute-start(f32[520,128]{1,0:T(8,128)S(1)} %merge.7.after), channel_id=1, source_target_pairs={{0,16},{4,12},{8,24},{12,4},{16,0},{20,28},{24,8},{28,20},{1,17},{... | collective-permute-start | bytes 798728 | tf_op jit(solution)/shard_map/ppermute | solution.py:367
  13.8 5.8 %copy-start = (f32[1024]{0:T(1024)S(1)}, f32[1024]{0:T(1024)}, u32[]{:S(2)}) copy-start(f32[1024]{0:T(1024)} %param.10) | copy-start | bytes 12292
  18.1 3.0 %collective-permute-start.3 = (f32[520,128]{1,0:T(8,128)S(1)}, f32[520,128]{1,0:T(8,128)S(1)}, u32[]{:S(2)}, u32[]{:S(2)}) collective-permute-start(f32[520,128]{1,0:T(8,128)S(1)} %get-tuple-element.65), channel_id=1, source_target_pairs={{0,4},{4,0},{8,12},{12,8},{16,20},{20,16},{24,28},{28,24},{1,5},{5... | collective-permute-start | bytes 798728 | tf_op jit(solution)/shard_map/ppermute | solution.py:367
  22.5 4.7 %collective-permute-start.6 = (f32[16,256]{1,0:T(8,128)S(1)}, f32[16,256]{1,0:T(8,128)S(1)}, u32[]{:S(2)}, u32[]{:S(2)}) collective-permute-start(f32[16,256]{1,0:T(8,128)S(1)} %get-tuple-element.75.rest_0_), channel_id=1, source_target_pairs={{0,3},{1,0},{2,1},{3,2},{4,7},{5,4},{6,5},{7,6},{8,11},{9,8},{10,9... | collective-permute-start | bytes 49160 | tf_op jit(solution)/shard_map/ppermute | solution.py:544
  26.3 3.5 %collective-permute-start.5 = (f32[16,256]{1,0:T(8,128)S(1)}, f32[16,256]{1,0:T(8,128)S(1)}, u32[]{:S(2)}, u32[]{:S(2)}) collective-permute-start(f32[16,256]{1,0:T(8,128)S(1)} %get-tuple-element.75.rest_0_), channel_id=1, source_target_pairs={{0,2},{1,3},{2,0},{3,1},{4,6},{5,7},{6,4},{7,5},{8,10},{9,11},{10,... | collective-permute-start | bytes 49160 | tf_op jit(solution)/shard_map/ppermute | solution.py:544
  26.3 4.5 %collective-permute-start.4 = (f32[16,256]{1,0:T(8,128)S(1)}, f32[16,256]{1,0:T(8,128)S(1)}, u32[]{:S(2)}, u32[]{:S(2)}) collective-permute-start(f32[16,256]{1,0:T(8,128)S(1)} %get-tuple-element.75.rest_0_), channel_id=1, source_target_pairs={{0,1},{1,2},{2,3},{3,0},{4,5},{5,6},{6,7},{7,4},{8,9},{9,10},{10,1... | collective-permute-start | bytes 49160 | tf_op jit(solution)/shard_map/ppermute | solution.py:544
  32.4 3.0 %collective-permute-start.7 = (f32[520,128]{1,0:T(8,128)S(1)}, f32[520,128]{1,0:T(8,128)S(1)}, u32[]{:S(2)}, u32[]{:S(2)}) collective-permute-start(f32[520,128]{1,0:T(8,128)S(1)} %get-tuple-element.81), channel_id=1, source_target_pairs={{0,4},{4,0},{8,12},{12,8},{16,20},{20,16},{24,28},{28,24},{1,5},{5... | collective-permute-start | bytes 798728 | tf_op jit(solution)/shard_map/ppermute | solution.py:367
  35.4 5.7 %collective-permute-start.8 = (f32[520,128]{1,0:T(8,128)S(1)}, f32[520,128]{1,0:T(8,128)S(1)}, u32[]{:S(2)}, u32[]{:S(2)}) collective-permute-start(f32[520,128]{1,0:T(8,128)S(1)} %merge.9.after.refs_0_), channel_id=1, source_target_pairs={{0,8},{4,20},{8,0},{12,28},{16,24},{20,4},{24,16},{28,12},{1,9},{5... | collective-permute-start | bytes 798728 | tf_op jit(solution)/shard_map/ppermute | solution.py:367
  41.2 5.7 %collective-permute-start.9 = (f32[520,128]{1,0:T(8,128)S(1)}, f32[520,128]{1,0:T(8,128)S(1)}, u32[]{:S(2)}, u32[]{:S(2)}) collective-permute-start(f32[520,128]{1,0:T(8,128)S(1)} %merge.10.after), channel_id=1, source_target_pairs={{0,16},{4,12},{8,24},{12,4},{16,0},{20,28},{24,8},{28,20},{1,17},{... | collective-permute-start | bytes 798728 | tf_op jit(solution)/shard_map/ppermute | solution.py:367
  47.1 3.6 %collective-permute-start.10 = (f32[520,128]{1,0:T(8,128)S(1)}, f32[520,128]{1,0:T(8,128)S(1)}, u32[]{:S(2)}, u32[]{:S(2)}) collective-permute-start(f32[520,128]{1,0:T(8,128)S(1)} %get-tuple-element.95), channel_id=1, source_target_pairs={{0,4},{4,0},{8,12},{12,8},{16,20},{20,16},{24,28},{28,24},{1,5},{5... | collective-permute-start | bytes 798728 | tf_op jit(solution)/shard_map/ppermute | solution.py:367

commit v4 on v3

--- a/solution.py
+++ b/solution.py
@@ -13,7 +13,7 @@
 PAD = 8
 NEVER = -1.0e9
 MIB = 1 << 20
-U_SCORE = 6
+U_SCORE = 4
 U_ATT = 6
 U_Q = 6
 U_K = 6
@@ -60,7 +60,7 @@
 
 
 def block(n):
-    return pl.ds(pl.multiple_of(n * C, C), C)
+    return pl.ds(n * C if isinstance(n, int) else pl.multiple_of(n * C, C), C)
 
 
 def state_rows(n, h, heads):
@@ -123,49 +123,48 @@
 
 
 def score_rows(n, h, heads):
-    return pl.ds(pl.multiple_of((n * heads + h) * C, C), C)
+    start = (n * heads + h) * C
+    return pl.ds(start if isinstance(start, int) else pl.multiple_of(start, C), C)
 
 
 def local_scores(
-    own, blocks, heads, after, k, v, q_hbm, g_hbm, q, g, local, scores, done, q_sems, g_sem
+    own, blocks, heads, after, k, v, gain, q_hbm, g_hbm, q, weighted, local, scores, done, g, sems
 ):
-    cols = pl.ds(half_start(own, heads * HD), heads * HD)
-
-    def q_copy(n):
-        return pltpu.make_async_copy(q_hbm.at[block(n), cols], q.at[block(n), :], q_sems.at[n])
-
-    for n in range(blocks):
-        q_copy(n).start()
-    g_copy = pltpu.make_async_copy(g_hbm.at[:, cols], g, g_sem)
+    off = half_start(own, heads * HD)
+    gains = gain[:, pl.ds(off, heads * HD)]
+    group = 2 if heads % 2 == 0 else 1
+    copies = []
+    for h in range(0, heads, group):
+        src, dst = pl.ds(off + h * HD, group * HD), pl.ds(h * HD, group * HD)
+        copies.append(pltpu.make_async_copy(q_hbm.at[:, src], q.at[:, dst], sems.at[h]))
+        copies[-1].start()
+    g_copy = pltpu.make_async_copy(g_hbm.at[:, pl.ds(off, heads * HD)], g, sems.at[heads])
     g_copy.start()
     causal = causal_mask()
-    every = range(heads)
-
-    def step(n, carry):
-        q_copy(n).wait()
-        rows = block(n)
-        raw = [dot(q[rows, head(h)], k[rows, head(h)], NT) for h in every]
-        low = [jnp.where(causal, s, 0.0).astype(BF16) for s in raw]
-        outs = [dot(low[h], v[rows, head(h)], NN) for h in every]
-        for h in every:
-            scores[score_rows(n, h, heads), :] = low[h]
-            local[rows, head(h)] = outs[h]
-        return carry
-
-    lax.fori_loop(0, blocks, step, 0, unroll=U_SCORE)
+    for h in range(0, heads, group):
+        copies[h // group].wait()
+        units = [(n, i) for n in range(blocks) for i in range(h, h + group)]
+        for at in range(0, len(units), U_SCORE):
+            now = units[at : at + U_SCORE]
+            raw = [dot(q[block(n), head(i)], k[block(n), head(i)], NT) for n, i in now]
+            low = [jnp.where(causal, s, 0.0).astype(BF16) for s in raw]
+            outs = [dot(s, v[block(n), head(i)], NN) for s, (n, i) in zip(low, now)]
+            for (n, i), s, out in zip(now, low, outs):
+                scores[score_rows(n, i, heads), :] = s
+                local[block(n), head(i)] = out
     g_copy.wait()
+    for n in range(blocks):
+        weighted[block(n), :] = g[block(n), :].astype(F32) * gains
     done[...] = jnp.zeros(done.shape, F32)
 
 
-def attend(own, blocks, heads, lanes, docs, inside, carry, q, local, g, gain, *rest):
+def attend(own, blocks, heads, lanes, docs, inside, carry, q, local, weighted, *rest):
     if own:
         attended, low, sums = rest
         sums[...] = jnp.zeros((C, HD), F32)
     else:
         sums_in, attended, low, message, sums = rest
         sums[...] = sums_in[...]
-    off = half_start(own, heads * HD)
-    gains = gain[:, pl.ds(off, heads * HD)]
     lane = lax.broadcasted_iota(jnp.int32, (T_ATT, HD), 1)
     every = range(heads)
 
@@ -184,8 +183,7 @@
                 out = local[rows, head(h)] + dot(q[rows, head(h)], states[h], NN)
                 attended[rows, head(h)] = out
                 square += out * out
-                weighted = g[rows, head(h)].astype(F32) * gains[:, h * HD : (h + 1) * HD]
-                inner += weighted * out
+                inner += weighted[rows, head(h)] * out
             square = jnp.sum(square, axis=1, keepdims=True)
             inner = jnp.sum(inner, axis=1, keepdims=True)
             sums[t : t + T_ATT, :] += jnp.where(lane == n, square, 0.0) + jnp.where(
@@ -201,7 +199,7 @@
 def mixed(own, blocks, heads, lanes, parts, docs, *rest):
     if not own:
         pieces, rest = rest[:parts], rest[parts:]
-        attended, q, g, gain, grad, inside, message, scale, slope, turn = rest
+        attended, q, weighted, grad, inside, message, scale, slope, turn = rest
         total = pieces[0][...]
         for piece in pieces[1:]:
             total = total + piece[...]
@@ -216,9 +214,7 @@
             scale[rows, :] = jnp.broadcast_to(columns[:, n : n + 1], (C, HD))
             slope[rows, :] = jnp.broadcast_to(columns[:, lanes + n : lanes + n + 1], (C, HD))
     else:
-        scale, slope, attended, q, g, gain, grad, inside, message = rest
-    off = half_start(own, heads * HD)
-    gains = gain[:, pl.ds(off, heads * HD)]
+        scale, slope, attended, q, weighted, grad, inside, message = rest
     every = range(heads)
     for h in every:
         inside[state_rows(blocks - 1, h, heads), :] = jnp.zeros((HD, HD), F32)
@@ -229,8 +225,7 @@
             r = scale[part, :]
             s = slope[part, :]
             for h in every:
-                weighted = g[part, head(h)].astype(F32) * gains[:, h * HD : (h + 1) * HD]
-                d = r * weighted - attended[part, head(h)] * s
+                d = r * weighted[part, head(h)] - attended[part, head(h)] * s
                 grad[part, head(h)] = d.astype(BF16)
         sums = [dot(q[rows, head(h)], grad[rows, head(h)], TN) for h in every]
         for h in every:
@@ -333,27 +328,31 @@
         return lax.rem(lax.div(rank, 1 << b), 2)
 
     ins, results = refs[:count], refs[count:]
-    rows = results[0].shape[0] - PAD
-    for terms, result in zip(outs, results):
-        keys = []
-        for source, flag in terms:
-            key = ins[source][rows : rows + 1, :]
-            keys.append(key if flag is None else jnp.where(flag(bit, core), key, NEVER))
-        latest = functools.reduce(jnp.maximum, keys)
-        parts = [
-            jnp.where(key == latest, ins[source][:rows, :], 0.0)
-            for (source, _), key in zip(terms, keys)
-        ]
-        result[:rows, :] = functools.reduce(jnp.add, parts)
-        result[rows:, :] = jnp.broadcast_to(latest, (PAD, HD))
+    for pieces, result in zip(outs, results):
+        at = 0
+        for rows, terms in pieces:
+            keys = []
+            for source, _, flag in terms:
+                end = ins[source].shape[0] - PAD
+                key = ins[source][end : end + 1, :]
+                keys.append(key if flag is None else jnp.where(flag(bit, core), key, NEVER))
+            latest = functools.reduce(jnp.maximum, keys)
+            parts = [
+                jnp.where(key == latest, ins[source][start : start + rows, :], 0.0)
+                for (source, start, _), key in zip(terms, keys)
+            ]
+            result[at : at + rows, :] = functools.reduce(jnp.add, parts)
+            at += rows
+        result[at:, :] = jnp.broadcast_to(latest, (PAD, HD))
 
 
 def merge(ins, outs, reverse, after=()):
     ins = list(ins) + list(after)
+    shapes = [pltpu.VMEM((sum(rows for rows, _ in pieces) + PAD, HD), F32) for pieces in outs]
     return pl.pallas_call(
         functools.partial(merge_kernel, reverse, outs, len(ins)),
         name="merge",
-        out_shape=[pltpu.VMEM(ins[0].shape, F32)] * len(outs),
+        out_shape=shapes,
         in_specs=[VM] * len(ins),
         out_specs=[VM] * len(outs),
         compiler_params=params(),
@@ -367,51 +366,81 @@
     return lax.ppermute(message, "ctx", pairs)
 
 
-def scan(theirs, mine, reverse, first_work, second_work):
+def scan(theirs, mine, reverse, ways, first_work, second_work):
+    rows = mine.shape[0] - PAD
+    part = rows // ways
+    every = range(ways)
     top = lax.axis_size("ctx").bit_length() - 1
     lo, hi = top - 2, top - 1
+
+    def routed(way, flag):
+        return lambda bit, core: flag(bit(lo), bit(hi), core if ways == 1 else way)
+
+    def axes(way):
+        return (lo, hi) if ways == 1 else ((lo, lo), (hi, hi))[way]
+
     beside = swap(theirs, 0, 0)
-    (total,) = merge([mine, beside], [[(0, None), (1, None)]], reverse)
+    totals = merge(
+        [mine, beside],
+        [[(part, [(0, w * part, None), (1, w * part, None)])] for w in every],
+        reverse,
+    )
     before = []
     for b in range(1, lo):
-        got = swap(total, b, b)
+        got = [swap(totals[w], b, b) for w in every]
 
         def is_high(bit, core, b=b):
             return bit(b) == 1
 
-        earlier = [(2, None)] if before else []
-        total, prior = merge(
-            [total, got] + before,
-            [[(0, None), (1, None)], [(1, is_high)] + earlier],
+        earlier = [[(2 * ways + w, 0, None)] if before else [] for w in every]
+        both = merge(
+            list(totals) + got + list(before),
+            [[(part, [(w, 0, None), (ways + w, 0, None)])] for w in every]
+            + [[(part, [(ways + w, 0, is_high)] + earlier[w])] for w in every],
             reverse,
         )
-        before = [prior]
-    first = swap(total, lo, hi)
-    first_done = first_work(total)
-    (onward,) = merge(
-        [total, first],
-        [
+        totals, before = both[:ways], both[ways:]
+    first = [swap(totals[w], *axes(w)) for w in every]
+    first_done = first_work(totals[0])
+    onward = [
+        merge(
+            [totals[w], first[w]],
             [
-                (0, lambda bit, core: core * bit(lo) * bit(hi) == 0),
-                (1, lambda bit, core: core * (1 - bit(hi)) == 0),
-            ]
-        ],
-        reverse,
-        first_done[-1:],
-    )
-    second = swap(onward, hi, lo)
-    second_done = second_work(onward, first_done)
+                [
+                    (
+                        part,
+                        [
+                            (0, 0, routed(w, lambda low, high, r: r * low * high == 0)),
+                            (1, 0, routed(w, lambda low, high, r: r * (1 - high) == 0)),
+                        ],
+                    )
+                ]
+            ],
+            reverse,
+            first_done[-1:],
+        )[0]
+        for w in every
+    ]
+    second = [swap(onward[w], *axes(w)[::-1] if ways == 1 else axes(1 - w)) for w in every]
+    second_done = second_work(onward[-1], first_done)
 
     def carried(neighbour, low_core):
         return [
-            (0, lambda bit, core: (1 - core) * bit(lo) + core * bit(hi) == 1),
-            (1, lambda bit, core: bit(hi) + core * bit(lo) > 0),
-            (neighbour, lambda bit, core: bit(0) == low_core),
-        ] + ([(4, None)] if before else [])
+            (
+                part,
+                [
+                    (w, 0, routed(w, lambda low, high, r: (1 - r) * low + r * high == 1)),
+                    (ways + w, 0, routed(w, lambda low, high, r: high + r * low > 0)),
+                    (neighbour, w * part, lambda bit, core: bit(0) == low_core),
+                ]
+                + ([(2 * ways + 2 + w, 0, None)] if before else []),
+            )
+            for w in every
+        ]
 
     carry_mine, carry_theirs = merge(
-        [first, second, beside, mine] + before,
-        [carried(2, 1), carried(3, 0)],
+        first + second + [beside, mine] + list(before),
+        [carried(2 * ways, 1), carried(2 * ways + 1, 0)],
         reverse,
         second_done[-1:],
     )
@@ -463,16 +492,16 @@
         return pl.pallas_call(
             functools.partial(local_scores, own, blocks, heads),
             name=label("scoring", own),
-            out_shape=[half_bf, half_bf, half_f32, pltpu.VMEM((pairs * C, C), BF16), token],
-            in_specs=[VM] * 3 + [HB] * 2,
+            out_shape=[half_bf, half_f32, half_f32, pltpu.VMEM((pairs * C, C), BF16), token],
+            in_specs=[VM] * 4 + [HB] * 2,
             out_specs=[VM] * 5,
-            scratch_shapes=[dma((blocks,)), dma],
+            scratch_shapes=[half_bf, dma((heads + 1,))],
             compiler_params=params(),
             cost_estimate=cost(4 * pairs * wide, 4 * tokens * cols),
-        )(after, k, v, queries, out_grad)
-
-    def attending(own, inside, carry, q, sv, g, sums):
-        ins = [docs, inside, carry, q, sv, g, gain] + ([] if own else [sums])
+        )(after, k, v, gain, queries, out_grad)
+
+    def attending(own, inside, carry, q, sv, weighted, sums):
+        ins = [docs, inside, carry, q, sv, weighted] + ([] if own else [sums])
         last = [pltpu.VMEM((C, HD), F32)] if own else [pltpu.VMEM((2 * lanes, C), F32)]
         return pl.pallas_call(
             functools.partial(attend, own, blocks, heads, lanes),
@@ -485,8 +514,8 @@
             cost_estimate=cost(2 * pairs * narrow, 1 << 20),
         )(*ins)
 
-    def mixing(own, before, attended, q, g):
-        ins = [docs] + before + [attended, q, g, gain]
+    def mixing(own, before, attended, q, weighted):
+        ins = [docs] + before + [attended, q, weighted]
         outs = [half_bf, states_f32, message] + ([] if own else [column, column])
         return pl.pallas_call(
             functools.partial(mixed, own, blocks, heads, lanes, tp),
@@ -531,24 +560,26 @@
 
     k1, v1, inside1, theirs, docs, k0 = states(False, None)
     v0, inside0, mine = states(True, k0)
-    carry0, carry1, (q1, g1, local1, scores1), (q0, g0, local0, scores0) = scan(
+    carry0, carry1, (q1, w1, local1, scores1), (q0, w0, local0, scores0) = scan(
         theirs,
         mine,
         False,
+        2,
         lambda after: scoring(False, k1, v1, after),
         lambda after, _: scoring(True, k0, v0, after),
     )
-    att0, low0, sums = attending(True, inside0, carry0, q0, local0, g0, None)
-    att1, low1, sums = attending(False, inside1, carry1, q1, local1, g1, sums)
+    att0, low0, sums = attending(True, inside0, carry0, q0, local0, w0, None)
+    att1, low1, sums = attending(False, inside1, carry1, q1, local1, w1, sums)
     parts = [sums] + [
-        lax.ppermute(sums, "tp", [(i, (i + s) % tp) for i in range(tp)]) for s in range(1, tp)
+        lax.ppermute(sums, "tp", [(i, i ^ s) for i in range(tp)]) for s in range(1, tp)
     ]
-    grad1, after1, theirs, scale, slope = mixing(False, parts, att1, q1, g1)
-    grad0, after0, mine = mixing(True, [scale, slope], att0, q0, g0)
+    grad1, after1, theirs, scale, slope = mixing(False, parts, att1, q1, w1)
+    grad0, after0, mine = mixing(True, [scale, slope], att0, q0, w0)
     carry0, carry1, (_, _, kl1, vl1), (normed, query_grad, kl0, vl0) = scan(
         theirs,
         mine,
         True,
+        1,
         lambda after: query_grads(False, k1, v1, q1, att1, scale, grad1, low1, scores1, (), after),
         lambda after, done: query_grads(
             True, k0, v0, q0, att0, scale, grad0, low0, scores0, done[:2], after

time: 53.1 us -> 51.7 us (0.974)
  waiting for transfers between devices: 4.95 us -> 3.36 us
  starting transfers between devices: 15.9 us -> 16.6 us
  Pallas kernels: 31.2 us -> 30.6 us
    ppermute x8 -> x10, starting transfers between devices: 11.6 us -> 12.9 us  [swap(): return lax.ppermute(message, 'ctx', pairs)]
    ppermute x3, waiting for transfers between devices: 4.03 us -> 3.23 us  [local(): lax.ppermute(sums, 'tp', [(i, i ^ s) for i in range(tp)])]
    ppermute x8 -> x10, waiting for transfers between devices: 0.92 us -> 0.13 us  [swap(): return lax.ppermute(message, 'ctx', pairs)]
    ppermute x3, starting transfers between devices: 4.31 us -> 3.72 us  [local(): lax.ppermute(sums, 'tp', [(i, i ^ s) for i in range(tp)])]
    pallas_call x2, Pallas kernels: 7.31 us -> 6.76 us  [scoring(): pl.pallas_call(functools.partial(local_scores, own, blocks, heads), name=...]
  transfers between devices with their start and end apart: 11 -> 13, of which waited for: 5 -> 3; matrix products, arithmetic and copies ran while one was open for 0% -> 0% of each run, Pallas kernels for 44% -> 44%
where the time goes in v4:
time: 51.7 us; the launch traced here: 51.6 us
  Pallas kernels  30.6 us (59%)
  starting transfers between devices  16.6 us (32%)
  waiting for transfers between devices  3.36 us (6%)
  between operations  0.97 us (2%)
    ppermute x10, starting transfers between devices, swap(): return lax.ppermute(message, 'ctx', pairs)  12.9 us
    pallas_call x2, Pallas kernels, query_grads(): pl.pallas_call(functools.partial(query_side, own, blocks, heads), name=la...  9.02 us
    pallas_call x2, Pallas kernels, scoring(): pl.pallas_call(functools.partial(local_scores, own, blocks, heads), name=...  6.76 us
    pallas_call x2, Pallas kernels, states(): pl.pallas_call(functools.partial(key_value_states, own, blocks, heads), n...  4.58 us
    pallas_call x2, Pallas kernels, key_grads(): pl.pallas_call(functools.partial(key_side, own, blocks, heads), name=labe...  4.09 us
    ppermute x3, starting transfers between devices, local(): lax.ppermute(sums, 'tp', [(i, i ^ s) for i in range(tp)])  3.72 us
    ppermute x3, waiting for transfers between devices, local(): lax.ppermute(sums, 'tp', [(i, i ^ s) for i in range(tp)])  3.23 us
    pallas_call x2, Pallas kernels, mixing(): pl.pallas_call(functools.partial(mixed, own, blocks, heads, lanes, tp), n...  2.9 us
  transfers between devices with their start and end apart: 13, of which 3 were waited for; matrix products, arithmetic and copies ran while one was open for 0% of the time, Pallas kernels for 44%

profile of v4, /device:TPU:1, one launch (start us, length us, event | category | flops | bytes accessed | tf_op | source)
XLA Modules:
  0.0 51.6 jit_solution(14970852253115708813)
XLA Ops:
  0.6 2.5 %states_other.1 = (bf16[1536,512]{1,0:T(8,128)(2,1)S(1)}, bf16[1536,512]{1,0:T(8,128)(2,1)S(1)}, f32[3072,128]{1,0:T(8,128)S(1)}, f32[520,128]{1,0:T(8,128)S(1)}...) custom-call(s32[6]{0:T(128)} %refs_1_.3, bf16[1536,1024]{1,0:T(8,128)(2,1)} %refs_1_.2, bf16[1536,1024]{1,0:T(8,128)(2,1)} %refs_2_.3), custom_call_target="tpu_custom_call" | custom-call | flops 201326592 | bytes 3145728 | tf_op jit(solution)/shard_map/states_other/pallas_call | solution.py:480
  3.2 0.0 copy-start
  3.2 0.1 collective-permute-start
  3.3 2.1 %states_own.1 = (bf16[1536,512]{1,0:T(8,128)(2,1)S(1)}, f32[3072,128]{1,0:T(8,128)S(1)}, f32[520,128]{1,0:T(8,128)S(1)}) custom-call(bf16[1536,512]{1,0:T(8,128)(2,1)S(1)} %get-tuple-element.59.refs_0_.k, s32[6]{0:T(128)} %refs_1_.3, bf16[1536,1024]{1,0:T(8,128)(2,1)} %refs_2_.3), custom_call_target="tpu_custom_call" | custom-call | flops 201326592 | bytes 3145728 | tf_op jit(solution)/shard_map/states_own/pallas_call | solution.py:480
  5.4 0.0 collective-permute-done.refs_1_.refs_4_
  5.4 2.7 %collective-permute-start.1 = (f32[264,128]{1,0:T(8,128)S(1)}, f32[264,128]{1,0:T(8,128)S(1)}, u32[]{:S(2)}, u32[]{:S(2)}) collective-permute-start(f32[264,128]{1,0:T(8,128)S(1)} %get-tuple-element.62.after.refs_0_), channel_id=1, source_target_pairs={{0,8},{4,12},{8,0},{12,4},{16,24},{20,28},{24,16},{28,20},{1,9},{5... | collective-permute-start | bytes 405512 | tf_op jit(solution)/shard_map/ppermute | solution.py:366
  8.1 1.2 %collective-permute-start.2 = (f32[264,128]{1,0:T(8,128)S(1)}, f32[264,128]{1,0:T(8,128)S(1)}, u32[]{:S(2)}, u32[]{:S(2)}) collective-permute-start(f32[264,128]{1,0:T(8,128)S(1)} %get-tuple-element.63.refs_0_), channel_id=1, source_target_pairs={{0,16},{4,20},{8,24},{12,28},{16,0},{20,4},{24,8},{28,12},{1,17},{... | collective-permute-start | bytes 405512 | tf_op jit(solution)/shard_map/ppermute | solution.py:366
  9.4 0.0 copy-done
  9.4 3.4 %scoring_other.1 = (bf16[1536,512]{1,0:T(8,128)(2,1)S(1)}, f32[1536,512]{1,0:T(8,128)S(1)}, f32[1536,512]{1,0:T(8,128)S(1)}, bf16[6144,256]{1,0:T(8,128)(2,1)S(1)}, f32[8,128]{1,0:T(8,128)S(1)}) custom-call(f32[264,128]{1,0:T(8,128)S(1)} %get-tuple-element.62.after.refs_0_, bf16[1536,512]{1,0:T(8,128)(2,1)S(1)} %get-tuple-element.64.k, ...), custom_call_target="tpu_custom_call" | custom-call | flops 805306368 | bytes 3145728 | tf_op jit(solution)/shard_map/scoring_other/pallas_call | solution.py:492
  12.8 0.0 collective-permute-done.1.refs_1_.refs_0_
  12.8 0.6 %collective-permute-start.3 = (f32[264,128]{1,0:T(8,128)S(1)}, f32[264,128]{1,0:T(8,128)S(1)}, u32[]{:S(2)}, u32[]{:S(2)}) collective-permute-start(f32[264,128]{1,0:T(8,128)S(1)} %merge.8), channel_id=1, source_target_pairs={{0,16},{4,20},{8,24},{12,28},{16,0},{20,4},{24,8},{28,12},{1,17},{... | collective-permute-start | bytes 405512 | tf_op jit(solution)/shard_map/ppermute | solution.py:366
  13.4 0.0 collective-permute-done.2.refs_1_
  13.5 1.3 %collective-permute-start.4 = (f32[264,128]{1,0:T(8,128)S(1)}, f32[264,128]{1,0:T(8,128)S(1)}, u32[]{:S(2)}, u32[]{:S(2)}) collective-permute-start(f32[264,128]{1,0:T(8,128)S(1)} %merge.9.after), channel_id=1, source_target_pairs={{0,8},{4,12},{8,0},{12,4},{16,24},{20,28},{24,16},{28,20},{1,9},{5... | collective-permute-start | bytes 405512 | tf_op jit(solution)/shard_map/ppermute | solution.py:366
  14.8 3.4 %scoring_own.1 = (bf16[1536,512]{1,0:T(8,128)(2,1)S(1)}, f32[1536,512]{1,0:T(8,128)S(1)}, f32[1536,512]{1,0:T(8,128)S(1)}, bf16[6144,256]{1,0:T(8,128)(2,1)S(1)}, f32[8,128]{1,0:T(8,128)S(1)}) custom-call(f32[264,128]{1,0:T(8,128)S(1)} %merge.9.after, bf16[1536,512]{1,0:T(8,128)(2,1)S(1)} %get-tuple-element.59.refs_0_.k, ...), custom_call_target="tpu_custom_call" | custom-call | flops 805306368 | bytes 3145728 | tf_op jit(solution)/shard_map/scoring_own/pallas_call | solution.py:492
  18.2 0.0 collective-permute-done.3.refs_2_
  18.2 0.0 collective-permute-done.4.refs_3_
  18.2 0.1 merge.10
  18.3 1.5 %collective-permute-start.5 = (f32[520,128]{1,0:T(8,128)S(1)}, f32[520,128]{1,0:T(8,128)S(1)}, u32[]{:S(2)}, u32[]{:S(2)}) collective-permute-start(f32[520,128]{1,0:T(8,128)S(1)} %get-tuple-element.69), channel_id=1, source_target_pairs={{0,4},{4,0},{8,12},{12,8},{16,20},{20,16},{24,28},{28,24},{1,5},{5... | collective-permute-start | bytes 798728 | tf_op jit(solution)/shard_map/ppermute | solution.py:366
  19.9 1.4 %attend_own.1 = (f32[1536,512]{1,0:T(8,128)S(1)}, bf16[3072,128]{1,0:T(8,128)(2,1)S(1)}, f32[256,128]{1,0:T(8,128)S(1)}) custom-call(f32[8,128]{1,0:T(8,128)S(1)} %get-tuple-element.57.docs, f32[3072,128]{1,0:T(8,128)S(1)} %get-tuple-element.73.inside, f32[520,128]{1,0:T(8,128)S(1)} %get-tuple-element.74.carry, ...), custom_call_target="tpu_custom_call" | custom-call | flops 201326592 | bytes 1048576 | tf_op jit(solution)/shard_map/attend_own/pallas_call | solution.py:506
  21.3 0.0 collective-permute-done.5.carry
  21.3 1.3 %attend_other.1 = (f32[1536,512]{1,0:T(8,128)S(1)}, bf16[3072,128]{1,0:T(8,128)(2,1)S(1)}, f32[16,256]{1,0:T(8,128)S(1)}) custom-call(f32[8,128]{1,0:T(8,128)S(1)} %get-tuple-element.57.docs, f32[3072,128]{1,0:T(8,128)S(1)} %get-tuple-element.58.inside, f32[520,128]{1,0:T(8,128)S(1)} %collective-permute-done.5.carry, ...), custom_call_target="tpu_custom_call" | custom-call | flops 201326592 | bytes 1048576 | tf_op jit(solution)/shard_map/attend_other/pallas_call | solution.py:506
  22.7 3.4 %collective-permute-start.8 = (f32[16,256]{1,0:T(8,128)S(1)}, f32[16,256]{1,0:T(8,128)S(1)}, u32[]{:S(2)}, u32[]{:S(2)}) collective-permute-start(f32[16,256]{1,0:T(8,128)S(1)} %get-tuple-element.79.rest_0_), channel_id=1, source_target_pairs={{0,3},{1,2},{2,1},{3,0},{4,7},{5,6},{6,5},{7,4},{8,11},{9,10},{10,... | collective-permute-start | bytes 49160 | tf_op jit(solution)/shard_map/ppermute | solution.py:574
  26.0 0.0 collective-permute-start.7
  26.0 0.3 collective-permute-start.6
  26.4 0.8 %collective-permute-done.8.rest_3_ = f32[16,256]{1,0:T(8,128)S(1)} collective-permute-done((f32[16,256]{1,0:T(8,128)S(1)}, f32[16,256]{1,0:T(8,128)S(1)}, u32[]{:S(2)}, u32[]{:S(2)}) %collective-permute-start.8) | collective-permute-done | bytes 16416 | tf_op jit(solution)/shard_map/ppermute | solution.py:574
  27.1 2.5 %collective-permute-done.7.rest_2_ = f32[16,256]{1,0:T(8,128)S(1)} collective-permute-done((f32[16,256]{1,0:T(8,128)S(1)}, f32[16,256]{1,0:T(8,128)S(1)}, u32[]{:S(2)}, u32[]{:S(2)}) %collective-permute-start.7) | collective-permute-done | bytes 16416 | tf_op jit(solution)/shard_map/ppermute | solution.py:574
  29.6 0.0 collective-permute-done.6.rest_1_
  29.6 1.4 %mixed_other.1 = (bf16[1536,512]{1,0:T(8,128)(2,1)S(1)}, f32[3072,128]{1,0:T(8,128)S(1)}, f32[520,128]{1,0:T(8,128)S(1)}, f32[1536,128]{1,0:T(8,128)S(1)}, f32[1536,128]{1,0:T(8,128)S(1)}) custom-call(f32[8,128]{1,0:T(8,128)S(1)} %get-tuple-element.57.docs, f32[16,256]{1,0:T(8,128)S(1)} %get-tuple-element.79.rest_0_, ...), custom_call_target="tpu_custom_call" | custom-call | flops 201326592 | bytes 1048576 | tf_op jit(solution)/shard_map/mixed_other/pallas_call | solution.py:520
  31.0 1.5 %collective-permute-start.9 = (f32[520,128]{1,0:T(8,128)S(1)}, f32[520,128]{1,0:T(8,128)S(1)}, u32[]{:S(2)}, u32[]{:S(2)}) collective-permute-start(f32[520,128]{1,0:T(8,128)S(1)} %get-tuple-element.85), channel_id=1, source_target_pairs={{0,4},{4,0},{8,12},{12,8},{16,20},{20,16},{24,28},{28,24},{1,5},{5... | collective-permute-start | bytes 798728 | tf_op jit(solution)/shard_map/ppermute | solution.py:366
  32.5 1.5 %mixed_own.1 = (bf16[1536,512]{1,0:T(8,128)(2,1)S(1)}, f32[3072,128]{1,0:T(8,128)S(1)}, f32[520,128]{1,0:T(8,128)S(1)}) custom-call(f32[8,128]{1,0:T(8,128)S(1)} %get-tuple-element.57.docs, f32[1536,128]{1,0:T(8,128)S(1)} %get-tuple-element.81.rest_0_.scale, f32[1536,128]{1,0:T(8,128)S(1)} %get-tuple-element.82.rest_1_, ...), custom_call_target="tpu_custom_call" | custom-call | flops 201326592 | bytes 1048576 | tf_op jit(solution)/shard_map/mixed_own/pallas_call | solution.py:520
  34.0 0.0 collective-permute-done.9.refs_1_.refs_2_
  34.0 0.9 %collective-permute-start.10 = (f32[520,128]{1,0:T(8,128)S(1)}, f32[520,128]{1,0:T(8,128)S(1)}, u32[]{:S(2)}, u32[]{:S(2)}) collective-permute-start(f32[520,128]{1,0:T(8,128)S(1)} %merge.11.after.refs_0_), channel_id=1, source_target_pairs={{0,8},{4,20},{8,0},{12,28},{16,24},{20,4},{24,16},{28,12},{1,9},{5... | collective-permute-start | bytes 798728 | tf_op jit(solution)/shard_map/ppermute | solution.py:366
  34.9 4.6 %query_side_other.1 = (bf16[1536,1024]{1,0:T(8,128)(2,1)}, bf16[1536,1024]{1,0:T(8,128)(2,1)}, f32[1536,512]{1,0:T(8,128)S(1)}, f32[1536,512]{1,0:T(8,128)S(1)}, f32[8,128]{1,0:T(8,128)S(1)}) custom-call(f32[520,128]{1,0:T(8,128)S(1)} %merge.11.after.refs_0_, bf16[1536,512]{1,0:T(8,128)(2,1)S(1)} %get-tuple-element.64.k, ...), custom_call_target="tpu_custom_call" | custom-call | flops 1610612736 | bytes 3145728 | tf_op jit(solution)/shard_map/query_side_other/pallas_call | solution.py:534
  39.6 0.1 collective-permute-done.10.refs_1_.refs_0_
  39.7 1.3 %collective-permute-start.11 = (f32[520,128]{1,0:T(8,128)S(1)}, f32[520,128]{1,0:T(8,128)S(1)}, u32[]{:S(2)}, u32[]{:S(2)}) collective-permute-start(f32[520,128]{1,0:T(8,128)S(1)} %merge.12.after), channel_id=1, source_target_pairs={{0,16},{4,12},{8,24},{12,4},{16,0},{20,28},{24,8},{28,20},{1,17},{... | collective-permute-start | bytes 798728 | tf_op jit(solution)/shard_map/ppermute | solution.py:366
  41.0 4.4 %query_side_own.1 = (bf16[1536,1024]{1,0:T(8,128)(2,1)}, bf16[1536,1024]{1,0:T(8,128)(2,1)}, f32[1536,512]{1,0:T(8,128)S(1)}, f32[1536,512]{1,0:T(8,128)S(1)}, f32[8,128]{1,0:T(8,128)S(1)}) custom-call(f32[520,128]{1,0:T(8,128)S(1)} %merge.12.after, ...), custom_call_target="tpu_custom_call", output_to_operand_aliasing={{0}: (10, {}), {1}: (11, {})} | custom-call | flops 1610612736 | bytes 3145728 | tf_op jit(solution)/shard_map/query_side_own/pallas_call | solution.py:534
  45.4 0.0 collective-permute-done.11.refs_1_
  45.4 0.1 merge.13
  45.6 1.7 %collective-permute-start.12 = (f32[520,128]{1,0:T(8,128)S(1)}, f32[520,128]{1,0:T(8,128)S(1)}, u32[]{:S(2)}, u32[]{:S(2)}) collective-permute-start(f32[520,128]{1,0:T(8,128)S(1)} %get-tuple-element.99), channel_id=1, source_target_pairs={{0,4},{4,0},{8,12},{12,8},{16,20},{20,16},{24,28},{28,24},{1,5},{5... | collective-permute-start | bytes 798728 | tf_op jit(solution)/shard_map/ppermute | solution.py:366
  47.3 2.0 %key_side_own.1 = (bf16[1536,1024]{1,0:T(8,128)(2,1)}, bf16[1536,1024]{1,0:T(8,128)(2,1)}) custom-call(f32[8,128]{1,0:T(8,128)S(1)} %get-tuple-element.57.docs, f32[3072,128]{1,0:T(8,128)S(1)} %get-tuple-element.102.inside, f32[520,128]{1,0:T(8,128)S(1)} %get-tuple-element.103.carry, bf16[1536,512]{1,0:T(8,128)(2,1)S(1)} %get-tuple-element.59.refs_0_.k, ...), custom_call_target="tpu_custom_call" | custom-call | flops 402653184 | bytes 3145728 | tf_op jit(solution)/shard_map/key_side_own/pallas_call | solution.py:549
  49.3 0.0 collective-permute-done.12.carry
  49.3 2.1 %key_side_other.1 = (bf16[1536,1024]{1,0:T(8,128)(2,1)}, bf16[1536,1024]{1,0:T(8,128)(2,1)}) custom-call(f32[8,128]{1,0:T(8,128)S(1)} %get-tuple-element.57.docs, f32[3072,128]{1,0:T(8,128)S(1)} %get-tuple-element.97.inside, f32[520,128]{1,0:T(8,128)S(1)} %collective-permute-done.12.carry, ...), custom_call_target="tpu_custom_call", output_to_operand_aliasing={{0}: (7, {}), {1}: (8, {})} | custom-call | flops 402653184 | bytes 3145728 | tf_op jit(solution)/shard_map/key_side_other/pallas_call | solution.py:549
  (5 shorter events, 0.2 us)
Async XLA Ops:
  3.2 6.2 %copy-start = (f32[1024]{0:T(1024)S(1)}, f32[1024]{0:T(1024)}, u32[]{:S(2)}) copy-start(f32[1024]{0:T(1024)} %param.10) | copy-start | bytes 12292
  3.2 2.2 %collective-permute-start = (f32[520,128]{1,0:T(8,128)S(1)}, f32[520,128]{1,0:T(8,128)S(1)}, u32[]{:S(2)}, u32[]{:S(2)}) collective-permute-start(f32[520,128]{1,0:T(8,128)S(1)} %get-tuple-element.61), channel_id=1, source_target_pairs={{0,4},{4,0},{8,12},{12,8},{16,20},{20,16},{24,28},{28,24},{1,5},{5... | collective-permute-start | bytes 798728 | tf_op jit(solution)/shard_map/ppermute | solution.py:366
  5.4 7.4 %collective-permute-start.1 = (f32[264,128]{1,0:T(8,128)S(1)}, f32[264,128]{1,0:T(8,128)S(1)}, u32[]{:S(2)}, u32[]{:S(2)}) collective-permute-start(f32[264,128]{1,0:T(8,128)S(1)} %get-tuple-element.62.after.refs_0_), channel_id=1, source_target_pairs={{0,8},{4,12},{8,0},{12,4},{16,24},{20,28},{24,16},{28,20},{1,9},{5... | collective-permute-start | bytes 405512 | tf_op jit(solution)/shard_map/ppermute | solution.py:366
  8.1 5.3 %collective-permute-start.2 = (f32[264,128]{1,0:T(8,128)S(1)}, f32[264,128]{1,0:T(8,128)S(1)}, u32[]{:S(2)}, u32[]{:S(2)}) collective-permute-start(f32[264,128]{1,0:T(8,128)S(1)} %get-tuple-element.63.refs_0_), channel_id=1, source_target_pairs={{0,16},{4,20},{8,24},{12,28},{16,0},{20,4},{24,8},{28,12},{1,17},{... | collective-permute-start | bytes 405512 | tf_op jit(solution)/shard_map/ppermute | solution.py:366
  12.8 5.3 %collective-permute-start.3 = (f32[264,128]{1,0:T(8,128)S(1)}, f32[264,128]{1,0:T(8,128)S(1)}, u32[]{:S(2)}, u32[]{:S(2)}) collective-permute-start(f32[264,128]{1,0:T(8,128)S(1)} %merge.8), channel_id=1, source_target_pairs={{0,16},{4,20},{8,24},{12,28},{16,0},{20,4},{24,8},{28,12},{1,17},{... | collective-permute-start | bytes 405512 | tf_op jit(solution)/shard_map/ppermute | solution.py:366
  13.5 4.7 %collective-permute-start.4 = (f32[264,128]{1,0:T(8,128)S(1)}, f32[264,128]{1,0:T(8,128)S(1)}, u32[]{:S(2)}, u32[]{:S(2)}) collective-permute-start(f32[264,128]{1,0:T(8,128)S(1)} %merge.9.after), channel_id=1, source_target_pairs={{0,8},{4,12},{8,0},{12,4},{16,24},{20,28},{24,16},{28,20},{1,9},{5... | collective-permute-start | bytes 405512 | tf_op jit(solution)/shard_map/ppermute | solution.py:366
  18.3 3.0 %collective-permute-start.5 = (f32[520,128]{1,0:T(8,128)S(1)}, f32[520,128]{1,0:T(8,128)S(1)}, u32[]{:S(2)}, u32[]{:S(2)}) collective-permute-start(f32[520,128]{1,0:T(8,128)S(1)} %get-tuple-element.69), channel_id=1, source_target_pairs={{0,4},{4,0},{8,12},{12,8},{16,20},{20,16},{24,28},{28,24},{1,5},{5... | collective-permute-start | bytes 798728 | tf_op jit(solution)/shard_map/ppermute | solution.py:366
  22.7 4.5 %collective-permute-start.8 = (f32[16,256]{1,0:T(8,128)S(1)}, f32[16,256]{1,0:T(8,128)S(1)}, u32[]{:S(2)}, u32[]{:S(2)}) collective-permute-start(f32[16,256]{1,0:T(8,128)S(1)} %get-tuple-element.79.rest_0_), channel_id=1, source_target_pairs={{0,3},{1,2},{2,1},{3,0},{4,7},{5,6},{6,5},{7,4},{8,11},{9,10},{10,... | collective-permute-start | bytes 49160 | tf_op jit(solution)/shard_map/ppermute | solution.py:574
  26.0 3.6 %collective-permute-start.7 = (f32[16,256]{1,0:T(8,128)S(1)}, f32[16,256]{1,0:T(8,128)S(1)}, u32[]{:S(2)}, u32[]{:S(2)}) collective-permute-start(f32[16,256]{1,0:T(8,128)S(1)} %get-tuple-element.79.rest_0_), channel_id=1, source_target_pairs={{0,2},{1,3},{2,0},{3,1},{4,6},{5,7},{6,4},{7,5},{8,10},{9,11},{10,... | collective-permute-start | bytes 49160 | tf_op jit(solution)/shard_map/ppermute | solution.py:574
  26.0 3.6 %collective-permute-start.6 = (f32[16,256]{1,0:T(8,128)S(1)}, f32[16,256]{1,0:T(8,128)S(1)}, u32[]{:S(2)}, u32[]{:S(2)}) collective-permute-start(f32[16,256]{1,0:T(8,128)S(1)} %get-tuple-element.79.rest_0_), channel_id=1, source_target_pairs={{0,1},{1,0},{2,3},{3,2},{4,5},{5,4},{6,7},{7,6},{8,9},{9,8},{10,11... | collective-permute-start | bytes 49160 | tf_op jit(solution)/shard_map/ppermute | solution.py:574
  31.0 3.0 %collective-permute-start.9 = (f32[520,128]{1,0:T(8,128)S(1)}, f32[520,128]{1,0:T(8,128)S(1)}, u32[]{:S(2)}, u32[]{:S(2)}) collective-permute-start(f32[520,128]{1,0:T(8,128)S(1)} %get-tuple-element.85), channel_id=1, source_target_pairs={{0,4},{4,0},{8,12},{12,8},{16,20},{20,16},{24,28},{28,24},{1,5},{5... | collective-permute-start | bytes 798728 | tf_op jit(solution)/shard_map/ppermute | solution.py:366
  34.0 5.6 %collective-permute-start.10 = (f32[520,128]{1,0:T(8,128)S(1)}, f32[520,128]{1,0:T(8,128)S(1)}, u32[]{:S(2)}, u32[]{:S(2)}) collective-permute-start(f32[520,128]{1,0:T(8,128)S(1)} %merge.11.after.refs_0_), channel_id=1, source_target_pairs={{0,8},{4,20},{8,0},{12,28},{16,24},{20,4},{24,16},{28,12},{1,9},{5... | collective-permute-start | bytes 798728 | tf_op jit(solution)/shard_map/ppermute | solution.py:366
  39.7 5.7 %collective-permute-start.11 = (f32[520,128]{1,0:T(8,128)S(1)}, f32[520,128]{1,0:T(8,128)S(1)}, u32[]{:S(2)}, u32[]{:S(2)}) collective-permute-start(f32[520,128]{1,0:T(8,128)S(1)} %merge.12.after), channel_id=1, source_target_pairs={{0,16},{4,12},{8,24},{12,4},{16,0},{20,28},{24,8},{28,20},{1,17},{... | collective-permute-start | bytes 798728 | tf_op jit(solution)/shard_map/ppermute | solution.py:366
  45.6 3.8 %collective-permute-start.12 = (f32[520,128]{1,0:T(8,128)S(1)}, f32[520,128]{1,0:T(8,128)S(1)}, u32[]{:S(2)}, u32[]{:S(2)}) collective-permute-start(f32[520,128]{1,0:T(8,128)S(1)} %get-tuple-element.99), channel_id=1, source_target_pairs={{0,4},{4,0},{8,12},{12,8},{16,20},{20,16},{24,28},{28,24},{1,5},{5... | collective-permute-start | bytes 798728 | tf_op jit(solution)/shard_map/ppermute | solution.py:366

commit v5 on v4

--- a/solution.py
+++ b/solution.py
@@ -17,7 +17,7 @@
 U_ATT = 6
 U_Q = 6
 U_K = 6
-T_ATT = 128
+T_ATT = 64
 T_MIX = 128
 
 epsilon = 1e-06
@@ -70,17 +70,17 @@
 
 def key_value_states(own, blocks, heads, *refs):
     if own:
-        k, docs_hbm, v_hbm, v, inside, message, docs, sems = refs
+        k, _, docs_hbm, v_hbm, v, inside, message, docs, sems = refs
     else:
-        docs_hbm, k_hbm, v_hbm, k, v, inside, message, table, k_own, docs, sems = refs
+        docs_hbm, k_hbm, v_hbm, k, v, inside, message, table, k_own, v_own, docs, sems = refs
     off = half_start(own, heads * HD)
     docs_copy = pltpu.make_async_copy(docs_hbm, docs, sems.at[2 * heads])
     width = 2 * HD if heads % 2 == 0 else HD
     groups = heads * HD // width
-    copies = []
-    for i in range(groups):
+    copies = [[] for _ in range(groups)]
+    for i in range(1 if own else 0, groups):
         src, dst = pl.ds(off + i * width, width), pl.ds(i * width, width)
-        copies.append([pltpu.make_async_copy(v_hbm.at[:, src], v.at[:, dst], sems.at[2 * i])])
+        copies[i].append(pltpu.make_async_copy(v_hbm.at[:, src], v.at[:, dst], sems.at[2 * i]))
         if not own:
             copies[i].append(
                 pltpu.make_async_copy(k_hbm.at[:, src], k.at[:, dst], sems.at[2 * i + 1])
@@ -88,13 +88,19 @@
         for copy in copies[i]:
             copy.start()
     docs_copy.start()
+    ahead = []
     if not own:
-        ahead = pltpu.make_async_copy(
-            k_hbm.at[:, pl.ds(half_start(True, heads * HD), heads * HD)],
-            k_own,
-            sems.at[2 * heads + 1],
-        )
-        ahead.start()
+        start = half_start(True, heads * HD)
+        ahead = [
+            pltpu.make_async_copy(
+                k_hbm.at[:, pl.ds(start, heads * HD)], k_own, sems.at[2 * heads + 1]
+            ),
+            pltpu.make_async_copy(
+                v_hbm.at[:, pl.ds(start, width)], v_own.at[:, :width], sems.at[2 * heads + 2]
+            ),
+        ]
+        for copy in ahead:
+            copy.start()
     docs_copy.wait()
     for h in range(heads):
         if h * HD % width == 0:
@@ -115,7 +121,8 @@
         table[...] = jnp.zeros(table.shape, F32)
         for n in range(blocks):
             table[n : n + 1, :] = jnp.full((1, HD), docs[n].astype(F32), F32)
-        ahead.wait()
+        for copy in ahead:
+            copy.wait()
 
 
 def causal_mask():
@@ -472,18 +479,19 @@
     ]
     token = pltpu.VMEM((PAD, HD), F32)
 
-    def states(own, k):
-        ins = [k, docs_hbm, values] if own else [docs_hbm, keys, values]
+    def states(own, ahead):
+        ins = ahead + ([docs_hbm, values] if own else [docs_hbm, keys, values])
         outs = [half_bf, states_f32, message]
         if not own:
-            outs = [half_bf] + outs + [pltpu.VMEM((lanes, HD), F32), half_bf]
+            outs = [half_bf] + outs + [pltpu.VMEM((lanes, HD), F32), half_bf, half_bf]
         return pl.pallas_call(
             functools.partial(key_value_states, own, blocks, heads),
             name=label("states", own),
             out_shape=outs,
-            in_specs=[VM, HB, HB] if own else [HB, HB, HB],
+            in_specs=[VM] * len(ahead) + [HB] * (len(ins) - len(ahead)),
             out_specs=[VM] * len(outs),
-            scratch_shapes=[pltpu.SMEM((blocks,), jnp.int32), dma((2 * heads + 2,))],
+            scratch_shapes=[pltpu.SMEM((blocks,), jnp.int32), dma((2 * heads + 3,))],
+            input_output_aliases={1: 0} if own else {},
             compiler_params=params(),
             cost_estimate=cost(2 * pairs * narrow, 4 * tokens * cols),
         )(*ins)
@@ -558,8 +566,8 @@
             cost_estimate=cost(4 * pairs * narrow, 4 * tokens * cols),
         )(*ins)
 
-    k1, v1, inside1, theirs, docs, k0 = states(False, None)
-    v0, inside0, mine = states(True, k0)
+    k1, v1, inside1, theirs, docs, k0, v0 = states(False, [])
+    v0, inside0, mine = states(True, [k0, v0])
     carry0, carry1, (q1, w1, local1, scores1), (q0, w0, local0, scores0) = scan(
         theirs,
         mine,

time: 51.7 us -> 51.5 us (level)
  transfers between devices with their start and end apart: 13 -> 13, of which waited for: 3 -> 3; matrix products, arithmetic and copies ran while one was open for 0% -> 0% of each run, Pallas kernels for 44% -> 43%
where the time goes in v5:
time: 51.5 us; the launch traced here: 51.4 us
  Pallas kernels  30.2 us (59%)
  starting transfers between devices  16.7 us (32%)
  waiting for transfers between devices  3.53 us (7%)
  between operations  0.97 us (2%)
    ppermute x10, starting transfers between devices, swap(): return lax.ppermute(message, 'ctx', pairs)  12.9 us
    pallas_call x2, Pallas kernels, query_grads(): pl.pallas_call(functools.partial(query_side, own, blocks, heads), name=la...  9.02 us
    pallas_call x2, Pallas kernels, scoring(): pl.pallas_call(functools.partial(local_scores, own, blocks, heads), name=...  6.76 us
    pallas_call x2, Pallas kernels, states(): pl.pallas_call(functools.partial(key_value_states, own, blocks, heads), n...  4.45 us
    pallas_call x2, Pallas kernels, key_grads(): pl.pallas_call(functools.partial(key_side, own, blocks, heads), name=labe...  4.09 us
    ppermute x3, starting transfers between devices, local(): lax.ppermute(sums, 'tp', [(i, i ^ s) for i in range(tp)])  3.72 us
    ppermute x3, waiting for transfers between devices, local(): lax.ppermute(sums, 'tp', [(i, i ^ s) for i in range(tp)])  3.39 us
    pallas_call x2, Pallas kernels, mixing(): pl.pallas_call(functools.partial(mixed, own, blocks, heads, lanes, tp), n...  2.9 us
  transfers between devices with their start and end apart: 13, of which 3 were waited for; matrix products, arithmetic and copies ran while one was open for 0% of the time, Pallas kernels for 43%

profile of v5, /device:TPU:1, one launch (start us, length us, event | category | flops | bytes accessed | tf_op | source)
XLA Modules:
  0.0 51.4 jit_solution(12191400653883134985)
XLA Ops:
  0.6 2.7 %states_other.1 = (bf16[1536,512]{1,0:T(8,128)(2,1)S(1)}, bf16[1536,512]{1,0:T(8,128)(2,1)S(1)}, f32[3072,128]{1,0:T(8,128)S(1)}, f32[520,128]{1,0:T(8,128)S(1)}...) custom-call(s32[6]{0:T(128)} %refs_2_.3, bf16[1536,1024]{1,0:T(8,128)(2,1)} %refs_1_.1, ...), custom_call_target="tpu_custom_call" | custom-call | flops 201326592 | bytes 3145728 | tf_op jit(solution)/shard_map/states_other/pallas_call | solution.py:487
  3.4 0.1 collective-permute-start
  3.5 0.0 copy-start
  3.5 1.7 %states_own.1 = (bf16[1536,512]{1,0:T(8,128)(2,1)S(1)}, f32[3072,128]{1,0:T(8,128)S(1)}, f32[520,128]{1,0:T(8,128)S(1)}) custom-call(bf16[1536,512]{1,0:T(8,128)(2,1)S(1)} %get-tuple-element.60.refs_0_.k, bf16[1536,512]{1,0:T(8,128)(2,1)S(1)} %get-tuple-element.61.refs_1_, s32[6]{0:T(128)} %refs_2_.3, ...), custom_call_target="tpu_custom_call", output_to_operand_aliasing={{0}: (1, {})} | custom-call | flops 201326592 | bytes 3145728 | tf_op jit(solution)/shard_map/states_own/pallas_call | solution.py:487
  5.2 0.0 collective-permute-done.refs_1_.refs_4_
  5.3 2.7 %collective-permute-start.1 = (f32[264,128]{1,0:T(8,128)S(1)}, f32[264,128]{1,0:T(8,128)S(1)}, u32[]{:S(2)}, u32[]{:S(2)}) collective-permute-start(f32[264,128]{1,0:T(8,128)S(1)} %get-tuple-element.64.after.refs_0_), channel_id=1, source_target_pairs={{0,8},{4,12},{8,0},{12,4},{16,24},{20,28},{24,16},{28,20},{1,9},{5... | collective-permute-start | bytes 405512 | tf_op jit(solution)/shard_map/ppermute | solution.py:373
  8.0 1.2 %collective-permute-start.2 = (f32[264,128]{1,0:T(8,128)S(1)}, f32[264,128]{1,0:T(8,128)S(1)}, u32[]{:S(2)}, u32[]{:S(2)}) collective-permute-start(f32[264,128]{1,0:T(8,128)S(1)} %get-tuple-element.65.refs_0_), channel_id=1, source_target_pairs={{0,16},{4,20},{8,24},{12,28},{16,0},{20,4},{24,8},{28,12},{1,17},{... | collective-permute-start | bytes 405512 | tf_op jit(solution)/shard_map/ppermute | solution.py:373
  9.2 0.0 copy-done
  9.2 3.4 %scoring_other.1 = (bf16[1536,512]{1,0:T(8,128)(2,1)S(1)}, f32[1536,512]{1,0:T(8,128)S(1)}, f32[1536,512]{1,0:T(8,128)S(1)}, bf16[6144,256]{1,0:T(8,128)(2,1)S(1)}, f32[8,128]{1,0:T(8,128)S(1)}) custom-call(f32[264,128]{1,0:T(8,128)S(1)} %get-tuple-element.64.after.refs_0_, bf16[1536,512]{1,0:T(8,128)(2,1)S(1)} %get-tuple-element.66.k, ...), custom_call_target="tpu_custom_call" | custom-call | flops 805306368 | bytes 3145728 | tf_op jit(solution)/shard_map/scoring_other/pallas_call | solution.py:500
  12.6 0.0 collective-permute-done.1.refs_1_.refs_0_
  12.7 0.6 %collective-permute-start.3 = (f32[264,128]{1,0:T(8,128)S(1)}, f32[264,128]{1,0:T(8,128)S(1)}, u32[]{:S(2)}, u32[]{:S(2)}) collective-permute-start(f32[264,128]{1,0:T(8,128)S(1)} %merge.8), channel_id=1, source_target_pairs={{0,16},{4,20},{8,24},{12,28},{16,0},{20,4},{24,8},{28,12},{1,17},{... | collective-permute-start | bytes 405512 | tf_op jit(solution)/shard_map/ppermute | solution.py:373
  13.3 0.0 collective-permute-done.2.refs_1_
  13.3 1.3 %collective-permute-start.4 = (f32[264,128]{1,0:T(8,128)S(1)}, f32[264,128]{1,0:T(8,128)S(1)}, u32[]{:S(2)}, u32[]{:S(2)}) collective-permute-start(f32[264,128]{1,0:T(8,128)S(1)} %merge.9.after), channel_id=1, source_target_pairs={{0,8},{4,12},{8,0},{12,4},{16,24},{20,28},{24,16},{28,20},{1,9},{5... | collective-permute-start | bytes 405512 | tf_op jit(solution)/shard_map/ppermute | solution.py:373
  14.6 3.4 %scoring_own.1 = (bf16[1536,512]{1,0:T(8,128)(2,1)S(1)}, f32[1536,512]{1,0:T(8,128)S(1)}, f32[1536,512]{1,0:T(8,128)S(1)}, bf16[6144,256]{1,0:T(8,128)(2,1)S(1)}, f32[8,128]{1,0:T(8,128)S(1)}) custom-call(f32[264,128]{1,0:T(8,128)S(1)} %merge.9.after, bf16[1536,512]{1,0:T(8,128)(2,1)S(1)} %get-tuple-element.60.refs_0_.k, ...), custom_call_target="tpu_custom_call" | custom-call | flops 805306368 | bytes 3145728 | tf_op jit(solution)/shard_map/scoring_own/pallas_call | solution.py:500
  18.0 0.0 collective-permute-done.3.refs_2_
  18.0 0.0 collective-permute-done.4.refs_3_
  18.0 0.1 merge.10
  18.2 1.6 %collective-permute-start.5 = (f32[520,128]{1,0:T(8,128)S(1)}, f32[520,128]{1,0:T(8,128)S(1)}, u32[]{:S(2)}, u32[]{:S(2)}) collective-permute-start(f32[520,128]{1,0:T(8,128)S(1)} %get-tuple-element.71), channel_id=1, source_target_pairs={{0,4},{4,0},{8,12},{12,8},{16,20},{20,16},{24,28},{28,24},{1,5},{5... | collective-permute-start | bytes 798728 | tf_op jit(solution)/shard_map/ppermute | solution.py:373
  19.7 1.3 %attend_own.1 = (f32[1536,512]{1,0:T(8,128)S(1)}, bf16[3072,128]{1,0:T(8,128)(2,1)S(1)}, f32[256,128]{1,0:T(8,128)S(1)}) custom-call(f32[8,128]{1,0:T(8,128)S(1)} %get-tuple-element.58.docs, f32[3072,128]{1,0:T(8,128)S(1)} %get-tuple-element.75.inside, f32[520,128]{1,0:T(8,128)S(1)} %get-tuple-element.76.carry, ...), custom_call_target="tpu_custom_call" | custom-call | flops 201326592 | bytes 1048576 | tf_op jit(solution)/shard_map/attend_own/pallas_call | solution.py:514
  21.0 0.0 collective-permute-done.5.carry
  21.0 1.3 %attend_other.1 = (f32[1536,512]{1,0:T(8,128)S(1)}, bf16[3072,128]{1,0:T(8,128)(2,1)S(1)}, f32[16,256]{1,0:T(8,128)S(1)}) custom-call(f32[8,128]{1,0:T(8,128)S(1)} %get-tuple-element.58.docs, f32[3072,128]{1,0:T(8,128)S(1)} %get-tuple-element.59.inside, f32[520,128]{1,0:T(8,128)S(1)} %collective-permute-done.5.carry, ...), custom_call_target="tpu_custom_call" | custom-call | flops 201326592 | bytes 1048576 | tf_op jit(solution)/shard_map/attend_other/pallas_call | solution.py:514
  22.3 3.4 %collective-permute-start.8 = (f32[16,256]{1,0:T(8,128)S(1)}, f32[16,256]{1,0:T(8,128)S(1)}, u32[]{:S(2)}, u32[]{:S(2)}) collective-permute-start(f32[16,256]{1,0:T(8,128)S(1)} %get-tuple-element.81.rest_0_), channel_id=1, source_target_pairs={{0,3},{1,2},{2,1},{3,0},{4,7},{5,6},{6,5},{7,4},{8,11},{9,10},{10,... | collective-permute-start | bytes 49160 | tf_op jit(solution)/shard_map/ppermute | solution.py:582
  25.6 0.0 collective-permute-start.7
  25.6 0.4 collective-permute-start.6
  26.0 0.8 %collective-permute-done.8.rest_3_ = f32[16,256]{1,0:T(8,128)S(1)} collective-permute-done((f32[16,256]{1,0:T(8,128)S(1)}, f32[16,256]{1,0:T(8,128)S(1)}, u32[]{:S(2)}, u32[]{:S(2)}) %collective-permute-start.8) | collective-permute-done | bytes 16416 | tf_op jit(solution)/shard_map/ppermute | solution.py:582
  26.8 2.6 %collective-permute-done.7.rest_2_ = f32[16,256]{1,0:T(8,128)S(1)} collective-permute-done((f32[16,256]{1,0:T(8,128)S(1)}, f32[16,256]{1,0:T(8,128)S(1)}, u32[]{:S(2)}, u32[]{:S(2)}) %collective-permute-start.7) | collective-permute-done | bytes 16416 | tf_op jit(solution)/shard_map/ppermute | solution.py:582
  29.4 0.0 collective-permute-done.6.rest_1_
  29.4 1.4 %mixed_other.1 = (bf16[1536,512]{1,0:T(8,128)(2,1)S(1)}, f32[3072,128]{1,0:T(8,128)S(1)}, f32[520,128]{1,0:T(8,128)S(1)}, f32[1536,128]{1,0:T(8,128)S(1)}, f32[1536,128]{1,0:T(8,128)S(1)}) custom-call(f32[8,128]{1,0:T(8,128)S(1)} %get-tuple-element.58.docs, f32[16,256]{1,0:T(8,128)S(1)} %get-tuple-element.81.rest_0_, ...), custom_call_target="tpu_custom_call" | custom-call | flops 201326592 | bytes 1048576 | tf_op jit(solution)/shard_map/mixed_other/pallas_call | solution.py:528
  30.8 1.5 %collective-permute-start.9 = (f32[520,128]{1,0:T(8,128)S(1)}, f32[520,128]{1,0:T(8,128)S(1)}, u32[]{:S(2)}, u32[]{:S(2)}) collective-permute-start(f32[520,128]{1,0:T(8,128)S(1)} %get-tuple-element.87), channel_id=1, source_target_pairs={{0,4},{4,0},{8,12},{12,8},{16,20},{20,16},{24,28},{28,24},{1,5},{5... | collective-permute-start | bytes 798728 | tf_op jit(solution)/shard_map/ppermute | solution.py:373
  32.3 1.5 %mixed_own.1 = (bf16[1536,512]{1,0:T(8,128)(2,1)S(1)}, f32[3072,128]{1,0:T(8,128)S(1)}, f32[520,128]{1,0:T(8,128)S(1)}) custom-call(f32[8,128]{1,0:T(8,128)S(1)} %get-tuple-element.58.docs, f32[1536,128]{1,0:T(8,128)S(1)} %get-tuple-element.83.rest_0_.scale, f32[1536,128]{1,0:T(8,128)S(1)} %get-tuple-element.84.rest_1_, ...), custom_call_target="tpu_custom_call" | custom-call | flops 201326592 | bytes 1048576 | tf_op jit(solution)/shard_map/mixed_own/pallas_call | solution.py:528
  33.8 0.0 collective-permute-done.9.refs_1_.refs_2_
  33.8 0.9 %collective-permute-start.10 = (f32[520,128]{1,0:T(8,128)S(1)}, f32[520,128]{1,0:T(8,128)S(1)}, u32[]{:S(2)}, u32[]{:S(2)}) collective-permute-start(f32[520,128]{1,0:T(8,128)S(1)} %merge.11.after.refs_0_), channel_id=1, source_target_pairs={{0,8},{4,20},{8,0},{12,28},{16,24},{20,4},{24,16},{28,12},{1,9},{5... | collective-permute-start | bytes 798728 | tf_op jit(solution)/shard_map/ppermute | solution.py:373
  34.7 4.6 %query_side_other.1 = (bf16[1536,1024]{1,0:T(8,128)(2,1)}, bf16[1536,1024]{1,0:T(8,128)(2,1)}, f32[1536,512]{1,0:T(8,128)S(1)}, f32[1536,512]{1,0:T(8,128)S(1)}, f32[8,128]{1,0:T(8,128)S(1)}) custom-call(f32[520,128]{1,0:T(8,128)S(1)} %merge.11.after.refs_0_, bf16[1536,512]{1,0:T(8,128)(2,1)S(1)} %get-tuple-element.66.k, ...), custom_call_target="tpu_custom_call" | custom-call | flops 1610612736 | bytes 3145728 | tf_op jit(solution)/shard_map/query_side_other/pallas_call | solution.py:542
  39.4 0.1 collective-permute-done.10.refs_1_.refs_0_
  39.5 1.3 %collective-permute-start.11 = (f32[520,128]{1,0:T(8,128)S(1)}, f32[520,128]{1,0:T(8,128)S(1)}, u32[]{:S(2)}, u32[]{:S(2)}) collective-permute-start(f32[520,128]{1,0:T(8,128)S(1)} %merge.12.after), channel_id=1, source_target_pairs={{0,16},{4,12},{8,24},{12,4},{16,0},{20,28},{24,8},{28,20},{1,17},{... | collective-permute-start | bytes 798728 | tf_op jit(solution)/shard_map/ppermute | solution.py:373
  40.8 4.4 %query_side_own.1 = (bf16[1536,1024]{1,0:T(8,128)(2,1)}, bf16[1536,1024]{1,0:T(8,128)(2,1)}, f32[1536,512]{1,0:T(8,128)S(1)}, f32[1536,512]{1,0:T(8,128)S(1)}, f32[8,128]{1,0:T(8,128)S(1)}) custom-call(f32[520,128]{1,0:T(8,128)S(1)} %merge.12.after, ...), custom_call_target="tpu_custom_call", output_to_operand_aliasing={{0}: (10, {}), {1}: (11, {})} | custom-call | flops 1610612736 | bytes 3145728 | tf_op jit(solution)/shard_map/query_side_own/pallas_call | solution.py:542
  45.2 0.0 collective-permute-done.11.refs_1_
  45.2 0.1 merge.13
  45.4 1.7 %collective-permute-start.12 = (f32[520,128]{1,0:T(8,128)S(1)}, f32[520,128]{1,0:T(8,128)S(1)}, u32[]{:S(2)}, u32[]{:S(2)}) collective-permute-start(f32[520,128]{1,0:T(8,128)S(1)} %get-tuple-element.101), channel_id=1, source_target_pairs={{0,4},{4,0},{8,12},{12,8},{16,20},{20,16},{24,28},{28,24},{1,5},{5... | collective-permute-start | bytes 798728 | tf_op jit(solution)/shard_map/ppermute | solution.py:373
  47.1 2.0 %key_side_own.1 = (bf16[1536,1024]{1,0:T(8,128)(2,1)}, bf16[1536,1024]{1,0:T(8,128)(2,1)}) custom-call(f32[8,128]{1,0:T(8,128)S(1)} %get-tuple-element.58.docs, f32[3072,128]{1,0:T(8,128)S(1)} %get-tuple-element.104.inside, f32[520,128]{1,0:T(8,128)S(1)} %get-tuple-element.105.carry, bf16[1536,512]{1,0:T(8,128)(2,1)S(1)} %get-tuple-element.60.refs_0_.k, ...), custom_call_target="tpu_custom_call" | custom-call | flops 402653184 | bytes 3145728 | tf_op jit(solution)/shard_map/key_side_own/pallas_call | solution.py:557
  49.1 0.0 collective-permute-done.12.carry
  49.1 2.1 %key_side_other.1 = (bf16[1536,1024]{1,0:T(8,128)(2,1)}, bf16[1536,1024]{1,0:T(8,128)(2,1)}) custom-call(f32[8,128]{1,0:T(8,128)S(1)} %get-tuple-element.58.docs, f32[3072,128]{1,0:T(8,128)S(1)} %get-tuple-element.99.inside, f32[520,128]{1,0:T(8,128)S(1)} %collective-permute-done.12.carry, ...), custom_call_target="tpu_custom_call", output_to_operand_aliasing={{0}: (7, {}), {1}: (8, {})} | custom-call | flops 402653184 | bytes 3145728 | tf_op jit(solution)/shard_map/key_side_other/pallas_call | solution.py:557
  (5 shorter events, 0.2 us)
Async XLA Ops:
  3.4 1.9 %collective-permute-start = (f32[520,128]{1,0:T(8,128)S(1)}, f32[520,128]{1,0:T(8,128)S(1)}, u32[]{:S(2)}, u32[]{:S(2)}) collective-permute-start(f32[520,128]{1,0:T(8,128)S(1)} %get-tuple-element.63), channel_id=1, source_target_pairs={{0,4},{4,0},{8,12},{12,8},{16,20},{20,16},{24,28},{28,24},{1,5},{5... | collective-permute-start | bytes 798728 | tf_op jit(solution)/shard_map/ppermute | solution.py:373
  3.5 5.8 %copy-start = (f32[1024]{0:T(1024)S(1)}, f32[1024]{0:T(1024)}, u32[]{:S(2)}) copy-start(f32[1024]{0:T(1024)} %param.10) | copy-start | bytes 12292
  5.3 7.4 %collective-permute-start.1 = (f32[264,128]{1,0:T(8,128)S(1)}, f32[264,128]{1,0:T(8,128)S(1)}, u32[]{:S(2)}, u32[]{:S(2)}) collective-permute-start(f32[264,128]{1,0:T(8,128)S(1)} %get-tuple-element.64.after.refs_0_), channel_id=1, source_target_pairs={{0,8},{4,12},{8,0},{12,4},{16,24},{20,28},{24,16},{28,20},{1,9},{5... | collective-permute-start | bytes 405512 | tf_op jit(solution)/shard_map/ppermute | solution.py:373
  8.0 5.3 %collective-permute-start.2 = (f32[264,128]{1,0:T(8,128)S(1)}, f32[264,128]{1,0:T(8,128)S(1)}, u32[]{:S(2)}, u32[]{:S(2)}) collective-permute-start(f32[264,128]{1,0:T(8,128)S(1)} %get-tuple-element.65.refs_0_), channel_id=1, source_target_pairs={{0,16},{4,20},{8,24},{12,28},{16,0},{20,4},{24,8},{28,12},{1,17},{... | collective-permute-start | bytes 405512 | tf_op jit(solution)/shard_map/ppermute | solution.py:373
  12.7 5.3 %collective-permute-start.3 = (f32[264,128]{1,0:T(8,128)S(1)}, f32[264,128]{1,0:T(8,128)S(1)}, u32[]{:S(2)}, u32[]{:S(2)}) collective-permute-start(f32[264,128]{1,0:T(8,128)S(1)} %merge.8), channel_id=1, source_target_pairs={{0,16},{4,20},{8,24},{12,28},{16,0},{20,4},{24,8},{28,12},{1,17},{... | collective-permute-start | bytes 405512 | tf_op jit(solution)/shard_map/ppermute | solution.py:373
  13.3 4.7 %collective-permute-start.4 = (f32[264,128]{1,0:T(8,128)S(1)}, f32[264,128]{1,0:T(8,128)S(1)}, u32[]{:S(2)}, u32[]{:S(2)}) collective-permute-start(f32[264,128]{1,0:T(8,128)S(1)} %merge.9.after), channel_id=1, source_target_pairs={{0,8},{4,12},{8,0},{12,4},{16,24},{20,28},{24,16},{28,20},{1,9},{5... | collective-permute-start | bytes 405512 | tf_op jit(solution)/shard_map/ppermute | solution.py:373
  18.2 2.8 %collective-permute-start.5 = (f32[520,128]{1,0:T(8,128)S(1)}, f32[520,128]{1,0:T(8,128)S(1)}, u32[]{:S(2)}, u32[]{:S(2)}) collective-permute-start(f32[520,128]{1,0:T(8,128)S(1)} %get-tuple-element.71), channel_id=1, source_target_pairs={{0,4},{4,0},{8,12},{12,8},{16,20},{20,16},{24,28},{28,24},{1,5},{5... | collective-permute-start | bytes 798728 | tf_op jit(solution)/shard_map/ppermute | solution.py:373
  22.3 4.5 %collective-permute-start.8 = (f32[16,256]{1,0:T(8,128)S(1)}, f32[16,256]{1,0:T(8,128)S(1)}, u32[]{:S(2)}, u32[]{:S(2)}) collective-permute-start(f32[16,256]{1,0:T(8,128)S(1)} %get-tuple-element.81.rest_0_), channel_id=1, source_target_pairs={{0,3},{1,2},{2,1},{3,0},{4,7},{5,6},{6,5},{7,4},{8,11},{9,10},{10,... | collective-permute-start | bytes 49160 | tf_op jit(solution)/shard_map/ppermute | solution.py:582
  25.6 3.7 %collective-permute-start.7 = (f32[16,256]{1,0:T(8,128)S(1)}, f32[16,256]{1,0:T(8,128)S(1)}, u32[]{:S(2)}, u32[]{:S(2)}) collective-permute-start(f32[16,256]{1,0:T(8,128)S(1)} %get-tuple-element.81.rest_0_), channel_id=1, source_target_pairs={{0,2},{1,3},{2,0},{3,1},{4,6},{5,7},{6,4},{7,5},{8,10},{9,11},{10,... | collective-permute-start | bytes 49160 | tf_op jit(solution)/shard_map/ppermute | solution.py:582
  25.6 3.7 %collective-permute-start.6 = (f32[16,256]{1,0:T(8,128)S(1)}, f32[16,256]{1,0:T(8,128)S(1)}, u32[]{:S(2)}, u32[]{:S(2)}) collective-permute-start(f32[16,256]{1,0:T(8,128)S(1)} %get-tuple-element.81.rest_0_), channel_id=1, source_target_pairs={{0,1},{1,0},{2,3},{3,2},{4,5},{5,4},{6,7},{7,6},{8,9},{9,8},{10,11... | collective-permute-start | bytes 49160 | tf_op jit(solution)/shard_map/ppermute | solution.py:582
  30.8 3.0 %collective-permute-start.9 = (f32[520,128]{1,0:T(8,128)S(1)}, f32[520,128]{1,0:T(8,128)S(1)}, u32[]{:S(2)}, u32[]{:S(2)}) collective-permute-start(f32[520,128]{1,0:T(8,128)S(1)} %get-tuple-element.87), channel_id=1, source_target_pairs={{0,4},{4,0},{8,12},{12,8},{16,20},{20,16},{24,28},{28,24},{1,5},{5... | collective-permute-start | bytes 798728 | tf_op jit(solution)/shard_map/ppermute | solution.py:373
  33.8 5.6 %collective-permute-start.10 = (f32[520,128]{1,0:T(8,128)S(1)}, f32[520,128]{1,0:T(8,128)S(1)}, u32[]{:S(2)}, u32[]{:S(2)}) collective-permute-start(f32[520,128]{1,0:T(8,128)S(1)} %merge.11.after.refs_0_), channel_id=1, source_target_pairs={{0,8},{4,20},{8,0},{12,28},{16,24},{20,4},{24,16},{28,12},{1,9},{5... | collective-permute-start | bytes 798728 | tf_op jit(solution)/shard_map/ppermute | solution.py:373
  39.5 5.7 %collective-permute-start.11 = (f32[520,128]{1,0:T(8,128)S(1)}, f32[520,128]{1,0:T(8,128)S(1)}, u32[]{:S(2)}, u32[]{:S(2)}) collective-permute-start(f32[520,128]{1,0:T(8,128)S(1)} %merge.12.after), channel_id=1, source_target_pairs={{0,16},{4,12},{8,24},{12,4},{16,0},{20,28},{24,8},{28,20},{1,17},{... | collective-permute-start | bytes 798728 | tf_op jit(solution)/shard_map/ppermute | solution.py:373
  45.4 3.8 %collective-permute-start.12 = (f32[520,128]{1,0:T(8,128)S(1)}, f32[520,128]{1,0:T(8,128)S(1)}, u32[]{:S(2)}, u32[]{:S(2)}) collective-permute-start(f32[520,128]{1,0:T(8,128)S(1)} %get-tuple-element.101), channel_id=1, source_target_pairs={{0,4},{4,0},{8,12},{12,8},{16,20},{20,16},{24,28},{28,24},{1,5},{5... | collective-permute-start | bytes 798728 | tf_op jit(solution)/shard_map/ppermute | solution.py:373

commit v6 on v5

--- a/solution.py
+++ b/solution.py
@@ -234,7 +234,14 @@
             for h in every:
                 d = r * weighted[part, head(h)] - attended[part, head(h)] * s
                 grad[part, head(h)] = d.astype(BF16)
-        sums = [dot(q[rows, head(h)], grad[rows, head(h)], TN) for h in every]
+        if own and heads % 2 == 0:
+            sums = []
+            for h in range(0, heads, 2):
+                both = pl.ds(h * HD, 2 * HD)
+                square = dot(q[rows, both], grad[rows, both], TN)
+                sums += [square[:HD, :HD], square[HD:, HD:]]
+        else:
+            sums = [dot(q[rows, head(h)], grad[rows, head(h)], TN) for h in every]
         for h in every:
             total = inside[state_rows(n, h, heads), :] + sums[h]
             if n > 0:

time: 51.5 us -> 51.5 us (level)
  no operation moved by 1% of the time
where the time goes in v6:
time: 51.5 us; the launch traced here: 51.4 us
  Pallas kernels  30 us (58%)
  starting transfers between devices  16.9 us (33%)
  waiting for transfers between devices  3.51 us (7%)
  between operations  0.97 us (2%)
    ppermute x10, starting transfers between devices, swap(): return lax.ppermute(message, 'ctx', pairs)  13.2 us
    pallas_call x2, Pallas kernels, query_grads(): pl.pallas_call(functools.partial(query_side, own, blocks, heads), name=la...  9.03 us
    pallas_call x2, Pallas kernels, scoring(): pl.pallas_call(functools.partial(local_scores, own, blocks, heads), name=...  6.76 us
    pallas_call x2, Pallas kernels, states(): pl.pallas_call(functools.partial(key_value_states, own, blocks, heads), n...  4.45 us
    pallas_call x2, Pallas kernels, key_grads(): pl.pallas_call(functools.partial(key_side, own, blocks, heads), name=labe...  4.09 us
    ppermute x3, starting transfers between devices, local(): lax.ppermute(sums, 'tp', [(i, i ^ s) for i in range(tp)])  3.72 us
    ppermute x3, waiting for transfers between devices, local(): lax.ppermute(sums, 'tp', [(i, i ^ s) for i in range(tp)])  3.39 us
    pallas_call x2, Pallas kernels, mixing(): pl.pallas_call(functools.partial(mixed, own, blocks, heads, lanes, tp), n...  2.65 us
  transfers between devices with their start and end apart: 13, of which 3 were waited for; matrix products, arithmetic and copies ran while one was open for 0% of the time, Pallas kernels for 43%

profile of v6, /device:TPU:1, one launch (start us, length us, event | category | flops | bytes accessed | tf_op | source)
XLA Modules:
  0.0 51.4 jit_solution(5202357085716936949)
XLA Ops:
  0.6 2.7 %states_other.1 = (bf16[1536,512]{1,0:T(8,128)(2,1)S(1)}, bf16[1536,512]{1,0:T(8,128)(2,1)S(1)}, f32[3072,128]{1,0:T(8,128)S(1)}, f32[520,128]{1,0:T(8,128)S(1)}...) custom-call(s32[6]{0:T(128)} %refs_2_.3, bf16[1536,1024]{1,0:T(8,128)(2,1)} %refs_1_.1, ...), custom_call_target="tpu_custom_call" | custom-call | flops 201326592 | bytes 3145728 | tf_op jit(solution)/shard_map/states_other/pallas_call | solution.py:494
  3.4 0.1 collective-permute-start
  3.5 0.0 copy-start
  3.5 1.7 %states_own.1 = (bf16[1536,512]{1,0:T(8,128)(2,1)S(1)}, f32[3072,128]{1,0:T(8,128)S(1)}, f32[520,128]{1,0:T(8,128)S(1)}) custom-call(bf16[1536,512]{1,0:T(8,128)(2,1)S(1)} %get-tuple-element.60.refs_0_.k, bf16[1536,512]{1,0:T(8,128)(2,1)S(1)} %get-tuple-element.61.refs_1_, s32[6]{0:T(128)} %refs_2_.3, ...), custom_call_target="tpu_custom_call", output_to_operand_aliasing={{0}: (1, {})} | custom-call | flops 201326592 | bytes 3145728 | tf_op jit(solution)/shard_map/states_own/pallas_call | solution.py:494
  5.2 0.0 collective-permute-done.refs_1_.refs_4_
  5.3 2.7 %collective-permute-start.1 = (f32[264,128]{1,0:T(8,128)S(1)}, f32[264,128]{1,0:T(8,128)S(1)}, u32[]{:S(2)}, u32[]{:S(2)}) collective-permute-start(f32[264,128]{1,0:T(8,128)S(1)} %get-tuple-element.64.after.refs_0_), channel_id=1, source_target_pairs={{0,8},{4,12},{8,0},{12,4},{16,24},{20,28},{24,16},{28,20},{1,9},{5... | collective-permute-start | bytes 405512 | tf_op jit(solution)/shard_map/ppermute | solution.py:380
  8.0 1.2 %collective-permute-start.2 = (f32[264,128]{1,0:T(8,128)S(1)}, f32[264,128]{1,0:T(8,128)S(1)}, u32[]{:S(2)}, u32[]{:S(2)}) collective-permute-start(f32[264,128]{1,0:T(8,128)S(1)} %get-tuple-element.65.refs_0_), channel_id=1, source_target_pairs={{0,16},{4,20},{8,24},{12,28},{16,0},{20,4},{24,8},{28,12},{1,17},{... | collective-permute-start | bytes 405512 | tf_op jit(solution)/shard_map/ppermute | solution.py:380
  9.2 0.0 copy-done
  9.2 3.4 %scoring_other.1 = (bf16[1536,512]{1,0:T(8,128)(2,1)S(1)}, f32[1536,512]{1,0:T(8,128)S(1)}, f32[1536,512]{1,0:T(8,128)S(1)}, bf16[6144,256]{1,0:T(8,128)(2,1)S(1)}, f32[8,128]{1,0:T(8,128)S(1)}) custom-call(f32[264,128]{1,0:T(8,128)S(1)} %get-tuple-element.64.after.refs_0_, bf16[1536,512]{1,0:T(8,128)(2,1)S(1)} %get-tuple-element.66.k, ...), custom_call_target="tpu_custom_call" | custom-call | flops 805306368 | bytes 3145728 | tf_op jit(solution)/shard_map/scoring_other/pallas_call | solution.py:507
  12.6 0.0 collective-permute-done.1.refs_1_.refs_0_
  12.7 0.6 %collective-permute-start.3 = (f32[264,128]{1,0:T(8,128)S(1)}, f32[264,128]{1,0:T(8,128)S(1)}, u32[]{:S(2)}, u32[]{:S(2)}) collective-permute-start(f32[264,128]{1,0:T(8,128)S(1)} %merge.8), channel_id=1, source_target_pairs={{0,16},{4,20},{8,24},{12,28},{16,0},{20,4},{24,8},{28,12},{1,17},{... | collective-permute-start | bytes 405512 | tf_op jit(solution)/shard_map/ppermute | solution.py:380
  13.3 0.0 collective-permute-done.2.refs_1_
  13.3 1.3 %collective-permute-start.4 = (f32[264,128]{1,0:T(8,128)S(1)}, f32[264,128]{1,0:T(8,128)S(1)}, u32[]{:S(2)}, u32[]{:S(2)}) collective-permute-start(f32[264,128]{1,0:T(8,128)S(1)} %merge.9.after), channel_id=1, source_target_pairs={{0,8},{4,12},{8,0},{12,4},{16,24},{20,28},{24,16},{28,20},{1,9},{5... | collective-permute-start | bytes 405512 | tf_op jit(solution)/shard_map/ppermute | solution.py:380
  14.6 3.4 %scoring_own.1 = (bf16[1536,512]{1,0:T(8,128)(2,1)S(1)}, f32[1536,512]{1,0:T(8,128)S(1)}, f32[1536,512]{1,0:T(8,128)S(1)}, bf16[6144,256]{1,0:T(8,128)(2,1)S(1)}, f32[8,128]{1,0:T(8,128)S(1)}) custom-call(f32[264,128]{1,0:T(8,128)S(1)} %merge.9.after, bf16[1536,512]{1,0:T(8,128)(2,1)S(1)} %get-tuple-element.60.refs_0_.k, ...), custom_call_target="tpu_custom_call" | custom-call | flops 805306368 | bytes 3145728 | tf_op jit(solution)/shard_map/scoring_own/pallas_call | solution.py:507
  18.0 0.0 collective-permute-done.3.refs_2_
  18.0 0.0 collective-permute-done.4.refs_3_
  18.0 0.1 merge.10
  18.2 1.6 %collective-permute-start.5 = (f32[520,128]{1,0:T(8,128)S(1)}, f32[520,128]{1,0:T(8,128)S(1)}, u32[]{:S(2)}, u32[]{:S(2)}) collective-permute-start(f32[520,128]{1,0:T(8,128)S(1)} %get-tuple-element.71), channel_id=1, source_target_pairs={{0,4},{4,0},{8,12},{12,8},{16,20},{20,16},{24,28},{28,24},{1,5},{5... | collective-permute-start | bytes 798728 | tf_op jit(solution)/shard_map/ppermute | solution.py:380
  19.7 1.3 %attend_own.1 = (f32[1536,512]{1,0:T(8,128)S(1)}, bf16[3072,128]{1,0:T(8,128)(2,1)S(1)}, f32[256,128]{1,0:T(8,128)S(1)}) custom-call(f32[8,128]{1,0:T(8,128)S(1)} %get-tuple-element.58.docs, f32[3072,128]{1,0:T(8,128)S(1)} %get-tuple-element.75.inside, f32[520,128]{1,0:T(8,128)S(1)} %get-tuple-element.76.carry, ...), custom_call_target="tpu_custom_call" | custom-call | flops 201326592 | bytes 1048576 | tf_op jit(solution)/shard_map/attend_own/pallas_call | solution.py:521
  21.0 0.0 collective-permute-done.5.carry
  21.0 1.3 %attend_other.1 = (f32[1536,512]{1,0:T(8,128)S(1)}, bf16[3072,128]{1,0:T(8,128)(2,1)S(1)}, f32[16,256]{1,0:T(8,128)S(1)}) custom-call(f32[8,128]{1,0:T(8,128)S(1)} %get-tuple-element.58.docs, f32[3072,128]{1,0:T(8,128)S(1)} %get-tuple-element.59.inside, f32[520,128]{1,0:T(8,128)S(1)} %collective-permute-done.5.carry, ...), custom_call_target="tpu_custom_call" | custom-call | flops 201326592 | bytes 1048576 | tf_op jit(solution)/shard_map/attend_other/pallas_call | solution.py:521
  22.3 3.4 %collective-permute-start.8 = (f32[16,256]{1,0:T(8,128)S(1)}, f32[16,256]{1,0:T(8,128)S(1)}, u32[]{:S(2)}, u32[]{:S(2)}) collective-permute-start(f32[16,256]{1,0:T(8,128)S(1)} %get-tuple-element.81.rest_0_), channel_id=1, source_target_pairs={{0,3},{1,2},{2,1},{3,0},{4,7},{5,6},{6,5},{7,4},{8,11},{9,10},{10,... | collective-permute-start | bytes 49160 | tf_op jit(solution)/shard_map/ppermute | solution.py:589
  25.6 0.0 collective-permute-start.7
  25.6 0.4 collective-permute-start.6
  26.0 0.8 %collective-permute-done.8.rest_3_ = f32[16,256]{1,0:T(8,128)S(1)} collective-permute-done((f32[16,256]{1,0:T(8,128)S(1)}, f32[16,256]{1,0:T(8,128)S(1)}, u32[]{:S(2)}, u32[]{:S(2)}) %collective-permute-start.8) | collective-permute-done | bytes 16416 | tf_op jit(solution)/shard_map/ppermute | solution.py:589
  26.8 2.6 %collective-permute-done.7.rest_2_ = f32[16,256]{1,0:T(8,128)S(1)} collective-permute-done((f32[16,256]{1,0:T(8,128)S(1)}, f32[16,256]{1,0:T(8,128)S(1)}, u32[]{:S(2)}, u32[]{:S(2)}) %collective-permute-start.7) | collective-permute-done | bytes 16416 | tf_op jit(solution)/shard_map/ppermute | solution.py:589
  29.4 0.0 collective-permute-done.6.rest_1_
  29.4 1.4 %mixed_other.1 = (bf16[1536,512]{1,0:T(8,128)(2,1)S(1)}, f32[3072,128]{1,0:T(8,128)S(1)}, f32[520,128]{1,0:T(8,128)S(1)}, f32[1536,128]{1,0:T(8,128)S(1)}, f32[1536,128]{1,0:T(8,128)S(1)}) custom-call(f32[8,128]{1,0:T(8,128)S(1)} %get-tuple-element.58.docs, f32[16,256]{1,0:T(8,128)S(1)} %get-tuple-element.81.rest_0_, ...), custom_call_target="tpu_custom_call" | custom-call | flops 201326592 | bytes 1048576 | tf_op jit(solution)/shard_map/mixed_other/pallas_call | solution.py:535
  30.8 1.5 %collective-permute-start.9 = (f32[520,128]{1,0:T(8,128)S(1)}, f32[520,128]{1,0:T(8,128)S(1)}, u32[]{:S(2)}, u32[]{:S(2)}) collective-permute-start(f32[520,128]{1,0:T(8,128)S(1)} %get-tuple-element.87), channel_id=1, source_target_pairs={{0,4},{4,0},{8,12},{12,8},{16,20},{20,16},{24,28},{28,24},{1,5},{5... | collective-permute-start | bytes 798728 | tf_op jit(solution)/shard_map/ppermute | solution.py:380
  32.3 1.2 %mixed_own.1 = (bf16[1536,512]{1,0:T(8,128)(2,1)S(1)}, f32[3072,128]{1,0:T(8,128)S(1)}, f32[520,128]{1,0:T(8,128)S(1)}) custom-call(f32[8,128]{1,0:T(8,128)S(1)} %get-tuple-element.58.docs, f32[1536,128]{1,0:T(8,128)S(1)} %get-tuple-element.83.rest_0_.scale, f32[1536,128]{1,0:T(8,128)S(1)} %get-tuple-element.84.rest_1_, ...), custom_call_target="tpu_custom_call" | custom-call | flops 201326592 | bytes 1048576 | tf_op jit(solution)/shard_map/mixed_own/pallas_call | solution.py:535
  33.5 0.0 collective-permute-done.9.refs_1_.refs_2_
  33.6 0.9 %collective-permute-start.10 = (f32[520,128]{1,0:T(8,128)S(1)}, f32[520,128]{1,0:T(8,128)S(1)}, u32[]{:S(2)}, u32[]{:S(2)}) collective-permute-start(f32[520,128]{1,0:T(8,128)S(1)} %merge.11.after.refs_0_), channel_id=1, source_target_pairs={{0,8},{4,20},{8,0},{12,28},{16,24},{20,4},{24,16},{28,12},{1,9},{5... | collective-permute-start | bytes 798728 | tf_op jit(solution)/shard_map/ppermute | solution.py:380
  34.5 4.6 %query_side_other.1 = (bf16[1536,1024]{1,0:T(8,128)(2,1)}, bf16[1536,1024]{1,0:T(8,128)(2,1)}, f32[1536,512]{1,0:T(8,128)S(1)}, f32[1536,512]{1,0:T(8,128)S(1)}, f32[8,128]{1,0:T(8,128)S(1)}) custom-call(f32[520,128]{1,0:T(8,128)S(1)} %merge.11.after.refs_0_, bf16[1536,512]{1,0:T(8,128)(2,1)S(1)} %get-tuple-element.66.k, ...), custom_call_target="tpu_custom_call" | custom-call | flops 1610612736 | bytes 3145728 | tf_op jit(solution)/shard_map/query_side_other/pallas_call | solution.py:549
  39.1 0.1 collective-permute-done.10.refs_1_.refs_0_
  39.3 1.3 %collective-permute-start.11 = (f32[520,128]{1,0:T(8,128)S(1)}, f32[520,128]{1,0:T(8,128)S(1)}, u32[]{:S(2)}, u32[]{:S(2)}) collective-permute-start(f32[520,128]{1,0:T(8,128)S(1)} %merge.12.after), channel_id=1, source_target_pairs={{0,16},{4,12},{8,24},{12,4},{16,0},{20,28},{24,8},{28,20},{1,17},{... | collective-permute-start | bytes 798728 | tf_op jit(solution)/shard_map/ppermute | solution.py:380
  40.5 4.4 %query_side_own.1 = (bf16[1536,1024]{1,0:T(8,128)(2,1)}, bf16[1536,1024]{1,0:T(8,128)(2,1)}, f32[1536,512]{1,0:T(8,128)S(1)}, f32[1536,512]{1,0:T(8,128)S(1)}, f32[8,128]{1,0:T(8,128)S(1)}) custom-call(f32[520,128]{1,0:T(8,128)S(1)} %merge.12.after, ...), custom_call_target="tpu_custom_call", output_to_operand_aliasing={{0}: (10, {}), {1}: (11, {})} | custom-call | flops 1610612736 | bytes 3145728 | tf_op jit(solution)/shard_map/query_side_own/pallas_call | solution.py:549
  45.0 0.0 collective-permute-done.11.refs_1_
  45.0 0.1 merge.13
  45.1 2.0 %collective-permute-start.12 = (f32[520,128]{1,0:T(8,128)S(1)}, f32[520,128]{1,0:T(8,128)S(1)}, u32[]{:S(2)}, u32[]{:S(2)}) collective-permute-start(f32[520,128]{1,0:T(8,128)S(1)} %get-tuple-element.101), channel_id=1, source_target_pairs={{0,4},{4,0},{8,12},{12,8},{16,20},{20,16},{24,28},{28,24},{1,5},{5... | collective-permute-start | bytes 798728 | tf_op jit(solution)/shard_map/ppermute | solution.py:380
  47.1 2.0 %key_side_own.1 = (bf16[1536,1024]{1,0:T(8,128)(2,1)}, bf16[1536,1024]{1,0:T(8,128)(2,1)}) custom-call(f32[8,128]{1,0:T(8,128)S(1)} %get-tuple-element.58.docs, f32[3072,128]{1,0:T(8,128)S(1)} %get-tuple-element.104.inside, f32[520,128]{1,0:T(8,128)S(1)} %get-tuple-element.105.carry, bf16[1536,512]{1,0:T(8,128)(2,1)S(1)} %get-tuple-element.60.refs_0_.k, ...), custom_call_target="tpu_custom_call" | custom-call | flops 402653184 | bytes 3145728 | tf_op jit(solution)/shard_map/key_side_own/pallas_call | solution.py:564
  49.1 0.0 collective-permute-done.12.carry
  49.1 2.1 %key_side_other.1 = (bf16[1536,1024]{1,0:T(8,128)(2,1)}, bf16[1536,1024]{1,0:T(8,128)(2,1)}) custom-call(f32[8,128]{1,0:T(8,128)S(1)} %get-tuple-element.58.docs, f32[3072,128]{1,0:T(8,128)S(1)} %get-tuple-element.99.inside, f32[520,128]{1,0:T(8,128)S(1)} %collective-permute-done.12.carry, ...), custom_call_target="tpu_custom_call", output_to_operand_aliasing={{0}: (7, {}), {1}: (8, {})} | custom-call | flops 402653184 | bytes 3145728 | tf_op jit(solution)/shard_map/key_side_other/pallas_call | solution.py:564
  (5 shorter events, 0.2 us)
Async XLA Ops:
  3.4 1.9 %collective-permute-start = (f32[520,128]{1,0:T(8,128)S(1)}, f32[520,128]{1,0:T(8,128)S(1)}, u32[]{:S(2)}, u32[]{:S(2)}) collective-permute-start(f32[520,128]{1,0:T(8,128)S(1)} %get-tuple-element.63), channel_id=1, source_target_pairs={{0,4},{4,0},{8,12},{12,8},{16,20},{20,16},{24,28},{28,24},{1,5},{5... | collective-permute-start | bytes 798728 | tf_op jit(solution)/shard_map/ppermute | solution.py:380
  3.5 5.8 %copy-start = (f32[1024]{0:T(1024)S(1)}, f32[1024]{0:T(1024)}, u32[]{:S(2)}) copy-start(f32[1024]{0:T(1024)} %param.10) | copy-start | bytes 12292
  5.3 7.4 %collective-permute-start.1 = (f32[264,128]{1,0:T(8,128)S(1)}, f32[264,128]{1,0:T(8,128)S(1)}, u32[]{:S(2)}, u32[]{:S(2)}) collective-permute-start(f32[264,128]{1,0:T(8,128)S(1)} %get-tuple-element.64.after.refs_0_), channel_id=1, source_target_pairs={{0,8},{4,12},{8,0},{12,4},{16,24},{20,28},{24,16},{28,20},{1,9},{5... | collective-permute-start | bytes 405512 | tf_op jit(solution)/shard_map/ppermute | solution.py:380
  8.0 5.3 %collective-permute-start.2 = (f32[264,128]{1,0:T(8,128)S(1)}, f32[264,128]{1,0:T(8,128)S(1)}, u32[]{:S(2)}, u32[]{:S(2)}) collective-permute-start(f32[264,128]{1,0:T(8,128)S(1)} %get-tuple-element.65.refs_0_), channel_id=1, source_target_pairs={{0,16},{4,20},{8,24},{12,28},{16,0},{20,4},{24,8},{28,12},{1,17},{... | collective-permute-start | bytes 405512 | tf_op jit(solution)/shard_map/ppermute | solution.py:380
  12.7 5.3 %collective-permute-start.3 = (f32[264,128]{1,0:T(8,128)S(1)}, f32[264,128]{1,0:T(8,128)S(1)}, u32[]{:S(2)}, u32[]{:S(2)}) collective-permute-start(f32[264,128]{1,0:T(8,128)S(1)} %merge.8), channel_id=1, source_target_pairs={{0,16},{4,20},{8,24},{12,28},{16,0},{20,4},{24,8},{28,12},{1,17},{... | collective-permute-start | bytes 405512 | tf_op jit(solution)/shard_map/ppermute | solution.py:380
  13.3 4.7 %collective-permute-start.4 = (f32[264,128]{1,0:T(8,128)S(1)}, f32[264,128]{1,0:T(8,128)S(1)}, u32[]{:S(2)}, u32[]{:S(2)}) collective-permute-start(f32[264,128]{1,0:T(8,128)S(1)} %merge.9.after), channel_id=1, source_target_pairs={{0,8},{4,12},{8,0},{12,4},{16,24},{20,28},{24,16},{28,20},{1,9},{5... | collective-permute-start | bytes 405512 | tf_op jit(solution)/shard_map/ppermute | solution.py:380
  18.2 2.8 %collective-permute-start.5 = (f32[520,128]{1,0:T(8,128)S(1)}, f32[520,128]{1,0:T(8,128)S(1)}, u32[]{:S(2)}, u32[]{:S(2)}) collective-permute-start(f32[520,128]{1,0:T(8,128)S(1)} %get-tuple-element.71), channel_id=1, source_target_pairs={{0,4},{4,0},{8,12},{12,8},{16,20},{20,16},{24,28},{28,24},{1,5},{5... | collective-permute-start | bytes 798728 | tf_op jit(solution)/shard_map/ppermute | solution.py:380
  22.3 4.5 %collective-permute-start.8 = (f32[16,256]{1,0:T(8,128)S(1)}, f32[16,256]{1,0:T(8,128)S(1)}, u32[]{:S(2)}, u32[]{:S(2)}) collective-permute-start(f32[16,256]{1,0:T(8,128)S(1)} %get-tuple-element.81.rest_0_), channel_id=1, source_target_pairs={{0,3},{1,2},{2,1},{3,0},{4,7},{5,6},{6,5},{7,4},{8,11},{9,10},{10,... | collective-permute-start | bytes 49160 | tf_op jit(solution)/shard_map/ppermute | solution.py:589
  25.6 3.7 %collective-permute-start.7 = (f32[16,256]{1,0:T(8,128)S(1)}, f32[16,256]{1,0:T(8,128)S(1)}, u32[]{:S(2)}, u32[]{:S(2)}) collective-permute-start(f32[16,256]{1,0:T(8,128)S(1)} %get-tuple-element.81.rest_0_), channel_id=1, source_target_pairs={{0,2},{1,3},{2,0},{3,1},{4,6},{5,7},{6,4},{7,5},{8,10},{9,11},{10,... | collective-permute-start | bytes 49160 | tf_op jit(solution)/shard_map/ppermute | solution.py:589
  25.6 3.7 %collective-permute-start.6 = (f32[16,256]{1,0:T(8,128)S(1)}, f32[16,256]{1,0:T(8,128)S(1)}, u32[]{:S(2)}, u32[]{:S(2)}) collective-permute-start(f32[16,256]{1,0:T(8,128)S(1)} %get-tuple-element.81.rest_0_), channel_id=1, source_target_pairs={{0,1},{1,0},{2,3},{3,2},{4,5},{5,4},{6,7},{7,6},{8,9},{9,8},{10,11... | collective-permute-start | bytes 49160 | tf_op jit(solution)/shard_map/ppermute | solution.py:589
  30.8 2.7 %collective-permute-start.9 = (f32[520,128]{1,0:T(8,128)S(1)}, f32[520,128]{1,0:T(8,128)S(1)}, u32[]{:S(2)}, u32[]{:S(2)}) collective-permute-start(f32[520,128]{1,0:T(8,128)S(1)} %get-tuple-element.87), channel_id=1, source_target_pairs={{0,4},{4,0},{8,12},{12,8},{16,20},{20,16},{24,28},{28,24},{1,5},{5... | collective-permute-start | bytes 798728 | tf_op jit(solution)/shard_map/ppermute | solution.py:380
  33.6 5.6 %collective-permute-start.10 = (f32[520,128]{1,0:T(8,128)S(1)}, f32[520,128]{1,0:T(8,128)S(1)}, u32[]{:S(2)}, u32[]{:S(2)}) collective-permute-start(f32[520,128]{1,0:T(8,128)S(1)} %merge.11.after.refs_0_), channel_id=1, source_target_pairs={{0,8},{4,20},{8,0},{12,28},{16,24},{20,4},{24,16},{28,12},{1,9},{5... | collective-permute-start | bytes 798728 | tf_op jit(solution)/shard_map/ppermute | solution.py:380
  39.3 5.7 %collective-permute-start.11 = (f32[520,128]{1,0:T(8,128)S(1)}, f32[520,128]{1,0:T(8,128)S(1)}, u32[]{:S(2)}, u32[]{:S(2)}) collective-permute-start(f32[520,128]{1,0:T(8,128)S(1)} %merge.12.after), channel_id=1, source_target_pairs={{0,16},{4,12},{8,24},{12,4},{16,0},{20,28},{24,8},{28,20},{1,17},{... | collective-permute-start | bytes 798728 | tf_op jit(solution)/shard_map/ppermute | solution.py:380
  45.1 4.0 %collective-permute-start.12 = (f32[520,128]{1,0:T(8,128)S(1)}, f32[520,128]{1,0:T(8,128)S(1)}, u32[]{:S(2)}, u32[]{:S(2)}) collective-permute-start(f32[520,128]{1,0:T(8,128)S(1)} %get-tuple-element.101), channel_id=1, source_target_pairs={{0,4},{4,0},{8,12},{12,8},{16,20},{20,16},{24,28},{28,24},{1,5},{5... | collective-permute-start | bytes 798728 | tf_op jit(solution)/shard_map/ppermute | solution.py:380

commit v7 on v5

--- a/solution.py
+++ b/solution.py
@@ -308,15 +308,15 @@
         for h in every:
             state = inside[state_rows(n, h, heads), :] + jnp.where(hit, carry[head(h), :], 0.0)
             states.append(state.astype(BF16))
+        key_copy, value_copy = store_blocks(n, n, pairs, cols, sems)
         kg = [dot(v[rows, head(h)], states[h], NT) for h in every]
+        for h in every:
+            stage_k[n, :, head(h)] = (kg[h] + key_local[rows, head(h)]).astype(BF16)
+        key_copy.start()
         vg = [dot(k[rows, head(h)], states[h], NN) for h in every]
-        kg = [(kg[h] + key_local[rows, head(h)]).astype(BF16) for h in every]
-        vg = [(vg[h] + value_local[rows, head(h)]).astype(BF16) for h in every]
         for h in every:
-            stage_k[n, :, head(h)] = kg[h]
-            stage_v[n, :, head(h)] = vg[h]
-        for copy in store_blocks(n, n, pairs, cols, sems):
-            copy.start()
+            stage_v[n, :, head(h)] = (vg[h] + value_local[rows, head(h)]).astype(BF16)
+        value_copy.start()
         return carried
 
     lax.fori_loop(0, blocks, step, 0, unroll=U_K)

time: 51.5 us -> 51.5 us (level)
  no operation moved by 1% of the time
where the time goes in v7:
time: 51.5 us; the launch traced here: 51.4 us
  Pallas kernels  30.2 us (59%)
  starting transfers between devices  16.7 us (32%)
  waiting for transfers between devices  3.53 us (7%)
  between operations  0.97 us (2%)
    ppermute x10, starting transfers between devices, swap(): return lax.ppermute(message, 'ctx', pairs)  12.9 us
    pallas_call x2, Pallas kernels, query_grads(): pl.pallas_call(functools.partial(query_side, own, blocks, heads), name=la...  9.02 us
    pallas_call x2, Pallas kernels, scoring(): pl.pallas_call(functools.partial(local_scores, own, blocks, heads), name=...  6.76 us
    pallas_call x2, Pallas kernels, states(): pl.pallas_call(functools.partial(key_value_states, own, blocks, heads), n...  4.45 us
    pallas_call x2, Pallas kernels, key_grads(): pl.pallas_call(functools.partial(key_side, own, blocks, heads), name=labe...  4.09 us
    ppermute x3, starting transfers between devices, local(): lax.ppermute(sums, 'tp', [(i, i ^ s) for i in range(tp)])  3.72 us
    ppermute x3, waiting for transfers between devices, local(): lax.ppermute(sums, 'tp', [(i, i ^ s) for i in range(tp)])  3.39 us
    pallas_call x2, Pallas kernels, mixing(): pl.pallas_call(functools.partial(mixed, own, blocks, heads, lanes, tp), n...  2.9 us
  transfers between devices with their start and end apart: 13, of which 3 were waited for; matrix products, arithmetic and copies ran while one was open for 0% of the time, Pallas kernels for 43%

profile of v7, /device:TPU:1, one launch (start us, length us, event | category | flops | bytes accessed | tf_op | source)
XLA Modules:
  0.0 51.4 jit_solution(12191400653883134985)
XLA Ops:
  0.6 2.7 %states_other.1 = (bf16[1536,512]{1,0:T(8,128)(2,1)S(1)}, bf16[1536,512]{1,0:T(8,128)(2,1)S(1)}, f32[3072,128]{1,0:T(8,128)S(1)}, f32[520,128]{1,0:T(8,128)S(1)}...) custom-call(s32[6]{0:T(128)} %refs_2_.3, bf16[1536,1024]{1,0:T(8,128)(2,1)} %refs_1_.1, ...), custom_call_target="tpu_custom_call" | custom-call | flops 201326592 | bytes 3145728 | tf_op jit(solution)/shard_map/states_other/pallas_call | solution.py:487
  3.4 0.1 collective-permute-start
  3.5 0.0 copy-start
  3.5 1.7 %states_own.1 = (bf16[1536,512]{1,0:T(8,128)(2,1)S(1)}, f32[3072,128]{1,0:T(8,128)S(1)}, f32[520,128]{1,0:T(8,128)S(1)}) custom-call(bf16[1536,512]{1,0:T(8,128)(2,1)S(1)} %get-tuple-element.60.refs_0_.k, bf16[1536,512]{1,0:T(8,128)(2,1)S(1)} %get-tuple-element.61.refs_1_, s32[6]{0:T(128)} %refs_2_.3, ...), custom_call_target="tpu_custom_call", output_to_operand_aliasing={{0}: (1, {})} | custom-call | flops 201326592 | bytes 3145728 | tf_op jit(solution)/shard_map/states_own/pallas_call | solution.py:487
  5.2 0.0 collective-permute-done.refs_1_.refs_4_
  5.3 2.7 %collective-permute-start.1 = (f32[264,128]{1,0:T(8,128)S(1)}, f32[264,128]{1,0:T(8,128)S(1)}, u32[]{:S(2)}, u32[]{:S(2)}) collective-permute-start(f32[264,128]{1,0:T(8,128)S(1)} %get-tuple-element.64.after.refs_0_), channel_id=1, source_target_pairs={{0,8},{4,12},{8,0},{12,4},{16,24},{20,28},{24,16},{28,20},{1,9},{5... | collective-permute-start | bytes 405512 | tf_op jit(solution)/shard_map/ppermute | solution.py:373
  8.0 1.2 %collective-permute-start.2 = (f32[264,128]{1,0:T(8,128)S(1)}, f32[264,128]{1,0:T(8,128)S(1)}, u32[]{:S(2)}, u32[]{:S(2)}) collective-permute-start(f32[264,128]{1,0:T(8,128)S(1)} %get-tuple-element.65.refs_0_), channel_id=1, source_target_pairs={{0,16},{4,20},{8,24},{12,28},{16,0},{20,4},{24,8},{28,12},{1,17},{... | collective-permute-start | bytes 405512 | tf_op jit(solution)/shard_map/ppermute | solution.py:373
  9.2 0.0 copy-done
  9.2 3.4 %scoring_other.1 = (bf16[1536,512]{1,0:T(8,128)(2,1)S(1)}, f32[1536,512]{1,0:T(8,128)S(1)}, f32[1536,512]{1,0:T(8,128)S(1)}, bf16[6144,256]{1,0:T(8,128)(2,1)S(1)}, f32[8,128]{1,0:T(8,128)S(1)}) custom-call(f32[264,128]{1,0:T(8,128)S(1)} %get-tuple-element.64.after.refs_0_, bf16[1536,512]{1,0:T(8,128)(2,1)S(1)} %get-tuple-element.66.k, ...), custom_call_target="tpu_custom_call" | custom-call | flops 805306368 | bytes 3145728 | tf_op jit(solution)/shard_map/scoring_other/pallas_call | solution.py:500
  12.6 0.0 collective-permute-done.1.refs_1_.refs_0_
  12.7 0.6 %collective-permute-start.3 = (f32[264,128]{1,0:T(8,128)S(1)}, f32[264,128]{1,0:T(8,128)S(1)}, u32[]{:S(2)}, u32[]{:S(2)}) collective-permute-start(f32[264,128]{1,0:T(8,128)S(1)} %merge.8), channel_id=1, source_target_pairs={{0,16},{4,20},{8,24},{12,28},{16,0},{20,4},{24,8},{28,12},{1,17},{... | collective-permute-start | bytes 405512 | tf_op jit(solution)/shard_map/ppermute | solution.py:373
  13.3 0.0 collective-permute-done.2.refs_1_
  13.3 1.3 %collective-permute-start.4 = (f32[264,128]{1,0:T(8,128)S(1)}, f32[264,128]{1,0:T(8,128)S(1)}, u32[]{:S(2)}, u32[]{:S(2)}) collective-permute-start(f32[264,128]{1,0:T(8,128)S(1)} %merge.9.after), channel_id=1, source_target_pairs={{0,8},{4,12},{8,0},{12,4},{16,24},{20,28},{24,16},{28,20},{1,9},{5... | collective-permute-start | bytes 405512 | tf_op jit(solution)/shard_map/ppermute | solution.py:373
  14.6 3.4 %scoring_own.1 = (bf16[1536,512]{1,0:T(8,128)(2,1)S(1)}, f32[1536,512]{1,0:T(8,128)S(1)}, f32[1536,512]{1,0:T(8,128)S(1)}, bf16[6144,256]{1,0:T(8,128)(2,1)S(1)}, f32[8,128]{1,0:T(8,128)S(1)}) custom-call(f32[264,128]{1,0:T(8,128)S(1)} %merge.9.after, bf16[1536,512]{1,0:T(8,128)(2,1)S(1)} %get-tuple-element.60.refs_0_.k, ...), custom_call_target="tpu_custom_call" | custom-call | flops 805306368 | bytes 3145728 | tf_op jit(solution)/shard_map/scoring_own/pallas_call | solution.py:500
  18.0 0.0 collective-permute-done.3.refs_2_
  18.0 0.0 collective-permute-done.4.refs_3_
  18.0 0.1 merge.10
  18.2 1.6 %collective-permute-start.5 = (f32[520,128]{1,0:T(8,128)S(1)}, f32[520,128]{1,0:T(8,128)S(1)}, u32[]{:S(2)}, u32[]{:S(2)}) collective-permute-start(f32[520,128]{1,0:T(8,128)S(1)} %get-tuple-element.71), channel_id=1, source_target_pairs={{0,4},{4,0},{8,12},{12,8},{16,20},{20,16},{24,28},{28,24},{1,5},{5... | collective-permute-start | bytes 798728 | tf_op jit(solution)/shard_map/ppermute | solution.py:373
  19.7 1.3 %attend_own.1 = (f32[1536,512]{1,0:T(8,128)S(1)}, bf16[3072,128]{1,0:T(8,128)(2,1)S(1)}, f32[256,128]{1,0:T(8,128)S(1)}) custom-call(f32[8,128]{1,0:T(8,128)S(1)} %get-tuple-element.58.docs, f32[3072,128]{1,0:T(8,128)S(1)} %get-tuple-element.75.inside, f32[520,128]{1,0:T(8,128)S(1)} %get-tuple-element.76.carry, ...), custom_call_target="tpu_custom_call" | custom-call | flops 201326592 | bytes 1048576 | tf_op jit(solution)/shard_map/attend_own/pallas_call | solution.py:514
  21.0 0.0 collective-permute-done.5.carry
  21.0 1.3 %attend_other.1 = (f32[1536,512]{1,0:T(8,128)S(1)}, bf16[3072,128]{1,0:T(8,128)(2,1)S(1)}, f32[16,256]{1,0:T(8,128)S(1)}) custom-call(f32[8,128]{1,0:T(8,128)S(1)} %get-tuple-element.58.docs, f32[3072,128]{1,0:T(8,128)S(1)} %get-tuple-element.59.inside, f32[520,128]{1,0:T(8,128)S(1)} %collective-permute-done.5.carry, ...), custom_call_target="tpu_custom_call" | custom-call | flops 201326592 | bytes 1048576 | tf_op jit(solution)/shard_map/attend_other/pallas_call | solution.py:514
  22.3 3.4 %collective-permute-start.8 = (f32[16,256]{1,0:T(8,128)S(1)}, f32[16,256]{1,0:T(8,128)S(1)}, u32[]{:S(2)}, u32[]{:S(2)}) collective-permute-start(f32[16,256]{1,0:T(8,128)S(1)} %get-tuple-element.81.rest_0_), channel_id=1, source_target_pairs={{0,3},{1,2},{2,1},{3,0},{4,7},{5,6},{6,5},{7,4},{8,11},{9,10},{10,... | collective-permute-start | bytes 49160 | tf_op jit(solution)/shard_map/ppermute | solution.py:582
  25.6 0.0 collective-permute-start.7
  25.6 0.4 collective-permute-start.6
  26.0 0.8 %collective-permute-done.8.rest_3_ = f32[16,256]{1,0:T(8,128)S(1)} collective-permute-done((f32[16,256]{1,0:T(8,128)S(1)}, f32[16,256]{1,0:T(8,128)S(1)}, u32[]{:S(2)}, u32[]{:S(2)}) %collective-permute-start.8) | collective-permute-done | bytes 16416 | tf_op jit(solution)/shard_map/ppermute | solution.py:582
  26.8 2.6 %collective-permute-done.7.rest_2_ = f32[16,256]{1,0:T(8,128)S(1)} collective-permute-done((f32[16,256]{1,0:T(8,128)S(1)}, f32[16,256]{1,0:T(8,128)S(1)}, u32[]{:S(2)}, u32[]{:S(2)}) %collective-permute-start.7) | collective-permute-done | bytes 16416 | tf_op jit(solution)/shard_map/ppermute | solution.py:582
  29.4 0.0 collective-permute-done.6.rest_1_
  29.4 1.4 %mixed_other.1 = (bf16[1536,512]{1,0:T(8,128)(2,1)S(1)}, f32[3072,128]{1,0:T(8,128)S(1)}, f32[520,128]{1,0:T(8,128)S(1)}, f32[1536,128]{1,0:T(8,128)S(1)}, f32[1536,128]{1,0:T(8,128)S(1)}) custom-call(f32[8,128]{1,0:T(8,128)S(1)} %get-tuple-element.58.docs, f32[16,256]{1,0:T(8,128)S(1)} %get-tuple-element.81.rest_0_, ...), custom_call_target="tpu_custom_call" | custom-call | flops 201326592 | bytes 1048576 | tf_op jit(solution)/shard_map/mixed_other/pallas_call | solution.py:528
  30.8 1.5 %collective-permute-start.9 = (f32[520,128]{1,0:T(8,128)S(1)}, f32[520,128]{1,0:T(8,128)S(1)}, u32[]{:S(2)}, u32[]{:S(2)}) collective-permute-start(f32[520,128]{1,0:T(8,128)S(1)} %get-tuple-element.87), channel_id=1, source_target_pairs={{0,4},{4,0},{8,12},{12,8},{16,20},{20,16},{24,28},{28,24},{1,5},{5... | collective-permute-start | bytes 798728 | tf_op jit(solution)/shard_map/ppermute | solution.py:373
  32.3 1.5 %mixed_own.1 = (bf16[1536,512]{1,0:T(8,128)(2,1)S(1)}, f32[3072,128]{1,0:T(8,128)S(1)}, f32[520,128]{1,0:T(8,128)S(1)}) custom-call(f32[8,128]{1,0:T(8,128)S(1)} %get-tuple-element.58.docs, f32[1536,128]{1,0:T(8,128)S(1)} %get-tuple-element.83.rest_0_.scale, f32[1536,128]{1,0:T(8,128)S(1)} %get-tuple-element.84.rest_1_, ...), custom_call_target="tpu_custom_call" | custom-call | flops 201326592 | bytes 1048576 | tf_op jit(solution)/shard_map/mixed_own/pallas_call | solution.py:528
  33.8 0.0 collective-permute-done.9.refs_1_.refs_2_
  33.8 0.9 %collective-permute-start.10 = (f32[520,128]{1,0:T(8,128)S(1)}, f32[520,128]{1,0:T(8,128)S(1)}, u32[]{:S(2)}, u32[]{:S(2)}) collective-permute-start(f32[520,128]{1,0:T(8,128)S(1)} %merge.11.after.refs_0_), channel_id=1, source_target_pairs={{0,8},{4,20},{8,0},{12,28},{16,24},{20,4},{24,16},{28,12},{1,9},{5... | collective-permute-start | bytes 798728 | tf_op jit(solution)/shard_map/ppermute | solution.py:373
  34.7 4.6 %query_side_other.1 = (bf16[1536,1024]{1,0:T(8,128)(2,1)}, bf16[1536,1024]{1,0:T(8,128)(2,1)}, f32[1536,512]{1,0:T(8,128)S(1)}, f32[1536,512]{1,0:T(8,128)S(1)}, f32[8,128]{1,0:T(8,128)S(1)}) custom-call(f32[520,128]{1,0:T(8,128)S(1)} %merge.11.after.refs_0_, bf16[1536,512]{1,0:T(8,128)(2,1)S(1)} %get-tuple-element.66.k, ...), custom_call_target="tpu_custom_call" | custom-call | flops 1610612736 | bytes 3145728 | tf_op jit(solution)/shard_map/query_side_other/pallas_call | solution.py:542
  39.4 0.1 collective-permute-done.10.refs_1_.refs_0_
  39.5 1.3 %collective-permute-start.11 = (f32[520,128]{1,0:T(8,128)S(1)}, f32[520,128]{1,0:T(8,128)S(1)}, u32[]{:S(2)}, u32[]{:S(2)}) collective-permute-start(f32[520,128]{1,0:T(8,128)S(1)} %merge.12.after), channel_id=1, source_target_pairs={{0,16},{4,12},{8,24},{12,4},{16,0},{20,28},{24,8},{28,20},{1,17},{... | collective-permute-start | bytes 798728 | tf_op jit(solution)/shard_map/ppermute | solution.py:373
  40.8 4.4 %query_side_own.1 = (bf16[1536,1024]{1,0:T(8,128)(2,1)}, bf16[1536,1024]{1,0:T(8,128)(2,1)}, f32[1536,512]{1,0:T(8,128)S(1)}, f32[1536,512]{1,0:T(8,128)S(1)}, f32[8,128]{1,0:T(8,128)S(1)}) custom-call(f32[520,128]{1,0:T(8,128)S(1)} %merge.12.after, ...), custom_call_target="tpu_custom_call", output_to_operand_aliasing={{0}: (10, {}), {1}: (11, {})} | custom-call | flops 1610612736 | bytes 3145728 | tf_op jit(solution)/shard_map/query_side_own/pallas_call | solution.py:542
  45.2 0.0 collective-permute-done.11.refs_1_
  45.2 0.1 merge.13
  45.4 1.7 %collective-permute-start.12 = (f32[520,128]{1,0:T(8,128)S(1)}, f32[520,128]{1,0:T(8,128)S(1)}, u32[]{:S(2)}, u32[]{:S(2)}) collective-permute-start(f32[520,128]{1,0:T(8,128)S(1)} %get-tuple-element.101), channel_id=1, source_target_pairs={{0,4},{4,0},{8,12},{12,8},{16,20},{20,16},{24,28},{28,24},{1,5},{5... | collective-permute-start | bytes 798728 | tf_op jit(solution)/shard_map/ppermute | solution.py:373
  47.1 2.0 %key_side_own.1 = (bf16[1536,1024]{1,0:T(8,128)(2,1)}, bf16[1536,1024]{1,0:T(8,128)(2,1)}) custom-call(f32[8,128]{1,0:T(8,128)S(1)} %get-tuple-element.58.docs, f32[3072,128]{1,0:T(8,128)S(1)} %get-tuple-element.104.inside, f32[520,128]{1,0:T(8,128)S(1)} %get-tuple-element.105.carry, bf16[1536,512]{1,0:T(8,128)(2,1)S(1)} %get-tuple-element.60.refs_0_.k, ...), custom_call_target="tpu_custom_call" | custom-call | flops 402653184 | bytes 3145728 | tf_op jit(solution)/shard_map/key_side_own/pallas_call | solution.py:557
  49.1 0.0 collective-permute-done.12.carry
  49.1 2.1 %key_side_other.1 = (bf16[1536,1024]{1,0:T(8,128)(2,1)}, bf16[1536,1024]{1,0:T(8,128)(2,1)}) custom-call(f32[8,128]{1,0:T(8,128)S(1)} %get-tuple-element.58.docs, f32[3072,128]{1,0:T(8,128)S(1)} %get-tuple-element.99.inside, f32[520,128]{1,0:T(8,128)S(1)} %collective-permute-done.12.carry, ...), custom_call_target="tpu_custom_call", output_to_operand_aliasing={{0}: (7, {}), {1}: (8, {})} | custom-call | flops 402653184 | bytes 3145728 | tf_op jit(solution)/shard_map/key_side_other/pallas_call | solution.py:557
  (5 shorter events, 0.2 us)
Async XLA Ops:
  3.4 1.9 %collective-permute-start = (f32[520,128]{1,0:T(8,128)S(1)}, f32[520,128]{1,0:T(8,128)S(1)}, u32[]{:S(2)}, u32[]{:S(2)}) collective-permute-start(f32[520,128]{1,0:T(8,128)S(1)} %get-tuple-element.63), channel_id=1, source_target_pairs={{0,4},{4,0},{8,12},{12,8},{16,20},{20,16},{24,28},{28,24},{1,5},{5... | collective-permute-start | bytes 798728 | tf_op jit(solution)/shard_map/ppermute | solution.py:373
  3.5 5.8 %copy-start = (f32[1024]{0:T(1024)S(1)}, f32[1024]{0:T(1024)}, u32[]{:S(2)}) copy-start(f32[1024]{0:T(1024)} %param.10) | copy-start | bytes 12292
  5.3 7.4 %collective-permute-start.1 = (f32[264,128]{1,0:T(8,128)S(1)}, f32[264,128]{1,0:T(8,128)S(1)}, u32[]{:S(2)}, u32[]{:S(2)}) collective-permute-start(f32[264,128]{1,0:T(8,128)S(1)} %get-tuple-element.64.after.refs_0_), channel_id=1, source_target_pairs={{0,8},{4,12},{8,0},{12,4},{16,24},{20,28},{24,16},{28,20},{1,9},{5... | collective-permute-start | bytes 405512 | tf_op jit(solution)/shard_map/ppermute | solution.py:373
  8.0 5.3 %collective-permute-start.2 = (f32[264,128]{1,0:T(8,128)S(1)}, f32[264,128]{1,0:T(8,128)S(1)}, u32[]{:S(2)}, u32[]{:S(2)}) collective-permute-start(f32[264,128]{1,0:T(8,128)S(1)} %get-tuple-element.65.refs_0_), channel_id=1, source_target_pairs={{0,16},{4,20},{8,24},{12,28},{16,0},{20,4},{24,8},{28,12},{1,17},{... | collective-permute-start | bytes 405512 | tf_op jit(solution)/shard_map/ppermute | solution.py:373
  12.7 5.3 %collective-permute-start.3 = (f32[264,128]{1,0:T(8,128)S(1)}, f32[264,128]{1,0:T(8,128)S(1)}, u32[]{:S(2)}, u32[]{:S(2)}) collective-permute-start(f32[264,128]{1,0:T(8,128)S(1)} %merge.8), channel_id=1, source_target_pairs={{0,16},{4,20},{8,24},{12,28},{16,0},{20,4},{24,8},{28,12},{1,17},{... | collective-permute-start | bytes 405512 | tf_op jit(solution)/shard_map/ppermute | solution.py:373
  13.3 4.7 %collective-permute-start.4 = (f32[264,128]{1,0:T(8,128)S(1)}, f32[264,128]{1,0:T(8,128)S(1)}, u32[]{:S(2)}, u32[]{:S(2)}) collective-permute-start(f32[264,128]{1,0:T(8,128)S(1)} %merge.9.after), channel_id=1, source_target_pairs={{0,8},{4,12},{8,0},{12,4},{16,24},{20,28},{24,16},{28,20},{1,9},{5... | collective-permute-start | bytes 405512 | tf_op jit(solution)/shard_map/ppermute | solution.py:373
  18.2 2.8 %collective-permute-start.5 = (f32[520,128]{1,0:T(8,128)S(1)}, f32[520,128]{1,0:T(8,128)S(1)}, u32[]{:S(2)}, u32[]{:S(2)}) collective-permute-start(f32[520,128]{1,0:T(8,128)S(1)} %get-tuple-element.71), channel_id=1, source_target_pairs={{0,4},{4,0},{8,12},{12,8},{16,20},{20,16},{24,28},{28,24},{1,5},{5... | collective-permute-start | bytes 798728 | tf_op jit(solution)/shard_map/ppermute | solution.py:373
  22.3 4.5 %collective-permute-start.8 = (f32[16,256]{1,0:T(8,128)S(1)}, f32[16,256]{1,0:T(8,128)S(1)}, u32[]{:S(2)}, u32[]{:S(2)}) collective-permute-start(f32[16,256]{1,0:T(8,128)S(1)} %get-tuple-element.81.rest_0_), channel_id=1, source_target_pairs={{0,3},{1,2},{2,1},{3,0},{4,7},{5,6},{6,5},{7,4},{8,11},{9,10},{10,... | collective-permute-start | bytes 49160 | tf_op jit(solution)/shard_map/ppermute | solution.py:582
  25.6 3.7 %collective-permute-start.7 = (f32[16,256]{1,0:T(8,128)S(1)}, f32[16,256]{1,0:T(8,128)S(1)}, u32[]{:S(2)}, u32[]{:S(2)}) collective-permute-start(f32[16,256]{1,0:T(8,128)S(1)} %get-tuple-element.81.rest_0_), channel_id=1, source_target_pairs={{0,2},{1,3},{2,0},{3,1},{4,6},{5,7},{6,4},{7,5},{8,10},{9,11},{10,... | collective-permute-start | bytes 49160 | tf_op jit(solution)/shard_map/ppermute | solution.py:582
  25.6 3.7 %collective-permute-start.6 = (f32[16,256]{1,0:T(8,128)S(1)}, f32[16,256]{1,0:T(8,128)S(1)}, u32[]{:S(2)}, u32[]{:S(2)}) collective-permute-start(f32[16,256]{1,0:T(8,128)S(1)} %get-tuple-element.81.rest_0_), channel_id=1, source_target_pairs={{0,1},{1,0},{2,3},{3,2},{4,5},{5,4},{6,7},{7,6},{8,9},{9,8},{10,11... | collective-permute-start | bytes 49160 | tf_op jit(solution)/shard_map/ppermute | solution.py:582
  30.8 3.0 %collective-permute-start.9 = (f32[520,128]{1,0:T(8,128)S(1)}, f32[520,128]{1,0:T(8,128)S(1)}, u32[]{:S(2)}, u32[]{:S(2)}) collective-permute-start(f32[520,128]{1,0:T(8,128)S(1)} %get-tuple-element.87), channel_id=1, source_target_pairs={{0,4},{4,0},{8,12},{12,8},{16,20},{20,16},{24,28},{28,24},{1,5},{5... | collective-permute-start | bytes 798728 | tf_op jit(solution)/shard_map/ppermute | solution.py:373
  33.8 5.6 %collective-permute-start.10 = (f32[520,128]{1,0:T(8,128)S(1)}, f32[520,128]{1,0:T(8,128)S(1)}, u32[]{:S(2)}, u32[]{:S(2)}) collective-permute-start(f32[520,128]{1,0:T(8,128)S(1)} %merge.11.after.refs_0_), channel_id=1, source_target_pairs={{0,8},{4,20},{8,0},{12,28},{16,24},{20,4},{24,16},{28,12},{1,9},{5... | collective-permute-start | bytes 798728 | tf_op jit(solution)/shard_map/ppermute | solution.py:373
  39.5 5.7 %collective-permute-start.11 = (f32[520,128]{1,0:T(8,128)S(1)}, f32[520,128]{1,0:T(8,128)S(1)}, u32[]{:S(2)}, u32[]{:S(2)}) collective-permute-start(f32[520,128]{1,0:T(8,128)S(1)} %merge.12.after), channel_id=1, source_target_pairs={{0,16},{4,12},{8,24},{12,4},{16,0},{20,28},{24,8},{28,20},{1,17},{... | collective-permute-start | bytes 798728 | tf_op jit(solution)/shard_map/ppermute | solution.py:373
  45.4 3.8 %collective-permute-start.12 = (f32[520,128]{1,0:T(8,128)S(1)}, f32[520,128]{1,0:T(8,128)S(1)}, u32[]{:S(2)}, u32[]{:S(2)}) collective-permute-start(f32[520,128]{1,0:T(8,128)S(1)} %get-tuple-element.101), channel_id=1, source_target_pairs={{0,4},{4,0},{8,12},{12,8},{16,20},{20,16},{24,28},{28,24},{1,5},{5... | collective-permute-start | bytes 798728 | tf_op jit(solution)/shard_map/ppermute | solution.py:373
